TPU v7x, 32 devices: a whole 2x2x4 slice. The times are simulated.
32 devices in a mesh: gx: 4 (over z), gy: 4 (over y, x), gz: 2 (over core).
Axes of the slice: x: 2, y: 2, z: 4, core: 2. Of those that a mesh axis runs over, the one named last changes fastest.
Arguments:
- electric: float32 [3, 32, 64, 256], P(None, 'gx', 'gy', 'gz'), may hold values from -6 to 6
- permittivity_class: int32 [32, 64, 256], P('gx', 'gy', 'gz'), may hold values from 0 to 3
- cell_index: int32 [4, 64, 128], P('gx', ('gy', 'gz')), may hold values from 0 to 16384, as said below
- polarization: float32 [2, 3, 4, 64, 128], P(None, None, 'gx', ('gy', 'gz')), may hold values from -3 to 3
- populations: float32 [2, 4, 64, 128], P(None, 'gx', ('gy', 'gz')), may hold values from 0.05 to 0.45
- resonance: float32 [4, 64, 128], P('gx', ('gy', 'gz')), may hold values from 0.5 to 1.5
- dephasing: float32 [4, 64, 128], P('gx', ('gy', 'gz')), may hold values from 0.05 to 0.8
- coupling: float32 [4, 64, 128], P('gx', ('gy', 'gz')), may hold values from 0.1 to 1
- pump_rate: float32 [4, 64, 128], P('gx', ('gy', 'gz')), may hold values from 0.02 to 0.4
Outputs:
- electric_out: float32 [3, 32, 64, 256], P(None, 'gx', 'gy', 'gz')
- magnetic_out: float32 [3, 32, 64, 256], P(None, 'gx', 'gy', 'gz')
- polarization_out: float32 [2, 3, 4, 64, 128], P(None, None, 'gx', ('gy', 'gz'))
- populations_out: float32 [2, 4, 64, 128], P(None, 'gx', ('gy', 'gz'))
Inputs may be any that keep to these rules, and one draw needn't show every extreme that they name: `cell_index`: A value below 16384 names the local cell (x 16 + y) * 128 + z of the target block; 16384 marks an empty slot. Every owner's buckets toward the devices of one index of gy, drawn from the seed, are full; each other bucket has an empty last slot.
All inputs are finite; a program needn't handle non-finite values.
Results may differ from a plain program's by a relative error of at most 0.0001.
Values sent between devices are 32-bit elements; how exact they have to be, the bound alone decides.
No kernel may reach another device: no remote copies, remote signals or barrier semaphores. Data moves between devices by JAX's collectives and lax.ppermute only.
A program may use at most 64 MiB of HBM per device.

v0:
```python
import jax
import jax.numpy as jnp
from jax import lax
from jax.sharding import PartitionSpec as P

STEPS = 4


time_step = 0.5
pump_decay = 0.2
upper_decay = 0.02
work_share = 0.05
class_permittivity = (1.0, 2.1, 6.0, 12.25)


def extended_2(block, sides, width):
    for axis, dim in sides:
        count = lax.axis_size(axis)
        forward = [(i, i + 1) for i in range(count - 1)]
        backward = [(target, source) for source, target in forward]
        low = lax.ppermute(
            lax.slice_in_dim(block, block.shape[dim] - width, None, axis=dim), axis, forward
        )
        high = lax.ppermute(lax.slice_in_dim(block, 0, width, axis=dim), axis, backward)
        block = jnp.concatenate([low, block, high], axis=dim)
    return block


def inverse_permittivity(classes):
    inverse = jnp.zeros(classes.shape, jnp.float32)
    for number, epsilon in enumerate(class_permittivity):
        inverse = inverse + jnp.where(classes == number, 1.0 / epsilon, 0.0)
    return inverse


def combine_curl(along_x, along_y, along_z):
    return jnp.stack([along_y[2] - along_z[1], along_z[0] - along_x[2], along_x[1] - along_y[0]])


def bloch_update(
    sample, current, previous, upper, pumped, resonance, dephasing, coupling, pump_rate
):
    lower = 1.0 - upper - pumped
    damping = 0.5 * time_step * dephasing
    stiffness = resonance * time_step * (resonance * time_step)
    advanced = (
        (2.0 - stiffness) * current
        - (1.0 - damping) * previous
        + coupling * (time_step * time_step) * (lower - upper) * sample
    ) / (1.0 + damping)
    work = jnp.sum(sample * (advanced - previous), axis=0) / (2.0 * time_step)
    pumped_next = pumped + time_step * (pump_rate * lower - pump_decay * pumped)
    upper_next = upper + time_step * (
        pump_decay * pumped - upper_decay * upper + work_share * work / resonance
    )
    return (advanced, current, upper_next, pumped_next)


def shards(
    electric,
    permittivity_class,
    cell_index,
    polarization,
    populations,
    resonance,
    dephasing,
    coupling,
    pump_rate,
):
    width_x, width_y, width_z = (electric.shape[1], electric.shape[2], electric.shape[3])
    cell_count = width_x * width_y * width_z
    bucket_count = cell_index.shape[1]
    slot_count = cell_index.shape[2]
    inverse = inverse_permittivity(permittivity_class)
    received = lax.all_to_all(cell_index, ("gy", "gz"), split_axis=1, concat_axis=1, tiled=True)
    safe_index = jnp.minimum(received, cell_count - 1).reshape(-1)
    weight = (received < cell_count).reshape(-1).astype(jnp.float32)
    dropped = received.reshape(-1)
    pos_x = lax.broadcasted_iota(jnp.int32, (1, width_x + 1, 1, 1), 1)
    pos_y = lax.broadcasted_iota(jnp.int32, (1, 1, width_y + 1, 1), 2)
    pos_z = lax.broadcasted_iota(jnp.int32, (1, 1, 1, width_z + 1), 3)
    keep_x = jnp.where((pos_x == 0) & (lax.axis_index("gx") == 0), 0.0, 1.0)
    keep_y = jnp.where((pos_y == 0) & (lax.axis_index("gy") == 0), 0.0, 1.0)
    keep_z = jnp.where((pos_z == 0) & (lax.axis_index("gz") == 0), 0.0, 1.0)
    boundary = keep_x * keep_y * keep_z
    extended = jnp.zeros((3, width_x + 1, width_y + 1, width_z + 1), jnp.float32)
    packed = jnp.concatenate(
        [
            polarization.reshape(6, 1, bucket_count, slot_count),
            populations,
            jnp.stack([resonance, dephasing, coupling, pump_rate]),
        ],
        axis=0,
    )
    moved = lax.all_to_all(packed, ("gy", "gz"), split_axis=2, concat_axis=2, tiled=True)
    current = moved[0:3]
    previous = moved[3:6]
    upper = moved[6]
    pumped = moved[7]
    freq = moved[8]
    dephase = moved[9]
    strength = moved[10]
    pumping = moved[11]
    for repeat in range(STEPS):
        padded = extended_2(electric, (("gx", 1), ("gy", 2), ("gz", 3)), 1)
        base = padded[:, :-1, :-1, :-1]
        advance_curl = combine_curl(
            padded[:, 1:, :-1, :-1] - base,
            padded[:, :-1, 1:, :-1] - base,
            padded[:, :-1, :-1, 1:] - base,
        )
        extended = (extended - time_step * advance_curl) * boundary
        sample = (electric.reshape(3, -1)[:, safe_index] * weight).reshape(
            3, 1, bucket_count, slot_count
        )
        advanced, previous, upper, pumped = bloch_update(
            sample, current, previous, upper, pumped, freq, dephase, strength, pumping
        )
        change = advanced - previous
        current = advanced
        flat_change = change.reshape(3, -1)
        summed = (
            jnp.zeros((3, cell_count), jnp.float32).at[:, dropped].add(flat_change, mode="drop")
        )
        inner = extended[:, 1:, 1:, 1:]
        curl = combine_curl(
            inner - extended[:, :-1, 1:, 1:],
            inner - extended[:, 1:, :-1, 1:],
            inner - extended[:, 1:, 1:, :-1],
        )
        electric = electric + inverse * (
            time_step * curl - summed.reshape(3, width_x, width_y, width_z)
        )
    states = jnp.concatenate([current, previous, upper[None], pumped[None]], axis=0)
    home = lax.all_to_all(states, ("gy", "gz"), split_axis=2, concat_axis=2, tiled=True)
    current = home[0:3]
    previous = home[3:6]
    upper = home[6]
    pumped = home[7]
    polar_out = jnp.stack([current, previous])
    popul_out = jnp.stack([upper, pumped])
    return (electric, extended[:, 1:, 1:, 1:], polar_out, popul_out)


def solution(mesh):
    return jax.shard_map(
        shards,
        mesh=mesh,
        in_specs=(
            P(None, "gx", "gy", "gz"),
            P("gx", "gy", "gz"),
            P("gx", ("gy", "gz"), None),
            P(None, None, "gx", ("gy", "gz"), None),
            P(None, "gx", ("gy", "gz"), None),
            P("gx", ("gy", "gz"), None),
            P("gx", ("gy", "gz"), None),
            P("gx", ("gy", "gz"), None),
            P("gx", ("gy", "gz"), None),
        ),
        out_specs=(
            P(None, "gx", "gy", "gz"),
            P(None, "gx", "gy", "gz"),
            P(None, None, "gx", ("gy", "gz"), None),
            P(None, "gx", ("gy", "gz"), None),
        ),
        check_vma=False,
    )
```

profile of v0, /device:TPU:21, one launch (start us, length us, event | category | flops | bytes accessed | tf_op | source)
XLA Modules:
  0.0 219.9 jit_solution(16094291337743988852)
XLA Ops:
  0.6 4.7 %all-to-all-start = ((s32[1,8,128]{2,0,1:T(1,128)}), s32[1,8,128]{2,0,1:T(1,128)S(1)}, u32[]{:S(2)}, u32[]{:S(2)}) async-start(s32[1,8,128]{2,0,1:T(1,128)} %bitcast.163), calls=%async_computation | async-start | bytes 8192 | tf_op jit(solution)/shard_map/all_to_all | solution.py:75
  6.1 3.2 %collective-permute-start = (f32[3,1,16,128]{3,2,1,0:T(8,128)S(1)}, f32[3,1,16,128]{3,2,1,0:T(8,128)S(1)}, u32[]{:S(2)}, u32[]{:S(2)}) collective-permute-start(f32[3,1,16,128]{3,2,1,0:T(8,128)S(1)} %get-tuple-element.117), channel_id=1, source_target_pairs={{0,8},{8,16},{16,24},{1,9},{9,17},{17,25},{2,10},{10,18},{18,26},{... | collective-permute-start | bytes 73736 | tf_op jit(solution)/shard_map/ppermute | solution.py:21
  9.3 2.1 collective-permute-start.1
  16.6 5.7 %copy.227 = f32[3,8,16,128]{0,3,2,1:T(8,128)} copy(f32[3,8,16,128]{3,2,1,0:T(8,128)} %param.9) | data formatting | bytes 393216 | tf_op args[0]
  23.0 4.8 %all-to-all-start.1 = ((f32[12,1,8,128]{3,0,1,2:T(8,128)}), f32[12,1,8,128]{3,0,1,2:T(8,128)S(1)}, u32[]{:S(2)}, u32[]{:S(2)}) async-start(f32[12,1,8,128]{3,0,1,2:T(8,128)} %copy.221), calls=%async_computation.1 | async-start | bytes 131072 | tf_op jit(solution)/shard_map/all_to_all | solution.py:95
  27.8 3.1 %collective-permute-start.3 = (f32[3,10,1,128]{3,2,1,0:T(1,128)S(1)}, f32[3,10,1,128]{3,2,1,0:T(1,128)S(1)}, u32[]{:S(2)}, u32[]{:S(2)}) collective-permute-start(f32[3,10,1,128]{3,2,1,0:T(1,128)S(1)} %get-tuple-element.97), channel_id=1, source_target_pairs={{2,0},{4,2},{6,4},{3,1},{5,3},{7,5},{10,8},{12,10},{14,12},{11,9},... | collective-permute-start | bytes 46088 | tf_op jit(solution)/shard_map/ppermute | solution.py:24
  30.9 2.2 collective-permute-start.2
  33.2 3.2 %collective-permute-done.2 = f32[3,10,1,128]{3,2,1,0:T(1,128)S(1)} collective-permute-done((f32[3,10,1,128]{3,2,1,0:T(1,128)S(1)}, f32[3,10,1,128]{3,2,1,0:T(1,128)S(1)}, u32[]{:S(2)}, u32[]{:S(2)}) %collective-permute-start.2) | collective-permute-done | bytes 15392 | tf_op jit(solution)/shard_map/ppermute | solution.py:21
  36.5 1.3 collective-permute-start.4
  37.9 6.2 %gather_fusion = f32[1024,3]{1,0:T(8,128)S(1)} fusion(f32[3,16384]{0,1:T(8,128)} %bitcast.124, s32[1024]{0:T(1024)S(1)} %broadcast_clamp_fusion), kind=kCustom, calls=%fused_computation | custom fusion | bytes 28672 | tf_op jit(solution)/shard_map/gather | solution.py:113
  44.2 3.7 %collective-permute-start.5 = (f32[3,10,18,1]{3,2,1,0:T(8,128)S(1)}, f32[3,10,18,1]{3,2,1,0:T(8,128)S(1)}, u32[]{:S(2)}, u32[]{:S(2)}) collective-permute-start(f32[3,10,18,1]{3,2,1,0:T(8,128)S(1)} %get-tuple-element.88), channel_id=1, source_target_pairs={{1,0},{3,2},{5,4},{7,6},{9,8},{11,10},{13,12},{15,14},{17,16},{19,... | collective-permute-start | bytes 6488 | tf_op jit(solution)/shard_map/ppermute | solution.py:24
  50.3 9.8 %scatter_custom_fusion = f32[3,16384]{0,1:T(8,128)} fusion(s32[1024]{0:T(1024)S(1)} %bitcast.159, f32[1024,3]{1,0:T(8,128)S(1)} %copy.229, f32[]{:T(128)} %constant.21.clone.1), kind=kCustom, calls=%fused_computation.14 | custom fusion | flops 3072 | bytes 196612 | tf_op jit(solution)/shard_map/scatter-add | solution.py:123
  60.1 5.2 %copy.230 = f32[3,8,16,128]{3,2,1,0:T(8,128)S(1)} copy(f32[3,8,16,128]{0,3,2,1:T(8,128)} %bitcast.121) | data formatting | bytes 393216 | tf_op jit(solution)/shard_map/reshape | solution.py:132
  65.4 4.7 %copy.232 = f32[3,8,16,128]{0,3,2,1:T(8,128)} copy(f32[3,8,16,128]{3,2,1,0:T(8,128)S(1)} %fusion.22) | data formatting | bytes 393216 | tf_op jit(solution)/shard_map/add | solution.py:131
  70.1 6.2 %gather_fusion.1 = f32[1024,3]{1,0:T(8,128)S(1)} fusion(f32[3,16384]{0,1:T(8,128)} %bitcast.126, s32[1024]{0:T(1024)S(1)} %broadcast_clamp_fusion), kind=kCustom, calls=%fused_computation.1 | custom fusion | bytes 28672 | tf_op jit(solution)/shard_map/gather | solution.py:113
  76.5 2.1 collective-permute-start.7
  78.5 3.2 %collective-permute-start.6 = (f32[3,1,16,128]{3,2,1,0:T(8,128)S(1)}, f32[3,1,16,128]{3,2,1,0:T(8,128)S(1)}, u32[]{:S(2)}, u32[]{:S(2)}) collective-permute-start(f32[3,1,16,128]{3,2,1,0:T(8,128)S(1)} %get-tuple-element.111), channel_id=1, source_target_pairs={{0,8},{8,16},{16,24},{1,9},{9,17},{17,25},{2,10},{10,18},{18,26},{... | collective-permute-start | bytes 73736 | tf_op jit(solution)/shard_map/ppermute | solution.py:21
  83.1 1.9 collective-permute-start.9
  85.1 3.4 %collective-permute-start.8 = (f32[3,10,1,128]{3,2,1,0:T(1,128)S(1)}, f32[3,10,1,128]{3,2,1,0:T(1,128)S(1)}, u32[]{:S(2)}, u32[]{:S(2)}) collective-permute-start(f32[3,10,1,128]{3,2,1,0:T(1,128)S(1)} %get-tuple-element.94), channel_id=1, source_target_pairs={{0,2},{2,4},{4,6},{1,3},{3,5},{5,7},{8,10},{10,12},{12,14},{9,11},... | collective-permute-start | bytes 46088 | tf_op jit(solution)/shard_map/ppermute | solution.py:21
  88.5 2.0 collective-permute-done.8
  90.7 1.3 collective-permute-start.10
  92.2 9.8 %scatter_custom_fusion.1 = f32[3,16384]{0,1:T(8,128)} fusion(s32[1024]{0:T(1024)S(1)} %bitcast.160, f32[1024,3]{1,0:T(8,128)S(1)} %copy.234, f32[]{:T(128)} %constant.21.clone.1), kind=kCustom, calls=%fused_computation.12 | custom fusion | flops 3072 | bytes 196612 | tf_op jit(solution)/shard_map/scatter-add | solution.py:123
  102.0 5.2 %copy.235 = f32[3,8,16,128]{3,2,1,0:T(8,128)S(1)} copy(f32[3,8,16,128]{0,3,2,1:T(8,128)} %bitcast.122) | data formatting | bytes 393216 | tf_op jit(solution)/shard_map/reshape | solution.py:132
  107.2 5.8 %collective-permute-start.11 = (f32[3,10,18,1]{3,2,1,0:T(8,128)S(1)}, f32[3,10,18,1]{3,2,1,0:T(8,128)S(1)}, u32[]{:S(2)}, u32[]{:S(2)}) collective-permute-start(f32[3,10,18,1]{3,2,1,0:T(8,128)S(1)} %get-tuple-element.86), channel_id=1, source_target_pairs={{1,0},{3,2},{5,4},{7,6},{9,8},{11,10},{13,12},{15,14},{17,16},{19,... | collective-permute-start | bytes 6488 | tf_op jit(solution)/shard_map/ppermute | solution.py:24
  113.1 1.4 maximum_maximum_fusion.1
  115.3 4.7 %copy.236 = f32[3,8,16,128]{0,3,2,1:T(8,128)} copy(f32[3,8,16,128]{3,2,1,0:T(8,128)S(1)} %fusion.25) | data formatting | bytes 393216 | tf_op jit(solution)/shard_map/add | solution.py:131
  120.0 6.2 %gather_fusion.2 = f32[1024,3]{1,0:T(8,128)S(1)} fusion(f32[3,16384]{0,1:T(8,128)} %bitcast.127, s32[1024]{0:T(1024)S(1)} %broadcast_clamp_fusion), kind=kCustom, calls=%fused_computation.2 | custom fusion | bytes 28672 | tf_op jit(solution)/shard_map/gather | solution.py:113
  126.4 1.9 collective-permute-start.13
  128.3 3.4 %collective-permute-start.12 = (f32[3,1,16,128]{3,2,1,0:T(8,128)S(1)}, f32[3,1,16,128]{3,2,1,0:T(8,128)S(1)}, u32[]{:S(2)}, u32[]{:S(2)}) collective-permute-start(f32[3,1,16,128]{3,2,1,0:T(8,128)S(1)} %get-tuple-element.106), channel_id=1, source_target_pairs={{0,8},{8,16},{16,24},{1,9},{9,17},{17,25},{2,10},{10,18},{18,26},{... | collective-permute-start | bytes 73736 | tf_op jit(solution)/shard_map/ppermute | solution.py:21
  132.9 1.9 collective-permute-start.15
  134.8 3.4 %collective-permute-start.14 = (f32[3,10,1,128]{3,2,1,0:T(1,128)S(1)}, f32[3,10,1,128]{3,2,1,0:T(1,128)S(1)}, u32[]{:S(2)}, u32[]{:S(2)}) collective-permute-start(f32[3,10,1,128]{3,2,1,0:T(1,128)S(1)} %get-tuple-element.92), channel_id=1, source_target_pairs={{0,2},{2,4},{4,6},{1,3},{3,5},{5,7},{8,10},{10,12},{12,14},{9,11},... | collective-permute-start | bytes 46088 | tf_op jit(solution)/shard_map/ppermute | solution.py:21
  138.2 2.0 collective-permute-done.14
  142.8 9.8 %scatter_custom_fusion.2 = f32[3,16384]{0,1:T(8,128)} fusion(s32[1024]{0:T(1024)S(1)} %bitcast.161, f32[1024,3]{1,0:T(8,128)S(1)} %copy.238, f32[]{:T(128)} %constant.21.clone.1), kind=kCustom, calls=%fused_computation.10 | custom fusion | flops 3072 | bytes 196612 | tf_op jit(solution)/shard_map/scatter-add | solution.py:123
  152.6 5.3 %copy.239 = f32[3,8,16,128]{3,2,1,0:T(8,128)S(1)} copy(f32[3,8,16,128]{0,3,2,1:T(8,128)} %bitcast.123) | data formatting | bytes 393216 | tf_op jit(solution)/shard_map/reshape | solution.py:132
  157.9 5.0 %collective-permute-start.17 = (f32[3,10,18,1]{3,2,1,0:T(8,128)S(1)}, f32[3,10,18,1]{3,2,1,0:T(8,128)S(1)}, u32[]{:S(2)}, u32[]{:S(2)}) collective-permute-start(f32[3,10,18,1]{3,2,1,0:T(8,128)S(1)} %copy-done.2), channel_id=1, source_target_pairs={{1,0},{3,2},{5,4},{7,6},{9,8},{11,10},{13,12},{15,14},{17,16},{19,... | collective-permute-start | bytes 6488 | tf_op jit(solution)/shard_map/ppermute | solution.py:24
  162.9 1.4 maximum_maximum_fusion.2
  165.2 4.7 %copy.240 = f32[3,8,16,128]{0,3,2,1:T(8,128)} copy(f32[3,8,16,128]{3,2,1,0:T(8,128)S(1)} %fusion.28) | data formatting | bytes 393216 | tf_op jit(solution)/shard_map/add | solution.py:131
  169.9 6.2 %gather_fusion.3 = f32[1024,3]{1,0:T(8,128)S(1)} fusion(f32[3,16384]{0,1:T(8,128)} %bitcast.125, s32[1024]{0:T(1024)S(1)} %broadcast_clamp_fusion), kind=kCustom, calls=%fused_computation.3 | custom fusion | bytes 28672 | tf_op jit(solution)/shard_map/gather | solution.py:113
  176.3 1.9 collective-permute-start.19
  178.3 3.4 %collective-permute-start.18 = (f32[3,1,16,128]{3,2,1,0:T(8,128)S(1)}, f32[3,1,16,128]{3,2,1,0:T(8,128)S(1)}, u32[]{:S(2)}, u32[]{:S(2)}) collective-permute-start(f32[3,1,16,128]{3,2,1,0:T(8,128)S(1)} %get-tuple-element.101), channel_id=1, source_target_pairs={{0,8},{8,16},{16,24},{1,9},{9,17},{17,25},{2,10},{10,18},{18,26},{... | collective-permute-start | bytes 73736 | tf_op jit(solution)/shard_map/ppermute | solution.py:21
  182.5 9.8 %scatter_custom_fusion.3 = f32[3,16384]{0,1:T(8,128)} fusion(s32[1024]{0:T(1024)S(1)} %bitcast.162, f32[1024,3]{1,0:T(8,128)S(1)} %copy.242, f32[]{:T(128)} %constant.21.clone.1), kind=kCustom, calls=%fused_computation.8 | custom fusion | flops 3072 | bytes 196612 | tf_op jit(solution)/shard_map/scatter-add | solution.py:123
  192.3 5.2 %copy.243 = f32[3,8,16,128]{3,2,1,0:T(8,128)S(1)} copy(f32[3,8,16,128]{0,3,2,1:T(8,128)} %bitcast.120) | data formatting | bytes 393216 | tf_op jit(solution)/shard_map/reshape | solution.py:132
  197.5 4.3 %all-to-all-start.2 = ((f32[8,1,8,128]{3,0,1,2:T(8,128)}), f32[8,1,8,128]{3,0,1,2:T(8,128)S(1)}, u32[]{:S(2)}, u32[]{:S(2)}) async-start(f32[8,1,8,128]{3,0,1,2:T(8,128)} %pad_maximum_fusion.22), calls=%async_computation.2 | async-start | bytes 65536 | tf_op jit(solution)/shard_map/all_to_all | solution.py:135
  201.9 3.1 %collective-permute-start.21 = (f32[3,10,1,128]{3,2,1,0:T(1,128)S(1)}, f32[3,10,1,128]{3,2,1,0:T(1,128)S(1)}, u32[]{:S(2)}, u32[]{:S(2)}) collective-permute-start(f32[3,10,1,128]{3,2,1,0:T(1,128)S(1)} %get-tuple-element.91), channel_id=1, source_target_pairs={{2,0},{4,2},{6,4},{3,1},{5,3},{7,5},{10,8},{12,10},{14,12},{11,9},... | collective-permute-start | bytes 46088 | tf_op jit(solution)/shard_map/ppermute | solution.py:24
  205.0 2.2 collective-permute-start.20
  207.2 3.1 %collective-permute-done.20 = f32[3,10,1,128]{3,2,1,0:T(1,128)S(1)} collective-permute-done((f32[3,10,1,128]{3,2,1,0:T(1,128)S(1)}, f32[3,10,1,128]{3,2,1,0:T(1,128)S(1)}, u32[]{:S(2)}, u32[]{:S(2)}) %collective-permute-start.20) | collective-permute-done | bytes 15392 | tf_op jit(solution)/shard_map/ppermute | solution.py:21
  210.6 1.3 collective-permute-start.22
  213.1 3.7 %collective-permute-start.23 = (f32[3,10,18,1]{3,2,1,0:T(8,128)S(1)}, f32[3,10,18,1]{3,2,1,0:T(8,128)S(1)}, u32[]{:S(2)}, u32[]{:S(2)}) collective-permute-start(f32[3,10,18,1]{3,2,1,0:T(8,128)S(1)} %get-tuple-element.82), channel_id=1, source_target_pairs={{1,0},{3,2},{5,4},{7,6},{9,8},{11,10},{13,12},{15,14},{17,16},{19,... | collective-permute-start | bytes 6488 | tf_op jit(solution)/shard_map/ppermute | solution.py:24
  (123 shorter events, 22.8 us)
Async XLA Ops:
  0.6 27.1 %copy-start = (f32[3,8,16,128]{3,2,1,0:T(8,128)S(1)}, f32[3,8,16,128]{3,2,1,0:T(8,128)}, u32[]{:S(2)}) copy-start(f32[3,8,16,128]{3,2,1,0:T(8,128)} %param.9) | copy-start | bytes 589828
  0.6 22.3 %all-to-all-start = ((s32[1,8,128]{2,0,1:T(1,128)}), s32[1,8,128]{2,0,1:T(1,128)S(1)}, u32[]{:S(2)}, u32[]{:S(2)}) async-start(s32[1,8,128]{2,0,1:T(1,128)} %bitcast.163), calls=%async_computation | async-start | bytes 8192 | tf_op jit(solution)/shard_map/all_to_all | solution.py:75
  6.1 21.6 %collective-permute-start = (f32[3,1,16,128]{3,2,1,0:T(8,128)S(1)}, f32[3,1,16,128]{3,2,1,0:T(8,128)S(1)}, u32[]{:S(2)}, u32[]{:S(2)}) collective-permute-start(f32[3,1,16,128]{3,2,1,0:T(8,128)S(1)} %get-tuple-element.117), channel_id=1, source_target_pairs={{0,8},{8,16},{16,24},{1,9},{9,17},{17,25},{2,10},{10,18},{18,26},{... | collective-permute-start | bytes 73736 | tf_op jit(solution)/shard_map/ppermute | solution.py:21
  9.3 18.5 %collective-permute-start.1 = (f32[3,1,16,128]{3,2,1,0:T(8,128)S(1)}, f32[3,1,16,128]{3,2,1,0:T(8,128)S(1)}, u32[]{:S(2)}, u32[]{:S(2)}) collective-permute-start(f32[3,1,16,128]{3,2,1,0:T(8,128)S(1)} %get-tuple-element.116), channel_id=1, source_target_pairs={{8,0},{16,8},{24,16},{9,1},{17,9},{25,17},{10,2},{18,10},{26,18},{... | collective-permute-start | bytes 73736 | tf_op jit(solution)/shard_map/ppermute | solution.py:24
  23.0 27.0 %all-to-all-start.1 = ((f32[12,1,8,128]{3,0,1,2:T(8,128)}), f32[12,1,8,128]{3,0,1,2:T(8,128)S(1)}, u32[]{:S(2)}, u32[]{:S(2)}) async-start(f32[12,1,8,128]{3,0,1,2:T(8,128)} %copy.221), calls=%async_computation.1 | async-start | bytes 131072 | tf_op jit(solution)/shard_map/all_to_all | solution.py:95
  27.8 5.3 %collective-permute-start.3 = (f32[3,10,1,128]{3,2,1,0:T(1,128)S(1)}, f32[3,10,1,128]{3,2,1,0:T(1,128)S(1)}, u32[]{:S(2)}, u32[]{:S(2)}) collective-permute-start(f32[3,10,1,128]{3,2,1,0:T(1,128)S(1)} %get-tuple-element.97), channel_id=1, source_target_pairs={{2,0},{4,2},{6,4},{3,1},{5,3},{7,5},{10,8},{12,10},{14,12},{11,9},... | collective-permute-start | bytes 46088 | tf_op jit(solution)/shard_map/ppermute | solution.py:24
  30.9 5.4 %collective-permute-start.2 = (f32[3,10,1,128]{3,2,1,0:T(1,128)S(1)}, f32[3,10,1,128]{3,2,1,0:T(1,128)S(1)}, u32[]{:S(2)}, u32[]{:S(2)}) collective-permute-start(f32[3,10,1,128]{3,2,1,0:T(1,128)S(1)} %get-tuple-element.96), channel_id=1, source_target_pairs={{0,2},{2,4},{4,6},{1,3},{3,5},{5,7},{8,10},{10,12},{12,14},{9,11},... | collective-permute-start | bytes 46088 | tf_op jit(solution)/shard_map/ppermute | solution.py:21
  36.5 11.4 %collective-permute-start.4 = (f32[3,10,18,1]{3,2,1,0:T(8,128)S(1)}, f32[3,10,18,1]{3,2,1,0:T(8,128)S(1)}, u32[]{:S(2)}, u32[]{:S(2)}) collective-permute-start(f32[3,10,18,1]{3,2,1,0:T(8,128)S(1)} %get-tuple-element.89), channel_id=1, source_target_pairs={{0,1},{2,3},{4,5},{6,7},{8,9},{10,11},{12,13},{14,15},{16,17},{18,... | collective-permute-start | bytes 6488 | tf_op jit(solution)/shard_map/ppermute | solution.py:21
  44.2 5.0 %collective-permute-start.5 = (f32[3,10,18,1]{3,2,1,0:T(8,128)S(1)}, f32[3,10,18,1]{3,2,1,0:T(8,128)S(1)}, u32[]{:S(2)}, u32[]{:S(2)}) collective-permute-start(f32[3,10,18,1]{3,2,1,0:T(8,128)S(1)} %get-tuple-element.88), channel_id=1, source_target_pairs={{1,0},{3,2},{5,4},{7,6},{9,8},{11,10},{13,12},{15,14},{17,16},{19,... | collective-permute-start | bytes 6488 | tf_op jit(solution)/shard_map/ppermute | solution.py:24
  76.5 5.4 %collective-permute-start.7 = (f32[3,1,16,128]{3,2,1,0:T(8,128)S(1)}, f32[3,1,16,128]{3,2,1,0:T(8,128)S(1)}, u32[]{:S(2)}, u32[]{:S(2)}) collective-permute-start(f32[3,1,16,128]{3,2,1,0:T(8,128)S(1)} %get-tuple-element.112), channel_id=1, source_target_pairs={{8,0},{16,8},{24,16},{9,1},{17,9},{25,17},{10,2},{18,10},{26,18},{... | collective-permute-start | bytes 73736 | tf_op jit(solution)/shard_map/ppermute | solution.py:24
  78.5 4.6 %collective-permute-start.6 = (f32[3,1,16,128]{3,2,1,0:T(8,128)S(1)}, f32[3,1,16,128]{3,2,1,0:T(8,128)S(1)}, u32[]{:S(2)}, u32[]{:S(2)}) collective-permute-start(f32[3,1,16,128]{3,2,1,0:T(8,128)S(1)} %get-tuple-element.111), channel_id=1, source_target_pairs={{0,8},{8,16},{16,24},{1,9},{9,17},{17,25},{2,10},{10,18},{18,26},{... | collective-permute-start | bytes 73736 | tf_op jit(solution)/shard_map/ppermute | solution.py:21
  83.1 5.3 %collective-permute-start.9 = (f32[3,10,1,128]{3,2,1,0:T(1,128)S(1)}, f32[3,10,1,128]{3,2,1,0:T(1,128)S(1)}, u32[]{:S(2)}, u32[]{:S(2)}) collective-permute-start(f32[3,10,1,128]{3,2,1,0:T(1,128)S(1)} %get-tuple-element.95), channel_id=1, source_target_pairs={{2,0},{4,2},{6,4},{3,1},{5,3},{7,5},{10,8},{12,10},{14,12},{11,9},... | collective-permute-start | bytes 46088 | tf_op jit(solution)/shard_map/ppermute | solution.py:24
  85.1 5.4 %collective-permute-start.8 = (f32[3,10,1,128]{3,2,1,0:T(1,128)S(1)}, f32[3,10,1,128]{3,2,1,0:T(1,128)S(1)}, u32[]{:S(2)}, u32[]{:S(2)}) collective-permute-start(f32[3,10,1,128]{3,2,1,0:T(1,128)S(1)} %get-tuple-element.94), channel_id=1, source_target_pairs={{0,2},{2,4},{4,6},{1,3},{3,5},{5,7},{8,10},{10,12},{12,14},{9,11},... | collective-permute-start | bytes 46088 | tf_op jit(solution)/shard_map/ppermute | solution.py:21
  90.7 22.4 %collective-permute-start.10 = (f32[3,10,18,1]{3,2,1,0:T(8,128)S(1)}, f32[3,10,18,1]{3,2,1,0:T(8,128)}, u32[]{:S(2)}, u32[]{:S(2)}) collective-permute-start(f32[3,10,18,1]{3,2,1,0:T(8,128)S(1)} %get-tuple-element.87), channel_id=1, source_target_pairs={{0,1},{2,3},{4,5},{6,7},{8,9},{10,11},{12,13},{14,15},{16,17},{18,... | collective-permute-start | bytes 6488 | tf_op jit(solution)/shard_map/ppermute | solution.py:21
  107.2 7.2 %collective-permute-start.11 = (f32[3,10,18,1]{3,2,1,0:T(8,128)S(1)}, f32[3,10,18,1]{3,2,1,0:T(8,128)S(1)}, u32[]{:S(2)}, u32[]{:S(2)}) collective-permute-start(f32[3,10,18,1]{3,2,1,0:T(8,128)S(1)} %get-tuple-element.86), channel_id=1, source_target_pairs={{1,0},{3,2},{5,4},{7,6},{9,8},{11,10},{13,12},{15,14},{17,16},{19,... | collective-permute-start | bytes 6488 | tf_op jit(solution)/shard_map/ppermute | solution.py:24
  126.4 5.4 %collective-permute-start.13 = (f32[3,1,16,128]{3,2,1,0:T(8,128)S(1)}, f32[3,1,16,128]{3,2,1,0:T(8,128)S(1)}, u32[]{:S(2)}, u32[]{:S(2)}) collective-permute-start(f32[3,1,16,128]{3,2,1,0:T(8,128)S(1)} %get-tuple-element.107), channel_id=1, source_target_pairs={{8,0},{16,8},{24,16},{9,1},{17,9},{25,17},{10,2},{18,10},{26,18},{... | collective-permute-start | bytes 73736 | tf_op jit(solution)/shard_map/ppermute | solution.py:24
  128.3 4.6 %collective-permute-start.12 = (f32[3,1,16,128]{3,2,1,0:T(8,128)S(1)}, f32[3,1,16,128]{3,2,1,0:T(8,128)S(1)}, u32[]{:S(2)}, u32[]{:S(2)}) collective-permute-start(f32[3,1,16,128]{3,2,1,0:T(8,128)S(1)} %get-tuple-element.106), channel_id=1, source_target_pairs={{0,8},{8,16},{16,24},{1,9},{9,17},{17,25},{2,10},{10,18},{18,26},{... | collective-permute-start | bytes 73736 | tf_op jit(solution)/shard_map/ppermute | solution.py:21
  132.9 5.3 %collective-permute-start.15 = (f32[3,10,1,128]{3,2,1,0:T(1,128)S(1)}, f32[3,10,1,128]{3,2,1,0:T(1,128)S(1)}, u32[]{:S(2)}, u32[]{:S(2)}) collective-permute-start(f32[3,10,1,128]{3,2,1,0:T(1,128)S(1)} %get-tuple-element.93), channel_id=1, source_target_pairs={{2,0},{4,2},{6,4},{3,1},{5,3},{7,5},{10,8},{12,10},{14,12},{11,9},... | collective-permute-start | bytes 46088 | tf_op jit(solution)/shard_map/ppermute | solution.py:24
  134.8 5.4 %collective-permute-start.14 = (f32[3,10,1,128]{3,2,1,0:T(1,128)S(1)}, f32[3,10,1,128]{3,2,1,0:T(1,128)S(1)}, u32[]{:S(2)}, u32[]{:S(2)}) collective-permute-start(f32[3,10,1,128]{3,2,1,0:T(1,128)S(1)} %get-tuple-element.92), channel_id=1, source_target_pairs={{0,2},{2,4},{4,6},{1,3},{3,5},{5,7},{8,10},{10,12},{12,14},{9,11},... | collective-permute-start | bytes 46088 | tf_op jit(solution)/shard_map/ppermute | solution.py:21
  141.2 21.6 %collective-permute-start.16 = (f32[3,10,18,1]{3,2,1,0:T(8,128)}, f32[3,10,18,1]{3,2,1,0:T(8,128)}, u32[]{:S(2)}, u32[]{:S(2)}) collective-permute-start(f32[3,10,18,1]{3,2,1,0:T(8,128)} %get-tuple-element.85), channel_id=1, source_target_pairs={{0,1},{2,3},{4,5},{6,7},{8,9},{10,11},{12,13},{14,15},{16,17},{18,... | collective-permute-start | bytes 6488 | tf_op jit(solution)/shard_map/ppermute | solution.py:21
  152.6 5.3 %copy-start.2 = (f32[3,10,18,1]{3,2,1,0:T(8,128)S(1)}, f32[3,10,18,1]{3,2,1,0:T(8,128)}, u32[]{:S(2)}) copy-start(f32[3,10,18,1]{3,2,1,0:T(8,128)} %get-tuple-element.84) | copy-start | bytes 6484
  157.9 6.4 %collective-permute-start.17 = (f32[3,10,18,1]{3,2,1,0:T(8,128)S(1)}, f32[3,10,18,1]{3,2,1,0:T(8,128)S(1)}, u32[]{:S(2)}, u32[]{:S(2)}) collective-permute-start(f32[3,10,18,1]{3,2,1,0:T(8,128)S(1)} %copy-done.2), channel_id=1, source_target_pairs={{1,0},{3,2},{5,4},{7,6},{9,8},{11,10},{13,12},{15,14},{17,16},{19,... | collective-permute-start | bytes 6488 | tf_op jit(solution)/shard_map/ppermute | solution.py:24
  176.3 25.5 %collective-permute-start.19 = (f32[3,1,16,128]{3,2,1,0:T(8,128)S(1)}, f32[3,1,16,128]{3,2,1,0:T(8,128)S(1)}, u32[]{:S(2)}, u32[]{:S(2)}) collective-permute-start(f32[3,1,16,128]{3,2,1,0:T(8,128)S(1)} %get-tuple-element.102), channel_id=1, source_target_pairs={{8,0},{16,8},{24,16},{9,1},{17,9},{25,17},{10,2},{18,10},{26,18},{... | collective-permute-start | bytes 73736 | tf_op jit(solution)/shard_map/ppermute | solution.py:24
  178.3 23.6 %collective-permute-start.18 = (f32[3,1,16,128]{3,2,1,0:T(8,128)S(1)}, f32[3,1,16,128]{3,2,1,0:T(8,128)S(1)}, u32[]{:S(2)}, u32[]{:S(2)}) collective-permute-start(f32[3,1,16,128]{3,2,1,0:T(8,128)S(1)} %get-tuple-element.101), channel_id=1, source_target_pairs={{0,8},{8,16},{16,24},{1,9},{9,17},{17,25},{2,10},{10,18},{18,26},{... | collective-permute-start | bytes 73736 | tf_op jit(solution)/shard_map/ppermute | solution.py:21
  197.5 9.6 %all-to-all-start.2 = ((f32[8,1,8,128]{3,0,1,2:T(8,128)}), f32[8,1,8,128]{3,0,1,2:T(8,128)S(1)}, u32[]{:S(2)}, u32[]{:S(2)}) async-start(f32[8,1,8,128]{3,0,1,2:T(8,128)} %pad_maximum_fusion.22), calls=%async_computation.2 | async-start | bytes 65536 | tf_op jit(solution)/shard_map/all_to_all | solution.py:135
  201.9 5.3 %collective-permute-start.21 = (f32[3,10,1,128]{3,2,1,0:T(1,128)S(1)}, f32[3,10,1,128]{3,2,1,0:T(1,128)S(1)}, u32[]{:S(2)}, u32[]{:S(2)}) collective-permute-start(f32[3,10,1,128]{3,2,1,0:T(1,128)S(1)} %get-tuple-element.91), channel_id=1, source_target_pairs={{2,0},{4,2},{6,4},{3,1},{5,3},{7,5},{10,8},{12,10},{14,12},{11,9},... | collective-permute-start | bytes 46088 | tf_op jit(solution)/shard_map/ppermute | solution.py:24
  205.0 5.4 %collective-permute-start.20 = (f32[3,10,1,128]{3,2,1,0:T(1,128)S(1)}, f32[3,10,1,128]{3,2,1,0:T(1,128)S(1)}, u32[]{:S(2)}, u32[]{:S(2)}) collective-permute-start(f32[3,10,1,128]{3,2,1,0:T(1,128)S(1)} %get-tuple-element.90), channel_id=1, source_target_pairs={{0,2},{2,4},{4,6},{1,3},{3,5},{5,7},{8,10},{10,12},{12,14},{9,11},... | collective-permute-start | bytes 46088 | tf_op jit(solution)/shard_map/ppermute | solution.py:21
  210.6 6.3 %collective-permute-start.22 = (f32[3,10,18,1]{3,2,1,0:T(8,128)S(1)}, f32[3,10,18,1]{3,2,1,0:T(8,128)S(1)}, u32[]{:S(2)}, u32[]{:S(2)}) collective-permute-start(f32[3,10,18,1]{3,2,1,0:T(8,128)S(1)} %get-tuple-element.83), channel_id=1, source_target_pairs={{0,1},{2,3},{4,5},{6,7},{8,9},{10,11},{12,13},{14,15},{16,17},{18,... | collective-permute-start | bytes 6488 | tf_op jit(solution)/shard_map/ppermute | solution.py:21
  213.1 5.0 %collective-permute-start.23 = (f32[3,10,18,1]{3,2,1,0:T(8,128)S(1)}, f32[3,10,18,1]{3,2,1,0:T(8,128)S(1)}, u32[]{:S(2)}, u32[]{:S(2)}) collective-permute-start(f32[3,10,18,1]{3,2,1,0:T(8,128)S(1)} %get-tuple-element.82), channel_id=1, source_target_pairs={{1,0},{3,2},{5,4},{7,6},{9,8},{11,10},{13,12},{15,14},{17,16},{19,... | collective-permute-start | bytes 6488 | tf_op jit(solution)/shard_map/ppermute | solution.py:24
  218.9 0.9 copy-start.1
where the time goes:
time: 222 us; the launch traced here: 220 us
  starting transfers between devices  79.4 us (36%)
  local copies, waits for them, and re-layouts  74.8 us (34%)
  other arithmetic  49.8 us (22%)
  waiting for transfers between devices  14.4 us (6%)
    scatter-add x4, other arithmetic, shards(): jnp.zeros((3, cell_count), jnp.float32).at[:, dropped]  39.2 us
    ppermute x12, starting transfers between devices, extended_2(): lax.ppermute(lax.slice_in_dim(block, 0, width, axis=dim), axis, backward)  36.3 us
    ppermute x12, starting transfers between devices, extended_2(): lax.ppermute(lax.slice_in_dim(block, block.shape[dim] - width, None, axis...  29.4 us
    gather x8, local copies, waits for them, and re-layouts, shards(): electric.reshape(3, -1)[:, safe_index] * weight  25.5 us
    reshape x4, local copies, waits for them, and re-layouts, shards(): summed.reshape(3, width_x, width_y, width_z)  20.9 us
    add x3, local copies, waits for them, and re-layouts, shards(): electric + inverse * (time_step * curl - summed.reshape(3, width_x, width...  14 us
    ppermute x12, waiting for transfers between devices, extended_2(): lax.ppermute(lax.slice_in_dim(block, block.shape[dim] - width, None, axis...  12.7 us
    unnamed x17, local copies, waits for them, and re-layouts  9.81 us
  transfers between devices with their start and end apart: 27, of which 8 were waited for; matrix products, arithmetic and copies ran while one was open for 32% of the time, Pallas kernels for 0%

commit v1 on v0

v1 whole, which is shorter than its diff:
```python
import functools

import jax
import jax.numpy as jnp
from jax import lax
from jax.experimental import pallas as pl
from jax.experimental.pallas import tpu as pltpu
from jax.sharding import PartitionSpec as P

STEPS = 4
TIME_STEP = 0.5
PUMP_DECAY = 0.2
UPPER_DECAY = 0.02
WORK_SHARE = 0.05
CLASS_PERMITTIVITY = (1.0, 2.1, 6.0, 12.25)

WIDTHS = (STEPS,) * 3 + (STEPS - 1,) * 4 + (STEPS - 2,) * 4 + (STEPS - 3,) * 9
FIELDS = len(WIDTHS)
ALL_WIDTHS = WIDTHS + (STEPS,)
BASES = tuple(sum(ALL_WIDTHS[:i]) for i in range(FIELDS + 1))
LAYERS = sum(ALL_WIDTHS)
LANE_BASES = tuple(2 * sum(WIDTHS[:i]) for i in range(FIELDS))
LANES = 128
VMEM_LIMIT = 56 * 1024 * 1024


def inverse_permittivity(classes):
    inverse = jnp.zeros(classes.shape, jnp.float32)
    for number, epsilon in enumerate(CLASS_PERMITTIVITY):
        inverse = jnp.where(classes == number, 1.0 / epsilon, inverse)
    return inverse


def halves(value):
    high = value.astype(jnp.bfloat16)
    low = (value - high.astype(jnp.float32)).astype(jnp.bfloat16)
    return high, low


def write_one_hots(index, row_hot, depth_hot, rows, depth):
    shift = depth.bit_length() - 1
    buckets, slots = index.shape
    for b in range(buckets):
        row = lax.shift_right_logical(index[b : b + 1], shift)
        deep = lax.bitwise_and(index[b : b + 1], depth - 1)
        rows_at = lax.broadcasted_iota(jnp.int32, (rows, slots), 0)
        deep_at = lax.broadcasted_iota(jnp.int32, (depth, slots), 0)
        hot = jnp.where(rows_at == row, 1.0, 0.0).astype(jnp.bfloat16)
        span = slice(b * slots, (b + 1) * slots)
        row_hot[0:rows, span] = hot
        row_hot[rows : 2 * rows, span] = hot
        depth_hot[:, span] = jnp.where(deep_at == deep, 1.0, 0.0).astype(jnp.bfloat16)


def gather_cells(cells, index, row_hot, depth):
    buckets, slots = index.shape
    parts = []
    for block in cells:
        high, low = halves(block.T)
        parts.append(jnp.concatenate([high, low], axis=1))
    left = jnp.concatenate(parts, axis=0)
    samples = [[], [], []]
    group = 2 if buckets % 2 == 0 else 1
    for start in range(0, buckets, group):
        span = slice(start * slots, (start + group) * slots)
        picked = jnp.dot(left, row_hot[:, span], preferred_element_type=jnp.float32)
        for b in range(start, start + group):
            deep = lax.bitwise_and(index[b : b + 1], depth - 1)
            hit = lax.broadcasted_iota(jnp.int32, (depth, slots), 0) == deep
            for c in range(3):
                part = picked[c * depth : (c + 1) * depth, (b - start) * slots : (b - start + 1) * slots]
                samples[c].append(jnp.sum(jnp.where(hit, part, 0.0), axis=0, keepdims=True))
    return [jnp.concatenate(rows, axis=0) for rows in samples]


def flat_row(value):
    buckets = value.shape[0]
    return jnp.concatenate([value[b : b + 1] for b in range(buckets)], axis=1)


def scatter_cells(values, row_hot, depth_hot, rows):
    hot = row_hot[0:rows, :]
    hot = jnp.concatenate([hot, hot], axis=1)
    deep = depth_hot[...]
    out = []
    for value in values:
        high, low = halves(flat_row(value))
        spread = jnp.concatenate([deep * high, deep * low], axis=1)
        out.append(
            lax.dot_general(
                hot, spread, (((1,), (1,)), ((), ())), preferred_element_type=jnp.float32
            )
        )
    return out


def emitter_constants(arrived):
    freq, dephase, strength, pumping = [arrived[:, f, :] for f in range(8, 12)]
    damping = 0.5 * TIME_STEP * dephase
    stiffness = freq * TIME_STEP * (freq * TIME_STEP)
    scale = 1.0 + damping
    keep = (2.0 - stiffness) / scale
    back = (1.0 - damping) / scale
    drive = strength * (TIME_STEP * TIME_STEP) / scale
    share = WORK_SHARE / freq
    return keep, back, drive, share, pumping


def bloch_step(sample, current, previous, upper, pumped, constants):
    keep, back, drive, share, pumping = constants
    lower = 1.0 - upper - pumped
    push = drive * (lower - upper)
    advanced = [keep * c - back * p + push * s for c, p, s in zip(current, previous, sample)]
    work = sum(s * (a - p) for s, a, p in zip(sample, advanced, previous)) / (2.0 * TIME_STEP)
    pumped_next = pumped + TIME_STEP * (pumping * lower - PUMP_DECAY * pumped)
    upper_next = upper + TIME_STEP * (
        PUMP_DECAY * pumped - UPPER_DECAY * upper + share * work
    )
    return advanced, current, upper_next, pumped_next


def pack_kernel(index, polar, popul, freq, dephase, strength, pumping, out):
    for i in range(2):
        for c in range(3):
            out[:, 3 * i + c, :] = polar[i, c, 0]
    for i in range(2):
        out[:, 6 + i, :] = popul[i, 0]
    for f, source in enumerate((freq, dephase, strength, pumping)):
        out[:, 8 + f, :] = source[0]
    out[:, 12, :] = index[0].astype(jnp.float32)


def first_kernel(arrived, electric, classes, fields, strip, states, row_hot, depth_hot):
    _, nx, ny, depth = electric.shape
    rows = nx * ny
    index = arrived[:, 12, :].astype(jnp.int32)
    write_one_hots(index, row_hot, depth_hot, rows, depth)
    for c in range(3):
        fields[c] = electric[c].reshape(rows, depth)
    fields[3] = inverse_permittivity(classes[...].reshape(rows, depth))
    sample = gather_cells([fields[c] for c in range(3)], index, row_hot, depth)
    constants = emitter_constants(arrived)
    keep, back, drive, share, pumping = constants
    start = [arrived[:, c, :] for c in range(3)]
    before = [arrived[:, 3 + c, :] for c in range(3)]
    now, _, upper, pumped = bloch_step(
        sample, start, before, arrived[:, 6, :], arrived[:, 7, :], constants
    )
    for c in range(3):
        states[c] = now[c]
        states[3 + c] = start[c]
    states[6] = upper
    states[7] = pumped
    lower = 1.0 - upper - pumped
    push = drive * (lower - upper)
    pumped_after = pumped + TIME_STEP * (pumping * lower - PUMP_DECAY * pumped)
    upper_free = upper + TIME_STEP * (PUMP_DECAY * pumped - UPPER_DECAY * upper)
    free = [keep * n - back * s for n, s in zip(now, start)]
    values = [n - s for n, s in zip(now, start)]
    values += [f - n for f, n in zip(free, now)]
    values.append(push)
    values += [(keep - 1.0) * f - back * n for f, n in zip(free, now)]
    values.append((keep - 1.0) * push)
    values.append(drive * (1.0 - pumped_after - 2.0 * upper_free))
    values += [-drive * share * (f - s) for f, s in zip(free, start)]
    values.append(-drive * share * push)
    for number, block in enumerate(scatter_cells(values, row_hot, depth_hot, rows)):
        fields[4 + number] = block
    lane = lax.broadcasted_iota(jnp.int32, (rows, depth), 1)
    packed = jnp.zeros((rows, depth), jnp.float32)
    for f, width in enumerate(WIDTHS):
        at = LANE_BASES[f]
        turned = pltpu.roll(fields[f], (at + width) % depth, 1)
        packed = jnp.where((lane >= at) & (lane < at + 2 * width), turned, packed)
    strip[...] = packed


def faces_x_kernel(nx, ny, count_z, fields, *refs):
    from_low, from_high, strip, low, high = refs
    rows, depth = strip.shape
    lane = lax.broadcasted_iota(jnp.int32, (rows, depth), 1)
    top = jnp.zeros((rows, depth), jnp.bool_)
    for f, width in enumerate(WIDTHS):
        at = LANE_BASES[f]
        top = top | ((lane >= at) & (lane < at + width))
    me = lax.axis_index("gz")
    strip[...] = jnp.where(
        top,
        jnp.where(me > 0, from_low[...], 0.0),
        jnp.where(me < count_z - 1, from_high[...], 0.0),
    )
    for f, width in enumerate(ALL_WIDTHS):
        source = fields.at[f] if f < FIELDS else strip
        for d in range(width):
            low[BASES[f] + d] = source[d * ny : (d + 1) * ny, :]
            high[BASES[f] + d] = source[(nx - 1 - d) * ny : (nx - d) * ny, :]


def faces_y_kernel(nx, ny, fields, strip, halo_low, halo_high, low, high):
    for f, width in enumerate(ALL_WIDTHS):
        source = fields.at[f] if f < FIELDS else strip
        for d in range(width):
            for face, y in ((low, d), (high, ny - 1 - d)):
                at = BASES[f] + d
                face[at, 0:nx, :] = source[pl.ds(y, nx, stride=ny), :]
                if width < STEPS:
                    face[at, nx : nx + 2 * STEPS, :] = jnp.zeros(
                        (2 * STEPS, face.shape[2]), jnp.float32
                    )
                for e in range(width):
                    face[at, nx + e : nx + e + 1, :] = halo_high[BASES[f] + e, y : y + 1, :]
                    last = nx + 2 * STEPS - 1 - e
                    face[at, last : last + 1, :] = halo_low[BASES[f] + e, y : y + 1, :]


def steps_kernel(
    fields, strip, x_low, x_high, y_low, y_high, arrived, states,
    electric, magnetic, result,
    wide, wide_strip, field, row_hot, depth_hot,
):
    _, nx, ny, depth = electric.shape
    rows = nx * ny
    ex, ey, ez = nx + 2 * STEPS, ny + 2 * STEPS, 2 * depth

    for f, width in enumerate(ALL_WIDTHS):
        source = fields.at[f] if f < FIELDS else strip
        target = wide.at[f] if f < FIELDS else wide_strip
        target[STEPS : STEPS + nx, 0:ny, 0:depth] = source[...].reshape(nx, ny, depth)
        target[:, ny : ny + 2 * STEPS, 0:depth] = jnp.zeros((ex, 2 * STEPS, depth), jnp.float32)
        for d in range(width):
            at = BASES[f] + d
            target[STEPS - 1 - d, 0:ny, 0:depth] = x_low[at]
            target[STEPS + nx + d, 0:ny, 0:depth] = x_high[at]
            for halo, y in ((y_low, ey - 1 - d), (y_high, ny + d)):
                for x in range(ex):
                    row = (x - STEPS) % ex
                    target[x, y : y + 1, 0:depth] = halo[at, row : row + 1, :]

    def spread(x, carry):
        value = wide_strip[x]
        for f, width in enumerate(WIDTHS):
            wide[f, x, :, depth:ez] = pltpu.roll(
                value, (-(LANE_BASES[f] + width)) % depth, 1
            )
        return carry

    lax.fori_loop(0, ex, spread, 0)
    row_at = lax.broadcasted_iota(jnp.int32, (ey, ez), 0)
    lane_at = lax.broadcasted_iota(jnp.int32, (ey, ez), 1)
    outside = ((row_at >= ey - STEPS) & (lax.axis_index("gy") == 0)) | (
        (lane_at >= ez - STEPS) & (lax.axis_index("gz") == 0)
    )
    inside = jnp.where(outside, 0.0, 1.0)
    first_x = lax.axis_index("gx") == 0

    index = arrived[:, 12, :].astype(jnp.int32)
    write_one_hots(index, row_hot, depth_hot, rows, depth)
    constants = emitter_constants(arrived)
    current = [states[c] for c in range(3)]
    previous = [states[3 + c] for c in range(3)]
    upper = states[6]
    pumped = states[7]

    def up_y(v):
        return pltpu.roll(v, ey - 1, 0)

    def up_z(v):
        return pltpu.roll(v, ez - 1, 1)

    def down_y(v):
        return pltpu.roll(v, 1, 0)

    def down_z(v):
        return pltpu.roll(v, 1, 1)

    def advance_magnetic(step, x):
        e0, e1, e2 = wide[0, x], wide[1, x], wide[2, x]
        f1, f2 = wide[1, x + 1], wide[2, x + 1]
        curl = (
            (up_y(e2) - e2) - (up_z(e1) - e1),
            (up_z(e0) - e0) - (f2 - e2),
            (f1 - e1) - (up_y(e0) - e0),
        )
        mask = inside * jnp.where(first_x & (x < STEPS), 0.0, 1.0)
        for c in range(3):
            change = -TIME_STEP * curl[c]
            if step > 1:
                change = field[c, x] + change
            field[c, x] = change * mask

    def advance_electric(step, x):
        m0, m1, m2 = field[0, x], field[1, x], field[2, x]
        l1, l2 = field[1, x - 1], field[2, x - 1]
        curl = (
            (m2 - down_y(m2)) - (m1 - down_z(m1)),
            (m0 - down_z(m0)) - (m2 - l2),
            (m1 - l1) - (m0 - down_y(m0)),
        )
        old = [wide[c, x] for c in range(3)]
        if step == 2:
            gain = wide[10, x]
            source = [wide[7 + c, x] + gain * old[c] for c in range(3)]
            ratio = wide[14, x]
            for c in range(3):
                wide[11 + c, x] = wide[11 + c, x] + ratio * old[c]
            square = old[0] * old[0] + old[1] * old[1] + old[2] * old[2]
            wide[15, x] = (
                wide[15, x]
                + (wide[16, x] * old[0] + wide[17, x] * old[1] + wide[18, x] * old[2])
                + wide[19, x] * square
            )
        elif step == 3:
            gain = wide[15, x]
            source = [wide[11 + c, x] + gain * old[c] for c in range(3)]
        else:
            source = [wide[4 + c, x] for c in range(3)]
        inverse = wide[3, x]
        for c in range(3):
            wide[c, x] = old[c] + inverse * (TIME_STEP * curl[c] - source[c])

    for step in range(1, STEPS + 1):
        if step > 1:
            cells = [
                wide[c, STEPS : STEPS + nx, 0:ny, 0:depth].reshape(rows, depth) for c in range(3)
            ]
            sample = gather_cells(cells, index, row_hot, depth)
            advanced, previous, upper, pumped = bloch_step(
                sample, current, previous, upper, pumped, constants
            )
            if step == STEPS:
                change = [a - c for a, c in zip(advanced, current)]
                for c, block in enumerate(scatter_cells(change, row_hot, depth_hot, rows)):
                    wide[4 + c, STEPS : STEPS + nx, 0:ny, 0:depth] = block.reshape(nx, ny, depth)
            current = advanced
        advance_magnetic(step, step - 1)

        def body(x, carry, step=step):
            advance_magnetic(step, x)
            advance_electric(step, x)
            return carry

        lax.fori_loop(step, ex - step, body, 0)
    for c in range(3):
        electric[c] = wide[c, STEPS : STEPS + nx, 0:ny, 0:depth]
        magnetic[c] = field[c, STEPS : STEPS + nx, 0:ny, 0:depth]
        result[:, c, :] = current[c]
        result[:, 3 + c, :] = previous[c]
    result[:, 6, :] = upper
    result[:, 7, :] = pumped


def call(kernel, out_shapes, scratch=()):
    return pl.pallas_call(
        kernel,
        out_shape=[jax.ShapeDtypeStruct(s, jnp.float32) for s in out_shapes],
        scratch_shapes=list(scratch),
        compiler_params=pltpu.CompilerParams(vmem_limit_bytes=VMEM_LIMIT),
    )


def shifted(value, axis, step):
    count = lax.axis_size(axis)
    pairs = [(i, i + step) for i in range(count) if 0 <= i + step < count]
    return lax.ppermute(value, axis, pairs)


def shards(
    electric, permittivity_class, cell_index, polarization, populations,
    resonance, dephasing, coupling, pump_rate,
):
    _, nx, ny, depth = electric.shape
    rows = nx * ny
    _, buckets, slots = cell_index.shape
    ex, ey, ez = nx + 2 * STEPS, ny + 2 * STEPS, 2 * depth
    hots = [
        pltpu.VMEM((2 * rows, buckets * slots), jnp.bfloat16),
        pltpu.VMEM((depth, buckets * slots), jnp.bfloat16),
    ]
    (packed,) = call(pack_kernel, [(buckets, 13, slots)])(
        cell_index, polarization, populations, resonance, dephasing, coupling, pump_rate
    )
    arrived = lax.all_to_all(packed, ("gy", "gz"), split_axis=0, concat_axis=0, tiled=True)
    fields, strip, states = call(
        first_kernel,
        [(FIELDS, rows, depth), (rows, depth), (8, buckets, slots)],
        hots,
    )(arrived, electric, permittivity_class)
    count_z = lax.axis_size("gz")
    if count_z == 2:
        from_low = from_high = lax.ppermute(strip, "gz", [(0, 1), (1, 0)])
    else:
        from_low = shifted(strip, "gz", 1)
        from_high = shifted(strip, "gz", -1)
    strip, face_low, face_high = call(
        functools.partial(faces_x_kernel, nx, ny, count_z),
        [(rows, depth), (LAYERS, ny, depth), (LAYERS, ny, depth)],
    )(fields, from_low, from_high)
    x_low = shifted(face_high, "gx", 1)
    x_high = shifted(face_low, "gx", -1)
    face_low, face_high = call(
        functools.partial(faces_y_kernel, nx, ny), [(LAYERS, ex, depth)] * 2
    )(fields, strip, x_low, x_high)
    y_low = shifted(face_high, "gy", 1)
    y_high = shifted(face_low, "gy", -1)
    electric, magnetic, result = call(
        steps_kernel,
        [electric.shape, electric.shape, (buckets, 8, slots)],
        [
            pltpu.VMEM((FIELDS, ex, ey, ez), jnp.float32),
            pltpu.VMEM((ex, ey, depth), jnp.float32),
            pltpu.VMEM((3, ex, ey, ez), jnp.float32),
        ]
        + hots,
    )(fields, strip, x_low, x_high, y_low, y_high, arrived, states)
    home = lax.all_to_all(result, ("gy", "gz"), split_axis=0, concat_axis=0, tiled=True)
    home = jnp.moveaxis(home, 1, 0)
    polar_out = home[0:6].reshape(polarization.shape)
    popul_out = home[6:8].reshape(populations.shape)
    return (electric, magnetic, polar_out, popul_out)


def solution(mesh):
    owners = P("gx", ("gy", "gz"), None)
    return jax.shard_map(
        shards,
        mesh=mesh,
        in_specs=(
            P(None, "gx", "gy", "gz"),
            P("gx", "gy", "gz"),
            owners,
            P(None, None, "gx", ("gy", "gz"), None),
            P(None, "gx", ("gy", "gz"), None),
            owners,
            owners,
            owners,
            owners,
        ),
        out_specs=(
            P(None, "gx", "gy", "gz"),
            P(None, "gx", "gy", "gz"),
            P(None, None, "gx", ("gy", "gz"), None),
            P(None, "gx", ("gy", "gz"), None),
        ),
        check_vma=False,
    )
```

time: 222 us -> 86.8 us (0.39)
  the two profiles are of different devices: /device:TPU:21 before, /device:TPU:0 now
where the time goes in v1:
time: 86.8 us; the launch traced here: 86.3 us
  waiting for transfers between devices  28.3 us (33%)
  Pallas kernels  26.9 us (31%)
  blocking collectives  18.4 us (21%)
  starting transfers between devices  8.68 us (10%)
  local copies, waits for them, and re-layouts  3.35 us (4%)
    ppermute x4, waiting for transfers between devices, shifted(): return lax.ppermute(value, axis, pairs)  26.9 us
    pallas_call x1, Pallas kernels, shards(): call(steps_kernel, [electric.shape, electric.shape, (buckets, 8, slots)],...  15.3 us
    all_to_all x1, blocking collectives, shards(): lax.all_to_all(packed, ('gy', 'gz'), split_axis=0, concat_axis=0, tiled=T...  10.3 us
    ppermute x4, starting transfers between devices, shifted(): return lax.ppermute(value, axis, pairs)  8.67 us
    all_to_all x1, blocking collectives, shards(): lax.all_to_all(result, ('gy', 'gz'), split_axis=0, concat_axis=0, tiled=T...  8.08 us
    pallas_call x1, Pallas kernels, shards(): call(first_kernel, [(FIELDS, rows, depth), (rows, depth), (8, buckets, sl...  5.11 us
    unnamed x11, local copies, waits for them, and re-layouts  2.73 us
    pallas_call x1, Pallas kernels, shards(): call(functools.partial(faces_y_kernel, nx, ny), [(LAYERS, ex, depth)] * 2)  2.71 us
  transfers between devices with their start and end apart: 5, of which 5 were waited for; matrix products, arithmetic and copies ran while one was open for 0% of the time, Pallas kernels for 0%

profile of v1, /device:TPU:0, one launch (start us, length us, event | category | flops | bytes accessed | tf_op | source)
XLA Modules:
  0.0 86.3 jit_solution(6011698206886420376)
XLA Ops:
  0.6 1.5 %shard_map.120 = f32[8,13,128]{2,1,0:T(8,128)} custom-call(s32[1,8,128]{2,1,0:T(8,128)} %index.1, f32[2,3,1,8,128]{4,3,2,1,0:T(8,128)} %polar.1, f32[2,1,8,128]{3,2,1,0:T(8,128)} %popul.1, f32[1,8,128]{2,1,0:T(8,128)} %freq.1, f32[1,8,128]{2,1,0:T(8,128)} %dephase.1, f32[1,8,128]{2,1,0:T(8,128)} %strength.1, f32[1,8,128]{2,1,0:T(8,128)} %pumping.1), custom_call_target="tpu_custom_call" | custom-call | tf_op jit(solution)/shard_map/pallas_call | solution.py:379
  2.1 10.3 %all_to_all.10.arrived = f32[8,13,128]{2,1,0:T(8,128)} all-to-all(f32[8,13,128]{2,1,0:T(8,128)} %shard_map.120), channel_id=1, replica_groups=mesh['gx'=4,'gy'=4,'gz'=2] {'gy','gz'}, dimensions={0} | all-to-all | bytes 106496 | tf_op jit(solution)/shard_map/all_to_all | solution.py:382
  12.4 5.1 %shard_map.121 = (f32[20,128,128]{2,1,0:T(8,128)}, f32[128,128]{1,0:T(8,128)}, f32[8,8,128]{2,1,0:T(8,128)}) custom-call(f32[8,13,128]{2,1,0:T(8,128)} %all_to_all.10.arrived, f32[3,8,16,128]{3,2,1,0:T(8,128)} %electric.1, s32[8,16,128]{2,1,0:T(8,128)} %classes.1), custom_call_target="tpu_custom_call" | custom-call | tf_op jit(solution)/shard_map/pallas_call | solution.py:383
  17.5 0.0 collective-permute-start
  17.5 1.5 %collective-permute-done.refs_0_.refs_1_ = f32[128,128]{1,0:T(8,128)S(1)} collective-permute-done((f32[128,128]{1,0:T(8,128)}, f32[128,128]{1,0:T(8,128)S(1)}, u32[]{:S(2)}, u32[]{:S(2)}) %collective-permute-start) | collective-permute-done | bytes 65568 | tf_op jit(solution)/shard_map/ppermute | solution.py:390
  18.9 0.0 copy-start.4
  18.9 0.6 copy-done.4
  19.6 2.3 %shard_map.122 = (f32[128,128]{1,0:T(8,128)}, f32[45,16,128]{2,1,0:T(8,128)}, f32[45,16,128]{2,1,0:T(8,128)}) custom-call(f32[20,128,128]{2,1,0:T(8,128)} %get-tuple-element.15.fields, f32[128,128]{1,0:T(8,128)} %copy-done.4, f32[128,128]{1,0:T(8,128)} %copy-done.4), custom_call_target="tpu_custom_call" | custom-call | tf_op jit(solution)/shard_map/pallas_call | solution.py:394
  21.9 3.6 %collective-permute-start.1 = (f32[45,16,128]{2,1,0:T(8,128)}, f32[45,16,128]{2,1,0:T(8,128)S(1)}, u32[]{:S(2)}, u32[]{:S(2)}) collective-permute-start(f32[45,16,128]{2,1,0:T(8,128)} %get-tuple-element.18), channel_id=1, source_target_pairs={{0,8},{8,16},{16,24},{1,9},{9,17},{17,25},{2,10},{10,18},{18,26},{... | collective-permute-start | bytes 1105928 | tf_op jit(solution)/shard_map/ppermute | solution.py:364
  25.5 1.3 %collective-permute-start.2 = (f32[45,16,128]{2,1,0:T(8,128)}, f32[45,16,128]{2,1,0:T(8,128)S(1)}, u32[]{:S(2)}, u32[]{:S(2)}) collective-permute-start(f32[45,16,128]{2,1,0:T(8,128)} %get-tuple-element.19), channel_id=1, source_target_pairs={{8,0},{16,8},{24,16},{9,1},{17,9},{25,17},{10,2},{18,10},{26,18},{... | collective-permute-start | bytes 1105928 | tf_op jit(solution)/shard_map/ppermute | solution.py:364
  26.8 7.1 %collective-permute-done.1.halo_low.x_low = f32[45,16,128]{2,1,0:T(8,128)S(1)} collective-permute-done((f32[45,16,128]{2,1,0:T(8,128)}, f32[45,16,128]{2,1,0:T(8,128)S(1)}, u32[]{:S(2)}, u32[]{:S(2)}) %collective-permute-start.1) | collective-permute-done | bytes 368672 | tf_op jit(solution)/shard_map/ppermute | solution.py:364
  33.9 0.0 copy-start
  33.9 4.0 %collective-permute-done.2.halo_high.x_high = f32[45,16,128]{2,1,0:T(8,128)S(1)} collective-permute-done((f32[45,16,128]{2,1,0:T(8,128)}, f32[45,16,128]{2,1,0:T(8,128)S(1)}, u32[]{:S(2)}, u32[]{:S(2)}) %collective-permute-start.2) | collective-permute-done | bytes 368672 | tf_op jit(solution)/shard_map/ppermute | solution.py:364
  38.0 0.0 copy-start.1
  38.0 0.0 copy-done
  38.0 0.7 copy-done.1
  38.7 2.7 %shard_map.123 = (f32[45,16,128]{2,1,0:T(8,128)}, f32[45,16,128]{2,1,0:T(8,128)}) custom-call(f32[20,128,128]{2,1,0:T(8,128)} %get-tuple-element.15.fields, f32[128,128]{1,0:T(8,128)} %get-tuple-element.17.strip, f32[45,16,128]{2,1,0:T(8,128)} %copy-done, f32[45,16,128]{2,1,0:T(8,128)} %copy-done.1), custom_call_target="tpu_custom_call" | custom-call | tf_op jit(solution)/shard_map/pallas_call | solution.py:400
  41.4 2.5 %collective-permute-start.3 = (f32[45,16,128]{2,1,0:T(8,128)}, f32[45,16,128]{2,1,0:T(8,128)S(1)}, u32[]{:S(2)}, u32[]{:S(2)}) collective-permute-start(f32[45,16,128]{2,1,0:T(8,128)} %get-tuple-element.20), channel_id=1, source_target_pairs={{0,2},{2,4},{4,6},{1,3},{3,5},{5,7},{8,10},{10,12},{12,14},{9,11},... | collective-permute-start | bytes 1105928 | tf_op jit(solution)/shard_map/ppermute | solution.py:364
  43.9 1.3 %collective-permute-start.4 = (f32[45,16,128]{2,1,0:T(8,128)}, f32[45,16,128]{2,1,0:T(8,128)S(1)}, u32[]{:S(2)}, u32[]{:S(2)}) collective-permute-start(f32[45,16,128]{2,1,0:T(8,128)} %get-tuple-element.21), channel_id=1, source_target_pairs={{2,0},{4,2},{6,4},{3,1},{5,3},{7,5},{10,8},{12,10},{14,12},{11,9},... | collective-permute-start | bytes 1105928 | tf_op jit(solution)/shard_map/ppermute | solution.py:364
  45.2 6.0 %collective-permute-done.3.y_low = f32[45,16,128]{2,1,0:T(8,128)S(1)} collective-permute-done((f32[45,16,128]{2,1,0:T(8,128)}, f32[45,16,128]{2,1,0:T(8,128)S(1)}, u32[]{:S(2)}, u32[]{:S(2)}) %collective-permute-start.3) | collective-permute-done | bytes 368672 | tf_op jit(solution)/shard_map/ppermute | solution.py:364
  51.2 0.0 copy-start.2
  51.2 9.7 %collective-permute-done.4.y_high = f32[45,16,128]{2,1,0:T(8,128)S(1)} collective-permute-done((f32[45,16,128]{2,1,0:T(8,128)}, f32[45,16,128]{2,1,0:T(8,128)S(1)}, u32[]{:S(2)}, u32[]{:S(2)}) %collective-permute-start.4) | collective-permute-done | bytes 368672 | tf_op jit(solution)/shard_map/ppermute | solution.py:364
  60.9 0.0 copy-start.3
  60.9 0.0 copy-done.2
  60.9 0.7 copy-done.3
  61.6 15.3 %shard_map.124 = (f32[3,8,16,128]{3,2,1,0:T(8,128)}, f32[3,8,16,128]{3,2,1,0:T(8,128)}, f32[8,8,128]{2,1,0:T(8,128)}) custom-call(f32[20,128,128]{2,1,0:T(8,128)} %get-tuple-element.15.fields, f32[128,128]{1,0:T(8,128)} %get-tuple-element.17.strip, f32[45,16,128]{2,1,0:T(8,128)} %copy-done, f32[45,16,128]{2,1,0:T(8,128)} %copy-done.1, ...), custom_call_target="tpu_custom_call" | custom-call | tf_op jit(solution)/shard_map/pallas_call | solution.py:405
  77.0 8.1 %all_to_all.11 = f32[8,8,128]{2,1,0:T(8,128)S(1)} all-to-all(f32[8,8,128]{2,1,0:T(8,128)} %get-tuple-element.25), channel_id=1, replica_groups=mesh['gx'=4,'gy'=4,'gz'=2] {'gy','gz'}, dimensions={0} | all-to-all | bytes 65536 | tf_op jit(solution)/shard_map/all_to_all | solution.py:415
  85.0 0.6 copy.17
  85.7 0.6 copy.15
  (1 shorter events, 0.0 us)
Async XLA Ops:
  17.5 1.5 %collective-permute-start = (f32[128,128]{1,0:T(8,128)}, f32[128,128]{1,0:T(8,128)S(1)}, u32[]{:S(2)}, u32[]{:S(2)}) collective-permute-start(f32[128,128]{1,0:T(8,128)} %get-tuple-element.16), channel_id=1, source_target_pairs={{0,1},{1,0},{2,3},{3,2},{4,5},{5,4},{6,7},{7,6},{8,9},{9,8},{10,11... | collective-permute-start | bytes 196616 | tf_op jit(solution)/shard_map/ppermute | solution.py:390
  18.9 0.6 copy-start.4
  21.9 12.1 %collective-permute-start.1 = (f32[45,16,128]{2,1,0:T(8,128)}, f32[45,16,128]{2,1,0:T(8,128)S(1)}, u32[]{:S(2)}, u32[]{:S(2)}) collective-permute-start(f32[45,16,128]{2,1,0:T(8,128)} %get-tuple-element.18), channel_id=1, source_target_pairs={{0,8},{8,16},{16,24},{1,9},{9,17},{17,25},{2,10},{10,18},{18,26},{... | collective-permute-start | bytes 1105928 | tf_op jit(solution)/shard_map/ppermute | solution.py:364
  25.5 12.5 %collective-permute-start.2 = (f32[45,16,128]{2,1,0:T(8,128)}, f32[45,16,128]{2,1,0:T(8,128)S(1)}, u32[]{:S(2)}, u32[]{:S(2)}) collective-permute-start(f32[45,16,128]{2,1,0:T(8,128)} %get-tuple-element.19), channel_id=1, source_target_pairs={{8,0},{16,8},{24,16},{9,1},{17,9},{25,17},{10,2},{18,10},{26,18},{... | collective-permute-start | bytes 1105928 | tf_op jit(solution)/shard_map/ppermute | solution.py:364
  33.9 4.0 %copy-start = (f32[45,16,128]{2,1,0:T(8,128)}, f32[45,16,128]{2,1,0:T(8,128)S(1)}, u32[]{:S(2)}) copy-start(f32[45,16,128]{2,1,0:T(8,128)S(1)} %collective-permute-done.1.halo_low.x_low) | copy-start | bytes 1105924
  38.0 0.8 copy-start.1
  41.4 9.8 %collective-permute-start.3 = (f32[45,16,128]{2,1,0:T(8,128)}, f32[45,16,128]{2,1,0:T(8,128)S(1)}, u32[]{:S(2)}, u32[]{:S(2)}) collective-permute-start(f32[45,16,128]{2,1,0:T(8,128)} %get-tuple-element.20), channel_id=1, source_target_pairs={{0,2},{2,4},{4,6},{1,3},{3,5},{5,7},{8,10},{10,12},{12,14},{9,11},... | collective-permute-start | bytes 1105928 | tf_op jit(solution)/shard_map/ppermute | solution.py:364
  43.9 17.0 %collective-permute-start.4 = (f32[45,16,128]{2,1,0:T(8,128)}, f32[45,16,128]{2,1,0:T(8,128)S(1)}, u32[]{:S(2)}, u32[]{:S(2)}) collective-permute-start(f32[45,16,128]{2,1,0:T(8,128)} %get-tuple-element.21), channel_id=1, source_target_pairs={{2,0},{4,2},{6,4},{3,1},{5,3},{7,5},{10,8},{12,10},{14,12},{11,9},... | collective-permute-start | bytes 1105928 | tf_op jit(solution)/shard_map/ppermute | solution.py:364
  51.2 9.7 %copy-start.2 = (f32[45,16,128]{2,1,0:T(8,128)}, f32[45,16,128]{2,1,0:T(8,128)S(1)}, u32[]{:S(2)}) copy-start(f32[45,16,128]{2,1,0:T(8,128)S(1)} %collective-permute-done.3.y_low) | copy-start | bytes 1105924
  60.9 0.7 copy-start.3

commit v2 on v1

--- a/solution.py
+++ b/solution.py
@@ -17,11 +17,40 @@
 WIDTHS = (STEPS,) * 3 + (STEPS - 1,) * 4 + (STEPS - 2,) * 4 + (STEPS - 3,) * 9
 FIELDS = len(WIDTHS)
 ALL_WIDTHS = WIDTHS + (STEPS,)
-BASES = tuple(sum(ALL_WIDTHS[:i]) for i in range(FIELDS + 1))
-LAYERS = sum(ALL_WIDTHS)
+VECTORS = (0, 4, 7, 11)
 LANE_BASES = tuple(2 * sum(WIDTHS[:i]) for i in range(FIELDS))
 LANES = 128
 VMEM_LIMIT = 56 * 1024 * 1024
+
+
+def layer_list(skip_axis):
+    layers = []
+    for f, width in enumerate(ALL_WIDTHS):
+        unused = skip_axis is not None and f - skip_axis in VECTORS
+        layers += [(f, d) for d in range(width - 1 if unused else width)]
+    return layers
+
+
+LAYERS_LOW = (layer_list(0), layer_list(1))
+LAYERS_HIGH = layer_list(None)
+
+
+def corner_rows(layers, halo_sign):
+    out = []
+    for f, d in layers:
+        width = ALL_WIDTHS[f]
+        for side in (-1, 1):
+            reach = width - d if side != halo_sign else width - 1 - d
+            for e in range(reach):
+                known = LAYERS_HIGH if side < 0 else LAYERS_LOW[0]
+                if (f, e) in known:
+                    out.append((f, d, side, e))
+    return out
+
+
+def face_rows(layers, halo_sign, nx):
+    count = len(layers) * nx + len(corner_rows(layers, halo_sign))
+    return -(-count // 8) * 8
 
 
 def inverse_permittivity(classes):
@@ -189,28 +218,28 @@
         jnp.where(me > 0, from_low[...], 0.0),
         jnp.where(me < count_z - 1, from_high[...], 0.0),
     )
-    for f, width in enumerate(ALL_WIDTHS):
+    for at, (f, d) in enumerate(LAYERS_LOW[0]):
         source = fields.at[f] if f < FIELDS else strip
-        for d in range(width):
-            low[BASES[f] + d] = source[d * ny : (d + 1) * ny, :]
-            high[BASES[f] + d] = source[(nx - 1 - d) * ny : (nx - d) * ny, :]
+        low[at] = source[d * ny : (d + 1) * ny, :]
+    for at, (f, d) in enumerate(LAYERS_HIGH):
+        source = fields.at[f] if f < FIELDS else strip
+        high[at] = source[(nx - 1 - d) * ny : (nx - d) * ny, :]
 
 
 def faces_y_kernel(nx, ny, fields, strip, halo_low, halo_high, low, high):
-    for f, width in enumerate(ALL_WIDTHS):
-        source = fields.at[f] if f < FIELDS else strip
-        for d in range(width):
-            for face, y in ((low, d), (high, ny - 1 - d)):
-                at = BASES[f] + d
-                face[at, 0:nx, :] = source[pl.ds(y, nx, stride=ny), :]
-                if width < STEPS:
-                    face[at, nx : nx + 2 * STEPS, :] = jnp.zeros(
-                        (2 * STEPS, face.shape[2]), jnp.float32
-                    )
-                for e in range(width):
-                    face[at, nx + e : nx + e + 1, :] = halo_high[BASES[f] + e, y : y + 1, :]
-                    last = nx + 2 * STEPS - 1 - e
-                    face[at, last : last + 1, :] = halo_low[BASES[f] + e, y : y + 1, :]
+    for face, layers, sign in ((low, LAYERS_LOW[1], -1), (high, LAYERS_HIGH, 1)):
+        for at, (f, d) in enumerate(layers):
+            source = fields.at[f] if f < FIELDS else strip
+            y = d if sign < 0 else ny - 1 - d
+            face[at * nx : (at + 1) * nx, :] = source[pl.ds(y, nx, stride=ny), :]
+        for row, (f, d, side, e) in enumerate(corner_rows(layers, -sign)):
+            y = d if sign < 0 else ny - 1 - d
+            if side < 0:
+                value = halo_low[LAYERS_HIGH.index((f, e)), y : y + 1, :]
+            else:
+                value = halo_high[LAYERS_LOW[0].index((f, e)), y : y + 1, :]
+            at = len(layers) * nx + row
+            face[at : at + 1, :] = value
 
 
 def steps_kernel(
@@ -222,29 +251,34 @@
     rows = nx * ny
     ex, ey, ez = nx + 2 * STEPS, ny + 2 * STEPS, 2 * depth
 
-    for f, width in enumerate(ALL_WIDTHS):
+    def target(f):
+        return wide.at[f] if f < FIELDS else wide_strip
+
+    for f in range(FIELDS + 1):
         source = fields.at[f] if f < FIELDS else strip
-        target = wide.at[f] if f < FIELDS else wide_strip
-        target[STEPS : STEPS + nx, 0:ny, 0:depth] = source[...].reshape(nx, ny, depth)
-        target[:, ny : ny + 2 * STEPS, 0:depth] = jnp.zeros((ex, 2 * STEPS, depth), jnp.float32)
-        for d in range(width):
-            at = BASES[f] + d
-            target[STEPS - 1 - d, 0:ny, 0:depth] = x_low[at]
-            target[STEPS + nx + d, 0:ny, 0:depth] = x_high[at]
-            for halo, y in ((y_low, ey - 1 - d), (y_high, ny + d)):
-                for x in range(ex):
-                    row = (x - STEPS) % ex
-                    target[x, y : y + 1, 0:depth] = halo[at, row : row + 1, :]
-
-    def spread(x, carry):
+        target(f)[STEPS : STEPS + nx, 0:ny, 0:depth] = source[...].reshape(nx, ny, depth)
+        target(f)[:, ny : ny + 2 * STEPS, 0:depth] = jnp.zeros((ex, 2 * STEPS, depth), jnp.float32)
+    for at, (f, d) in enumerate(LAYERS_HIGH):
+        target(f)[STEPS - 1 - d, 0:ny, 0:depth] = x_low[at]
+    for at, (f, d) in enumerate(LAYERS_LOW[0]):
+        target(f)[STEPS + nx + d, 0:ny, 0:depth] = x_high[at]
+    for halo, layers, sign in ((y_low, LAYERS_HIGH, -1), (y_high, LAYERS_LOW[1], 1)):
+        for at, (f, d) in enumerate(layers):
+            y = ey - 1 - d if sign < 0 else ny + d
+            for x in range(nx):
+                target(f)[STEPS + x, y : y + 1, 0:depth] = halo[at * nx + x : at * nx + x + 1, :]
+        for row, (f, d, side, e) in enumerate(corner_rows(layers, sign)):
+            y = ey - 1 - d if sign < 0 else ny + d
+            x = STEPS - 1 - e if side < 0 else STEPS + nx + e
+            at = len(layers) * nx + row
+            target(f)[x, y : y + 1, 0:depth] = halo[at : at + 1, :]
+
+    for x in range(ex):
         value = wide_strip[x]
         for f, width in enumerate(WIDTHS):
             wide[f, x, :, depth:ez] = pltpu.roll(
                 value, (-(LANE_BASES[f] + width)) % depth, 1
             )
-        return carry
-
-    lax.fori_loop(0, ex, spread, 0)
     row_at = lax.broadcasted_iota(jnp.int32, (ey, ez), 0)
     lane_at = lax.broadcasted_iota(jnp.int32, (ey, ez), 1)
     outside = ((row_at >= ey - STEPS) & (lax.axis_index("gy") == 0)) | (
@@ -281,7 +315,7 @@
             (up_z(e0) - e0) - (f2 - e2),
             (f1 - e1) - (up_y(e0) - e0),
         )
-        mask = inside * jnp.where(first_x & (x < STEPS), 0.0, 1.0)
+        mask = inside * jnp.where(first_x, 0.0, 1.0) if x < STEPS else inside
         for c in range(3):
             change = -TIME_STEP * curl[c]
             if step > 1:
@@ -334,12 +368,9 @@
             current = advanced
         advance_magnetic(step, step - 1)
 
-        def body(x, carry, step=step):
+        for x in range(step, ex - step):
             advance_magnetic(step, x)
             advance_electric(step, x)
-            return carry
-
-        lax.fori_loop(step, ex - step, body, 0)
     for c in range(3):
         electric[c] = wide[c, STEPS : STEPS + nx, 0:ny, 0:depth]
         magnetic[c] = field[c, STEPS : STEPS + nx, 0:ny, 0:depth]
@@ -349,13 +380,21 @@
     result[:, 7, :] = pumped
 
 
-def call(kernel, out_shapes, scratch=()):
+def call(kernel, out_shapes, scratch=(), final=0):
+    shapes = [
+        jax.ShapeDtypeStruct(s, jnp.float32) if i < final else pltpu.VMEM(s, jnp.float32)
+        for i, s in enumerate(out_shapes)
+    ]
     return pl.pallas_call(
         kernel,
-        out_shape=[jax.ShapeDtypeStruct(s, jnp.float32) for s in out_shapes],
+        out_shape=shapes,
         scratch_shapes=list(scratch),
         compiler_params=pltpu.CompilerParams(vmem_limit_bytes=VMEM_LIMIT),
     )
+
+
+def near(*values):
+    return [pltpu.with_memory_space_constraint(v, pltpu.VMEM) for v in values]
 
 
 def shifted(value, axis, step):
@@ -380,11 +419,13 @@
         cell_index, polarization, populations, resonance, dephasing, coupling, pump_rate
     )
     arrived = lax.all_to_all(packed, ("gy", "gz"), split_axis=0, concat_axis=0, tiled=True)
+    (arrived,) = near(arrived)
     fields, strip, states = call(
         first_kernel,
         [(FIELDS, rows, depth), (rows, depth), (8, buckets, slots)],
         hots,
     )(arrived, electric, permittivity_class)
+    fields, strip, states = near(fields, strip, states)
     count_z = lax.axis_size("gz")
     if count_z == 2:
         from_low = from_high = lax.ppermute(strip, "gz", [(0, 1), (1, 0)])
@@ -393,15 +434,22 @@
         from_high = shifted(strip, "gz", -1)
     strip, face_low, face_high = call(
         functools.partial(faces_x_kernel, nx, ny, count_z),
-        [(rows, depth), (LAYERS, ny, depth), (LAYERS, ny, depth)],
-    )(fields, from_low, from_high)
+        [(rows, depth), (len(LAYERS_LOW[0]), ny, depth), (len(LAYERS_HIGH), ny, depth)],
+    )(fields, *near(from_low, from_high))
+    (strip,) = near(strip)
     x_low = shifted(face_high, "gx", 1)
     x_high = shifted(face_low, "gx", -1)
+    x_low, x_high = near(x_low, x_high)
     face_low, face_high = call(
-        functools.partial(faces_y_kernel, nx, ny), [(LAYERS, ex, depth)] * 2
+        functools.partial(faces_y_kernel, nx, ny),
+        [
+            (face_rows(LAYERS_LOW[1], 1, nx), depth),
+            (face_rows(LAYERS_HIGH, -1, nx), depth),
+        ],
     )(fields, strip, x_low, x_high)
     y_low = shifted(face_high, "gy", 1)
     y_high = shifted(face_low, "gy", -1)
+    y_low, y_high = near(y_low, y_high)
     electric, magnetic, result = call(
         steps_kernel,
         [electric.shape, electric.shape, (buckets, 8, slots)],
@@ -411,6 +459,7 @@
             pltpu.VMEM((3, ex, ey, ez), jnp.float32),
         ]
         + hots,
+        final=2,
     )(fields, strip, x_low, x_high, y_low, y_high, arrived, states)
     home = lax.all_to_all(result, ("gy", "gz"), split_axis=0, concat_axis=0, tiled=True)
     home = jnp.moveaxis(home, 1, 0)

time: 86.8 us -> 61.2 us (0.71)
  Pallas kernels: 26.9 us -> 11.5 us
  waiting for transfers between devices: 28.3 us -> 21.6 us
  local copies, waits for them, and re-layouts: 3.35 us -> 1.22 us
  blocking collectives: 18.4 us -> 17.2 us
    pallas_call x1, Pallas kernels: 15.3 us -> 6.36 us  [shards(): call(steps_kernel, [electric.shape, electric.shape, (buckets, 8, slots)],...]
    ppermute x4, waiting for transfers between devices: 26.9 us -> 20.3 us  [shifted(): return lax.ppermute(value, axis, pairs)]
    pallas_call x1, Pallas kernels: 2.71 us -> 0.21 us  [shards(): call(functools.partial(faces_y_kernel, nx, ny), [(face_rows(LAYERS_LOW[1]...]
    pallas_call x1, Pallas kernels: 2.28 us -> 0.06 us  [shards(): call(functools.partial(faces_x_kernel, nx, ny, count_z), [(rows, depth),...]
    unnamed x11 -> x1, local copies, waits for them, and re-layouts: 2.73 us -> 0.6 us
    pallas_call x1, Pallas kernels: 5.11 us -> 4.05 us  [shards(): call(first_kernel, [(FIELDS, rows, depth), (rows, depth), (8, buckets, sl...]
    all_to_all x1, blocking collectives: 8.08 us -> 7.2 us  [shards(): lax.all_to_all(result, ('gy', 'gz'), split_axis=0, concat_axis=0, tiled=T...]
  transfers between devices with their start and end apart: 5 -> 5, of which waited for: 5 -> 3; matrix products, arithmetic and copies ran while one was open for 0% -> 0% of each run, Pallas kernels for 0% -> 0%
where the time goes in v2:
time: 61.2 us; the launch traced here: 60.8 us
  waiting for transfers between devices  21.6 us (35%)
  blocking collectives  17.2 us (28%)
  Pallas kernels  11.5 us (19%)
  starting transfers between devices  8.64 us (14%)
  local copies, waits for them, and re-layouts  1.22 us (2%)
  between operations  0.7 us (1%)
    ppermute x4, waiting for transfers between devices, shifted(): return lax.ppermute(value, axis, pairs)  20.3 us
    all_to_all x1, blocking collectives, shards(): lax.all_to_all(packed, ('gy', 'gz'), split_axis=0, concat_axis=0, tiled=T...  9.99 us
    ppermute x4, starting transfers between devices, shifted(): return lax.ppermute(value, axis, pairs)  8.57 us
    all_to_all x1, blocking collectives, shards(): lax.all_to_all(result, ('gy', 'gz'), split_axis=0, concat_axis=0, tiled=T...  7.2 us
    pallas_call x1, Pallas kernels, shards(): call(steps_kernel, [electric.shape, electric.shape, (buckets, 8, slots)],...  6.36 us
    pallas_call x1, Pallas kernels, shards(): call(first_kernel, [(FIELDS, rows, depth), (rows, depth), (8, buckets, sl...  4.05 us
    ppermute x1, waiting for transfers between devices, shards(): from_low = from_high = lax.ppermute(strip, 'gz', [(0, 1), (1, 0)])  1.24 us
  transfers between devices with their start and end apart: 5, of which 3 were waited for; matrix products, arithmetic and copies ran while one was open for 0% of the time, Pallas kernels for 0%

profile of v2, /device:TPU:0, one launch (start us, length us, event | category | flops | bytes accessed | tf_op | source)
XLA Modules:
  0.0 60.8 jit_solution(4154132895025938360)
XLA Ops:
  0.6 0.8 %shard_map.120 = f32[8,13,128]{2,1,0:T(8,128)S(1)} custom-call(s32[1,8,128]{2,1,0:T(8,128)} %index.1, f32[2,3,1,8,128]{4,3,2,1,0:T(8,128)} %polar.1, f32[2,1,8,128]{3,2,1,0:T(8,128)} %popul.1, f32[1,8,128]{2,1,0:T(8,128)} %freq.1, f32[1,8,128]{2,1,0:T(8,128)} %dephase.1, f32[1,8,128]{2,1,0:T(8,128)} %strength.1, f32[1,8,128]{2,1,0:T(8,128)} %pumping.1), custom_call_target="tpu_custom_call" | custom-call | tf_op jit(solution)/shard_map/pallas_call | solution.py:418
  1.5 10.0 %all_to_all.10.arrived = f32[8,13,128]{2,1,0:T(8,128)S(1)} all-to-all(f32[8,13,128]{2,1,0:T(8,128)S(1)} %shard_map.120), channel_id=1, replica_groups=mesh['gx'=4,'gy'=4,'gz'=2] {'gy','gz'}, dimensions={0} | all-to-all | bytes 106496 | tf_op jit(solution)/shard_map/all_to_all | solution.py:421
  11.4 4.0 %shard_map.121 = (f32[20,128,128]{2,1,0:T(8,128)S(1)}, f32[128,128]{1,0:T(8,128)S(1)}, f32[8,8,128]{2,1,0:T(8,128)S(1)}) custom-call(f32[8,13,128]{2,1,0:T(8,128)S(1)} %all_to_all.10.arrived, f32[3,8,16,128]{3,2,1,0:T(8,128)} %electric.1, s32[8,16,128]{2,1,0:T(8,128)} %classes.1), custom_call_target="tpu_custom_call" | custom-call | tf_op jit(solution)/shard_map/pallas_call | solution.py:423
  15.5 0.1 collective-permute-start
  15.6 1.2 %collective-permute-done.refs_0_.refs_1_ = f32[128,128]{1,0:T(8,128)S(1)} collective-permute-done((f32[128,128]{1,0:T(8,128)S(1)}, f32[128,128]{1,0:T(8,128)S(1)}, u32[]{:S(2)}, u32[]{:S(2)}) %collective-permute-start) | collective-permute-done | bytes 65568 | tf_op jit(solution)/shard_map/ppermute | solution.py:431
  16.8 0.1 shard_map.122
  16.9 3.5 %collective-permute-start.1 = (f32[45,16,128]{2,1,0:T(8,128)S(1)}, f32[45,16,128]{2,1,0:T(8,128)S(1)}, u32[]{:S(2)}, u32[]{:S(2)}) collective-permute-start(f32[45,16,128]{2,1,0:T(8,128)S(1)} %get-tuple-element.18), channel_id=1, source_target_pairs={{0,8},{8,16},{16,24},{1,9},{9,17},{17,25},{2,10},{10,18},{18,26},{... | collective-permute-start | bytes 1105928 | tf_op jit(solution)/shard_map/ppermute | solution.py:403
  20.4 1.3 %collective-permute-start.2 = (f32[41,16,128]{2,1,0:T(8,128)S(1)}, f32[41,16,128]{2,1,0:T(8,128)S(1)}, u32[]{:S(2)}, u32[]{:S(2)}) collective-permute-start(f32[41,16,128]{2,1,0:T(8,128)S(1)} %get-tuple-element.19), channel_id=1, source_target_pairs={{8,0},{16,8},{24,16},{9,1},{17,9},{25,17},{10,2},{18,10},{26,18},{... | collective-permute-start | bytes 1007624 | tf_op jit(solution)/shard_map/ppermute | solution.py:403
  21.7 10.3 %collective-permute-done.2.halo_high.x_high = f32[41,16,128]{2,1,0:T(8,128)S(1)} collective-permute-done((f32[41,16,128]{2,1,0:T(8,128)S(1)}, f32[41,16,128]{2,1,0:T(8,128)S(1)}, u32[]{:S(2)}, u32[]{:S(2)}) %collective-permute-start.2) | collective-permute-done | bytes 335904 | tf_op jit(solution)/shard_map/ppermute | solution.py:403
  32.0 0.0 collective-permute-done.1.halo_low.x_low
  32.0 0.2 shard_map.123
  32.2 2.5 %collective-permute-start.3 = (f32[488,128]{1,0:T(8,128)S(1)}, f32[488,128]{1,0:T(8,128)S(1)}, u32[]{:S(2)}, u32[]{:S(2)}) collective-permute-start(f32[488,128]{1,0:T(8,128)S(1)} %get-tuple-element.20), channel_id=1, source_target_pairs={{0,2},{2,4},{4,6},{1,3},{3,5},{5,7},{8,10},{10,12},{12,14},{9,11},... | collective-permute-start | bytes 749576 | tf_op jit(solution)/shard_map/ppermute | solution.py:403
  34.7 1.3 %collective-permute-start.4 = (f32[456,128]{1,0:T(8,128)S(1)}, f32[456,128]{1,0:T(8,128)S(1)}, u32[]{:S(2)}, u32[]{:S(2)}) collective-permute-start(f32[456,128]{1,0:T(8,128)S(1)} %get-tuple-element.21), channel_id=1, source_target_pairs={{2,0},{4,2},{6,4},{3,1},{5,3},{7,5},{10,8},{12,10},{14,12},{11,9},... | collective-permute-start | bytes 700424 | tf_op jit(solution)/shard_map/ppermute | solution.py:403
  36.0 10.1 %collective-permute-done.4.y_high = f32[456,128]{1,0:T(8,128)S(1)} collective-permute-done((f32[456,128]{1,0:T(8,128)S(1)}, f32[456,128]{1,0:T(8,128)S(1)}, u32[]{:S(2)}, u32[]{:S(2)}) %collective-permute-start.4) | collective-permute-done | bytes 233504 | tf_op jit(solution)/shard_map/ppermute | solution.py:403
  46.0 0.0 collective-permute-done.3.y_low
  46.0 6.4 %shard_map.124 = (f32[3,8,16,128]{3,2,1,0:T(8,128)}, f32[3,8,16,128]{3,2,1,0:T(8,128)}, f32[8,8,128]{2,1,0:T(8,128)S(1)}) custom-call(f32[20,128,128]{2,1,0:T(8,128)S(1)} %get-tuple-element.15.fields, f32[128,128]{1,0:T(8,128)S(1)} %get-tuple-element.17.strip, f32[45,16,128]{2,1,0:T(8,128)S(1)} %collective-permute-done.1.halo_low.x_low, ...), custom_call_target="tpu_custom_call" | custom-call | tf_op jit(solution)/shard_map/pallas_call | solution.py:453
  52.4 7.2 %all_to_all.11 = f32[8,8,128]{2,1,0:T(8,128)S(1)} all-to-all(f32[8,8,128]{2,1,0:T(8,128)S(1)} %get-tuple-element.25), channel_id=1, replica_groups=mesh['gx'=4,'gy'=4,'gz'=2] {'gy','gz'}, dimensions={0} | all-to-all | bytes 65536 | tf_op jit(solution)/shard_map/all_to_all | solution.py:464
  59.6 0.6 copy.17
  60.2 0.6 %copy.15 = f32[6,8,128]{2,1,0:T(8,128)} copy(f32[6,8,128]{2,0,1:T(8,128)S(1)} %bitcast.8) | data formatting | bytes 49152 | tf_op jit(solution)/shard_map/slice | solution.py:466
  (1 shorter events, 0.0 us)
Async XLA Ops:
  15.5 1.3 %collective-permute-start = (f32[128,128]{1,0:T(8,128)S(1)}, f32[128,128]{1,0:T(8,128)S(1)}, u32[]{:S(2)}, u32[]{:S(2)}) collective-permute-start(f32[128,128]{1,0:T(8,128)S(1)} %get-tuple-element.16), channel_id=1, source_target_pairs={{0,1},{1,0},{2,3},{3,2},{4,5},{5,4},{6,7},{7,6},{8,9},{9,8},{10,11... | collective-permute-start | bytes 196616 | tf_op jit(solution)/shard_map/ppermute | solution.py:431
  16.9 15.1 %collective-permute-start.1 = (f32[45,16,128]{2,1,0:T(8,128)S(1)}, f32[45,16,128]{2,1,0:T(8,128)S(1)}, u32[]{:S(2)}, u32[]{:S(2)}) collective-permute-start(f32[45,16,128]{2,1,0:T(8,128)S(1)} %get-tuple-element.18), channel_id=1, source_target_pairs={{0,8},{8,16},{16,24},{1,9},{9,17},{17,25},{2,10},{10,18},{18,26},{... | collective-permute-start | bytes 1105928 | tf_op jit(solution)/shard_map/ppermute | solution.py:403
  20.4 11.6 %collective-permute-start.2 = (f32[41,16,128]{2,1,0:T(8,128)S(1)}, f32[41,16,128]{2,1,0:T(8,128)S(1)}, u32[]{:S(2)}, u32[]{:S(2)}) collective-permute-start(f32[41,16,128]{2,1,0:T(8,128)S(1)} %get-tuple-element.19), channel_id=1, source_target_pairs={{8,0},{16,8},{24,16},{9,1},{17,9},{25,17},{10,2},{18,10},{26,18},{... | collective-permute-start | bytes 1007624 | tf_op jit(solution)/shard_map/ppermute | solution.py:403
  32.2 13.9 %collective-permute-start.3 = (f32[488,128]{1,0:T(8,128)S(1)}, f32[488,128]{1,0:T(8,128)S(1)}, u32[]{:S(2)}, u32[]{:S(2)}) collective-permute-start(f32[488,128]{1,0:T(8,128)S(1)} %get-tuple-element.20), channel_id=1, source_target_pairs={{0,2},{2,4},{4,6},{1,3},{3,5},{5,7},{8,10},{10,12},{12,14},{9,11},... | collective-permute-start | bytes 749576 | tf_op jit(solution)/shard_map/ppermute | solution.py:403
  34.7 11.4 %collective-permute-start.4 = (f32[456,128]{1,0:T(8,128)S(1)}, f32[456,128]{1,0:T(8,128)S(1)}, u32[]{:S(2)}, u32[]{:S(2)}) collective-permute-start(f32[456,128]{1,0:T(8,128)S(1)} %get-tuple-element.21), channel_id=1, source_target_pairs={{2,0},{4,2},{6,4},{3,1},{5,3},{7,5},{10,8},{12,10},{14,12},{11,9},... | collective-permute-start | bytes 700424 | tf_op jit(solution)/shard_map/ppermute | solution.py:403

commit v3 on v2

v3 whole, which is shorter than its diff:
```python
import functools

import jax
import jax.numpy as jnp
from jax import lax
from jax.experimental import pallas as pl
from jax.experimental.pallas import tpu as pltpu
from jax.sharding import PartitionSpec as P

STEPS = 4
TIME_STEP = 0.5
PUMP_DECAY = 0.2
UPPER_DECAY = 0.02
WORK_SHARE = 0.05
CLASS_PERMITTIVITY = (1.0, 2.1, 6.0, 12.25)

WIDTHS = (STEPS,) * 3 + (STEPS - 1,) * 4 + (STEPS - 2,) * 4 + (STEPS - 3,) * 9
FIELDS = len(WIDTHS)
GRID = 4
ALL_WIDTHS = WIDTHS + (STEPS,)
VECTORS = (0, 4, 7, 11)
LANE_BASES = tuple(2 * sum(WIDTHS[:i]) for i in range(FIELDS))
LANES = 128
VMEM_LIMIT = 24 * 1024 * 1024
HIGH_LIMIT = 56 * 1024 * 1024


def layer_list(skip_axis):
    layers = []
    for f, width in enumerate(ALL_WIDTHS):
        unused = skip_axis is not None and f - skip_axis in VECTORS
        layers += [(f, d) for d in range(width - 1 if unused else width)]
    return layers


LAYERS_LOW = (layer_list(0), layer_list(1))
LAYERS_HIGH = layer_list(None)


def corner_rows(layers, halo_sign):
    out = []
    for f, d in layers:
        width = ALL_WIDTHS[f]
        for side in (-1, 1):
            reach = width - d if side != halo_sign else width - 1 - d
            for e in range(reach):
                known = LAYERS_HIGH if side < 0 else LAYERS_LOW[0]
                if (f, e) in known:
                    out.append((f, d, side, e))
    return out


def corner_shape(layers, halo_sign, depth):
    return (-(-len(corner_rows(layers, halo_sign)) // 8) * 8, depth)


def inverse_permittivity(classes):
    inverse = jnp.zeros(classes.shape, jnp.float32)
    for number, epsilon in enumerate(CLASS_PERMITTIVITY):
        inverse = jnp.where(classes == number, 1.0 / epsilon, inverse)
    return inverse


def halves(value):
    high = value.astype(jnp.bfloat16)
    low = (value - high.astype(jnp.float32)).astype(jnp.bfloat16)
    return high, low


def write_one_hots(index, row_hot, depth_hot, rows, depth):
    shift = depth.bit_length() - 1
    buckets, slots = index.shape
    for b in range(buckets):
        row = lax.shift_right_logical(index[b : b + 1], shift)
        deep = lax.bitwise_and(index[b : b + 1], depth - 1)
        rows_at = lax.broadcasted_iota(jnp.int32, (rows, slots), 0)
        deep_at = lax.broadcasted_iota(jnp.int32, (depth, slots), 0)
        hot = jnp.where(rows_at == row, 1.0, 0.0).astype(jnp.bfloat16)
        span = slice(b * slots, (b + 1) * slots)
        row_hot[0:rows, span] = hot
        row_hot[rows : 2 * rows, span] = hot
        depth_hot[:, span] = jnp.where(deep_at == deep, 1.0, 0.0).astype(jnp.bfloat16)


def cell_halves(cells):
    parts = []
    for block in cells:
        parts.append(jnp.concatenate(halves(block.T), axis=1))
    return jnp.concatenate(parts, axis=0)


def gather_cells(left, index, row_hot, depth):
    buckets, slots = index.shape
    samples = [[], [], []]
    group = 2 if buckets % 2 == 0 else 1
    for start in range(0, buckets, group):
        span = slice(start * slots, (start + group) * slots)
        picked = jnp.dot(left, row_hot[:, span], preferred_element_type=jnp.float32)
        for b in range(start, start + group):
            deep = lax.bitwise_and(index[b : b + 1], depth - 1)
            hit = lax.broadcasted_iota(jnp.int32, (depth, slots), 0) == deep
            for c in range(3):
                part = picked[c * depth : (c + 1) * depth, (b - start) * slots : (b - start + 1) * slots]
                samples[c].append(jnp.sum(jnp.where(hit, part, 0.0), axis=0, keepdims=True))
    return [jnp.concatenate(rows, axis=0) for rows in samples]


def flat_row(value):
    buckets = value.shape[0]
    return jnp.concatenate([value[b : b + 1] for b in range(buckets)], axis=1)


def scatter_cells(values, row_hot, depth_hot, rows):
    hot = row_hot[0:rows, :]
    hot = jnp.concatenate([hot, hot], axis=1)
    deep = depth_hot[...]
    out = []
    for value in values:
        high, low = halves(flat_row(value))
        spread = jnp.concatenate([deep * high, deep * low], axis=1)
        out.append(
            lax.dot_general(
                hot, spread, (((1,), (1,)), ((), ())), preferred_element_type=jnp.float32
            )
        )
    return out


def emitter_constants(arrived):
    freq, dephase, strength, pumping = [arrived[:, f, :] for f in range(8, 12)]
    damping = 0.5 * TIME_STEP * dephase
    stiffness = freq * TIME_STEP * (freq * TIME_STEP)
    scale = 1.0 + damping
    keep = (2.0 - stiffness) / scale
    back = (1.0 - damping) / scale
    drive = strength * (TIME_STEP * TIME_STEP) / scale
    share = WORK_SHARE / freq
    return keep, back, drive, share, pumping


def bloch_step(sample, current, previous, upper, pumped, constants):
    keep, back, drive, share, pumping = constants
    lower = 1.0 - upper - pumped
    push = drive * (lower - upper)
    advanced = [keep * c - back * p + push * s for c, p, s in zip(current, previous, sample)]
    work = sum(s * (a - p) for s, a, p in zip(sample, advanced, previous)) / (2.0 * TIME_STEP)
    pumped_next = pumped + TIME_STEP * (pumping * lower - PUMP_DECAY * pumped)
    upper_next = upper + TIME_STEP * (
        PUMP_DECAY * pumped - UPPER_DECAY * upper + share * work
    )
    return advanced, current, upper_next, pumped_next


def pack_kernel(index, polar, popul, freq, dephase, strength, pumping, out):
    for i in range(2):
        for c in range(3):
            out[:, 3 * i + c, :] = polar[i, c, 0]
    for i in range(2):
        out[:, 6 + i, :] = popul[i, 0]
    for f, source in enumerate((freq, dephase, strength, pumping)):
        out[:, 8 + f, :] = source[0]
    out[:, 12, :] = index[0].astype(jnp.float32)


def source_of(base, coefs, strip, f):
    if f < GRID:
        return base.at[f]
    return coefs.at[f - GRID] if f < FIELDS else strip


def base_kernel(electric, classes, base, left):
    _, nx, ny, depth = electric.shape
    rows = nx * ny
    for c in range(3):
        base[c] = electric[c].reshape(rows, depth)
    base[3] = inverse_permittivity(classes[...].reshape(rows, depth)) * -(TIME_STEP**2)
    left[...] = cell_halves([base[c] for c in range(3)])


def first_kernel(arrived, base, left, coefs, strip, states, row_hot, depth_hot):
    _, rows, depth = base.shape
    index = arrived[:, 12, :].astype(jnp.int32)
    write_one_hots(index, row_hot, depth_hot, rows, depth)
    sample = gather_cells(left[...], index, row_hot, depth)
    constants = emitter_constants(arrived)
    keep, back, drive, share, pumping = constants
    start = [arrived[:, c, :] for c in range(3)]
    before = [arrived[:, 3 + c, :] for c in range(3)]
    now, _, upper, pumped = bloch_step(
        sample, start, before, arrived[:, 6, :], arrived[:, 7, :], constants
    )
    for c in range(3):
        states[c] = now[c]
        states[3 + c] = start[c]
    states[6] = upper
    states[7] = pumped
    lower = 1.0 - upper - pumped
    push = drive * (lower - upper)
    pumped_after = pumped + TIME_STEP * (pumping * lower - PUMP_DECAY * pumped)
    upper_free = upper + TIME_STEP * (PUMP_DECAY * pumped - UPPER_DECAY * upper)
    free = [keep * n - back * s for n, s in zip(now, start)]
    values = [n - s for n, s in zip(now, start)]
    values += [f - n for f, n in zip(free, now)]
    values.append(push)
    values += [(keep - 1.0) * f - back * n for f, n in zip(free, now)]
    values.append((keep - 1.0) * push)
    values.append(drive * (1.0 - pumped_after - 2.0 * upper_free))
    values += [-drive * share * (f - s) for f, s in zip(free, start)]
    values.append(-drive * share * push)
    values = [value * (1.0 / TIME_STEP**2) for value in values]
    for number, block in enumerate(scatter_cells(values, row_hot, depth_hot, rows)):
        coefs[number] = block
    lane = lax.broadcasted_iota(jnp.int32, (rows, depth), 1)
    packed = jnp.zeros((rows, depth), jnp.float32)
    for f, width in enumerate(WIDTHS):
        at = LANE_BASES[f]
        turned = pltpu.roll(source_of(base, coefs, strip, f)[...], (at + width) % depth, 1)
        packed = jnp.where((lane >= at) & (lane < at + 2 * width), turned, packed)
    strip[...] = packed


def faces_kernel(nx, ny, count_z, base, coefs, from_low, from_high, strip, x_low, x_high, y_low, y_high):
    rows, depth = strip.shape
    lane = lax.broadcasted_iota(jnp.int32, (rows, depth), 1)
    top = jnp.zeros((rows, depth), jnp.bool_)
    for f, width in enumerate(WIDTHS):
        at = LANE_BASES[f]
        top = top | ((lane >= at) & (lane < at + width))
    me = lax.axis_index("gz")
    strip[...] = jnp.where(
        top,
        jnp.where(me > 0, from_low[...], 0.0),
        jnp.where(me < count_z - 1, from_high[...], 0.0),
    )

    def source(f):
        return source_of(base, coefs, strip, f)

    for at, (f, d) in enumerate(LAYERS_LOW[0]):
        x_low[at] = source(f)[d * ny : (d + 1) * ny, :]
    for at, (f, d) in enumerate(LAYERS_HIGH):
        x_high[at] = source(f)[(nx - 1 - d) * ny : (nx - d) * ny, :]
    for at, (f, d) in enumerate(LAYERS_LOW[1]):
        y_low[at] = source(f)[pl.ds(d, nx, stride=ny), :]
    for at, (f, d) in enumerate(LAYERS_HIGH):
        y_high[at] = source(f)[pl.ds(ny - 1 - d, nx, stride=ny), :]


def corners_kernel(halo_low, halo_high, low, high):
    ny = halo_low.shape[1]
    for face, layers, sign in ((low, LAYERS_LOW[1], -1), (high, LAYERS_HIGH, 1)):
        for row, (f, d, side, e) in enumerate(corner_rows(layers, -sign)):
            y = d if sign < 0 else ny - 1 - d
            if side < 0:
                value = halo_low[LAYERS_HIGH.index((f, e)), y : y + 1, :]
            else:
                value = halo_high[LAYERS_LOW[0].index((f, e)), y : y + 1, :]
            face[row : row + 1, :] = value


def place(cells, wide, wide_strip, f):
    if f < 3:
        return cells.at[f]
    return wide.at[f - 3] if f < FIELDS else wide_strip


def assemble_kernel(
    base, coefs, strip, x_low, x_high, y_low, y_high, cells, wide, wide_strip
):
    _, ny, depth = x_low.shape
    nx = y_low.shape[1]
    ex, ey, ez = nx + 2 * STEPS, ny + 2 * STEPS, 2 * depth
    for f in range(FIELDS + 1):
        source = source_of(base, coefs, strip, f)
        target = place(cells, wide, wide_strip, f)
        target[STEPS : STEPS + nx, 0:ny, 0:depth] = source[...].reshape(nx, ny, depth)
        target[:, ny:ey, 0:depth] = jnp.zeros((ex, 2 * STEPS, depth), jnp.float32)
    for at, (f, d) in enumerate(LAYERS_HIGH):
        place(cells, wide, wide_strip, f)[STEPS - 1 - d, 0:ny, 0:depth] = x_low[at]
    for at, (f, d) in enumerate(LAYERS_LOW[0]):
        place(cells, wide, wide_strip, f)[STEPS + nx + d, 0:ny, 0:depth] = x_high[at]
    for halo, layers, sign in ((y_low, LAYERS_HIGH, -1), (y_high, LAYERS_LOW[1], 1)):
        for at, (f, d) in enumerate(layers):
            y = ey - 1 - d if sign < 0 else ny + d
            for x in range(nx):
                place(cells, wide, wide_strip, f)[STEPS + x, y : y + 1, 0:depth] = halo[at, x : x + 1, :]
    for x in range(ex):
        value = wide_strip[x]
        for f, width in enumerate(WIDTHS):
            place(cells, wide, wide_strip, f)[x, :, depth:ez] = pltpu.roll(
                value, (-(LANE_BASES[f] + width)) % depth, 1
            )


def rolls(ey, ez):
    return (
        lambda v: pltpu.roll(v, ey - 1, 0),
        lambda v: pltpu.roll(v, ez - 1, 1),
        lambda v: pltpu.roll(v, 1, 0),
        lambda v: pltpu.roll(v, 1, 1),
    )


def inside_mask(ey, ez):
    row_at = lax.broadcasted_iota(jnp.int32, (ey, ez), 0)
    lane_at = lax.broadcasted_iota(jnp.int32, (ey, ez), 1)
    outside = ((row_at >= ey - STEPS) & (lax.axis_index("gy") == 0)) | (
        (lane_at >= ez - STEPS) & (lax.axis_index("gz") == 0)
    )
    return jnp.where(outside, 0.0, 1.0)


def advance_magnetic(cells, field, inside, step, x):
    _, _, ey, ez = cells.shape
    up_y, up_z, _, _ = rolls(ey, ez)
    e0, e1, e2 = cells[0, x], cells[1, x], cells[2, x]
    f1, f2 = cells[1, x + 1], cells[2, x + 1]
    curl = (
        (up_y(e2) - e2) - (up_z(e1) - e1),
        (up_z(e0) - e0) - (f2 - e2),
        (f1 - e1) - (up_y(e0) - e0),
    )
    mask = inside
    if x < STEPS:
        mask = inside * jnp.where(lax.axis_index("gx") == 0, 0.0, 1.0)
    for c in range(3):
        change = curl[c] * mask
        field[c, x] = field[c, x] + change if step > 1 else change


def backward_curl(field, x):
    _, _, ey, ez = field.shape
    _, _, down_y, down_z = rolls(ey, ez)
    m0, m1, m2 = field[0, x], field[1, x], field[2, x]
    l1, l2 = field[1, x - 1], field[2, x - 1]
    return (
        (m2 - down_y(m2)) - (m1 - down_z(m1)),
        (m0 - down_z(m0)) - (m2 - l2),
        (m1 - l1) - (m0 - down_y(m0)),
    )


def advance_electric(cells, wide, field, step, x):
    curl = backward_curl(field, x)
    old = [cells[c, x] for c in range(3)]
    if step == 2:
        gain = wide[7, x]
        source = [wide[4 + c, x] + gain * old[c] for c in range(3)]
        if STEPS - 2 < x < wide.shape[1] - STEPS + 1:
            ratio = wide[11, x]
            for c in range(3):
                wide[8 + c, x] = wide[8 + c, x] + ratio * old[c]
            square = old[0] * old[0] + old[1] * old[1] + old[2] * old[2]
            wide[12, x] = (
                wide[12, x]
                + (wide[13, x] * old[0] + wide[14, x] * old[1] + wide[15, x] * old[2])
                + wide[16, x] * square
            )
    elif step == 3:
        gain = wide[12, x]
        source = [wide[8 + c, x] + gain * old[c] for c in range(3)]
    else:
        source = [wide[1 + c, x] for c in range(3)]
    scale = wide[0, x]
    for c in range(3):
        cells[c, x] = old[c] + scale * (curl[c] + source[c])


def steps_kernel(
    c_low, c_high, _cells, _wide, wide_strip, row_hot, depth_hot, arrived, states,
    cells, wide, field, result, changes,
):
    _, ex, ey, ez = wide.shape
    nx, ny, depth = ex - 2 * STEPS, ey - 2 * STEPS, ez // 2
    rows = nx * ny
    for corner, layers, sign in ((c_low, LAYERS_HIGH, -1), (c_high, LAYERS_LOW[1], 1)):
        for row, (f, d, side, e) in enumerate(corner_rows(layers, sign)):
            y = ey - 1 - d if sign < 0 else ny + d
            x = STEPS - 1 - e if side < 0 else STEPS + nx + e
            place(cells, wide, wide_strip, f)[x, y : y + 1, 0:depth] = corner[row : row + 1, :]
    for x in (*range(STEPS), *range(STEPS + nx, ex)):
        value = wide_strip[x, ny:ey]
        for f, width in enumerate(WIDTHS):
            place(cells, wide, wide_strip, f)[x, ny:ey, depth:ez] = pltpu.roll(
                value, (-(LANE_BASES[f] + width)) % depth, 1
            )
    inside = inside_mask(ey, ez)
    index = arrived[:, 12, :].astype(jnp.int32)
    constants = emitter_constants(arrived)
    current = [states[c] for c in range(3)]
    previous = [states[3 + c] for c in range(3)]
    upper = states[6]
    pumped = states[7]
    for step in range(1, STEPS + 1):
        if step > 1:
            own = [
                cells[c, STEPS : STEPS + nx, 0:ny, 0:depth].reshape(rows, depth) for c in range(3)
            ]
            sample = gather_cells(cell_halves(own), index, row_hot, depth)
            advanced, previous, upper, pumped = bloch_step(
                sample, current, previous, upper, pumped, constants
            )
            if step == STEPS:
                change = [
                    (a - c) * (1.0 / TIME_STEP**2) for a, c in zip(advanced, current)
                ]
            current = advanced
        if step < STEPS:
            advance_magnetic(cells, field, inside, step, step - 1)
            for x in range(step, ex - step):
                advance_magnetic(cells, field, inside, step, x)
                advance_electric(cells, wide, field, step, x)
    for c in range(3):
        result[:, c, :] = current[c]
        result[:, 3 + c, :] = previous[c]
    result[:, 6, :] = upper
    result[:, 7, :] = pumped
    for c in range(3):
        changes[c] = change[c]


def last_kernel(cells, base, field, changes, row_hot, depth_hot, electric, magnetic):
    _, nx, ny, depth = electric.shape
    rows = nx * ny
    ey, ez = cells.shape[2:]
    sources = scatter_cells([changes[c] for c in range(3)], row_hot, depth_hot, rows)
    inside = inside_mask(ey, ez)
    advance_magnetic(cells, field, inside, STEPS, STEPS - 1)
    for x in range(STEPS, STEPS + nx):
        advance_magnetic(cells, field, inside, STEPS, x)
        curl = backward_curl(field, x)
        span = slice((x - STEPS) * ny, (x - STEPS + 1) * ny)
        scale = base[3, span]
        for c in range(3):
            own = curl[c][0:ny, 0:depth] + sources[c][span]
            electric[c, x - STEPS] = cells[c, x, 0:ny, 0:depth] + scale * own
            magnetic[c, x - STEPS] = field[c, x, 0:ny, 0:depth] * -TIME_STEP


def unpack_kernel(home, polar, popul):
    for i in range(2):
        for c in range(3):
            polar[i, c, 0] = home[:, 3 * i + c, :]
        popul[i, 0] = home[:, 6 + i, :]


def call(kernel, outs, final=(), aliases=None, limit=VMEM_LIMIT):
    shapes = [pltpu.VMEM(s[:-1], s[-1]) if isinstance(s[-1], type) else pltpu.VMEM(s, jnp.float32) for s in outs]
    shapes += [jax.ShapeDtypeStruct(s, jnp.float32) for s in final]
    return pl.pallas_call(
        kernel,
        out_shape=shapes,
        input_output_aliases=aliases or {},
        compiler_params=pltpu.CompilerParams(vmem_limit_bytes=limit),
    )


def near(*values):
    return [pltpu.with_memory_space_constraint(v, pltpu.VMEM) for v in values]


def shifted(value, axis, step):
    count = lax.axis_size(axis)
    pairs = [(i, i + step) for i in range(count) if 0 <= i + step < count]
    return lax.ppermute(value, axis, pairs)


def shards(
    electric, permittivity_class, cell_index, polarization, populations,
    resonance, dephasing, coupling, pump_rate,
):
    _, nx, ny, depth = electric.shape
    rows = nx * ny
    _, buckets, slots = cell_index.shape
    ex, ey, ez = nx + 2 * STEPS, ny + 2 * STEPS, 2 * depth
    hots = [
        (2 * rows, buckets * slots, jnp.bfloat16),
        (depth, buckets * slots, jnp.bfloat16),
    ]
    (packed,) = call(pack_kernel, [(buckets, 13, slots)], limit=HIGH_LIMIT)(
        cell_index, polarization, populations, resonance, dephasing, coupling, pump_rate
    )
    base, left = near(
        *call(
            base_kernel,
            [(GRID, rows, depth), (3 * depth, 2 * rows, jnp.bfloat16)],
            limit=HIGH_LIMIT,
        )(electric, permittivity_class)
    )
    arrived = lax.all_to_all(packed, ("gy", "gz"), split_axis=0, concat_axis=0, tiled=True)
    (arrived,) = near(arrived)
    coefs, strip, states, row_hot, depth_hot = near(
        *call(
            first_kernel,
            [(FIELDS - GRID, rows, depth), (rows, depth), (8, buckets, slots), *hots],
        )(arrived, base, left)
    )
    count_z = lax.axis_size("gz")
    if count_z == 2:
        from_low = from_high = lax.ppermute(strip, "gz", [(0, 1), (1, 0)])
    else:
        from_low = shifted(strip, "gz", 1)
        from_high = shifted(strip, "gz", -1)
    strip, *faces = call(
        functools.partial(faces_kernel, nx, ny, count_z),
        [
            (rows, depth),
            (len(LAYERS_LOW[0]), ny, depth),
            (len(LAYERS_HIGH), ny, depth),
            (len(LAYERS_LOW[1]), nx, depth),
            (len(LAYERS_HIGH), nx, depth),
        ],
    )(base, coefs, *near(from_low, from_high))
    (strip,) = near(strip)
    x_low, x_high = near(shifted(faces[1], "gx", 1), shifted(faces[0], "gx", -1))
    y_low, y_high = near(shifted(faces[3], "gy", 1), shifted(faces[2], "gy", -1))
    low, high = call(
        corners_kernel,
        [corner_shape(LAYERS_LOW[1], 1, depth), corner_shape(LAYERS_HIGH, -1, depth)],
    )(x_low, x_high)
    c_low, c_high = near(shifted(high, "gy", 1), shifted(low, "gy", -1))
    cells, wide, wide_strip = near(
        *call(
            assemble_kernel, [(3, ex, ey, ez), (FIELDS - 3, ex, ey, ez), (ex, ey, depth)]
        )(base, coefs, strip, x_low, x_high, y_low, y_high)
    )
    cells, _, field, result, changes = near(
        *call(
            steps_kernel,
            [
                cells.shape,
                wide.shape,
                (3, ex, ey, ez),
                (buckets, 8, slots),
                (3, buckets, slots),
            ],
            aliases={2: 0, 3: 1},
        )(c_low, c_high, cells, wide, wide_strip, row_hot, depth_hot, arrived, states)
    )
    home = lax.all_to_all(result, ("gy", "gz"), split_axis=0, concat_axis=0, tiled=True)
    electric, magnetic = call(last_kernel, [], [electric.shape, electric.shape])(
        cells, base, field, changes, row_hot, depth_hot
    )
    polar_out, popul_out = call(unpack_kernel, [], [polarization.shape, populations.shape])(
        *near(home)
    )
    return (electric, magnetic, polar_out, popul_out)


def solution(mesh):
    owners = P("gx", ("gy", "gz"), None)
    return jax.shard_map(
        shards,
        mesh=mesh,
        in_specs=(
            P(None, "gx", "gy", "gz"),
            P("gx", "gy", "gz"),
            owners,
            P(None, None, "gx", ("gy", "gz"), None),
            P(None, "gx", ("gy", "gz"), None),
            owners,
            owners,
            owners,
            owners,
        ),
        out_specs=(
            P(None, "gx", "gy", "gz"),
            P(None, "gx", "gy", "gz"),
            P(None, None, "gx", ("gy", "gz"), None),
            P(None, "gx", ("gy", "gz"), None),
        ),
        check_vma=False,
    )
```

time: 61.2 us -> 54.8 us (0.90)
  blocking collectives: 17.2 us -> 0 us
  starting transfers between devices: 8.64 us -> 21.2 us
  waiting for transfers between devices: 21.6 us -> 18.7 us
  Pallas kernels: 11.5 us -> 13.7 us
  local copies, waits for them, and re-layouts: 1.22 us -> 0 us
    all_to_all x2 -> x0, blocking collectives: 17.2 us -> none  [the longest x1 9.99 us: shards(): lax.all_to_all(packed, ('gy', 'gz'), split_axis=0, concat_axis=0, tiled=T...]
    ppermute x4 -> x6, waiting for transfers between devices: 20.3 us -> 9.98 us  [shifted(): return lax.ppermute(value, axis, pairs)]
    all_to_all x0 -> x2, starting transfers between devices: none -> 8.8 us  [the longest x1 5.17 us: shards(): lax.all_to_all(packed, ('gy', 'gz'), split_axis=0, concat_axis=0, tiled=T...]
    all_to_all x0 -> x2, waiting for transfers between devices: none -> 7.47 us  [the longest x1 3.94 us: shards(): lax.all_to_all(packed, ('gy', 'gz'), split_axis=0, concat_axis=0, tiled=T...]
    ppermute x4 -> x6, starting transfers between devices: 8.57 us -> 12.3 us  [shifted(): return lax.ppermute(value, axis, pairs)]
    pallas_call x5 -> x9, Pallas kernels: 11.5 us -> 13.7 us  [the longest x1 4.51 us: shards(): call(steps_kernel, [cells.shape, wide.shape, (3, ex, ey, ez), (buckets, 8...]
    slice x1 -> x0, local copies, waits for them, and re-layouts: 0.61 us -> none  [shards(): polar_out = home[0:6].reshape(polarization.shape)]
  transfers between devices with their start and end apart: 5 -> 9, of which waited for: 3 -> 5; matrix products, arithmetic and copies ran while one was open for 0% -> 0% of each run, Pallas kernels for 0% -> 7%
where the time goes in v3:
time: 54.8 us; the launch traced here: 54.3 us
  starting transfers between devices  21.2 us (39%)
  waiting for transfers between devices  18.7 us (34%)
  Pallas kernels  13.7 us (25%)
  between operations  0.74 us (1%)
    ppermute x6, starting transfers between devices, shifted(): return lax.ppermute(value, axis, pairs)  12.3 us
    ppermute x6, waiting for transfers between devices, shifted(): return lax.ppermute(value, axis, pairs)  9.98 us
    all_to_all x1, starting transfers between devices, shards(): lax.all_to_all(packed, ('gy', 'gz'), split_axis=0, concat_axis=0, tiled=T...  5.17 us
    pallas_call x1, Pallas kernels, shards(): call(steps_kernel, [cells.shape, wide.shape, (3, ex, ey, ez), (buckets, 8...  4.51 us
    all_to_all x1, waiting for transfers between devices, shards(): lax.all_to_all(packed, ('gy', 'gz'), split_axis=0, concat_axis=0, tiled=T...  3.94 us
    all_to_all x1, starting transfers between devices, shards(): lax.all_to_all(result, ('gy', 'gz'), split_axis=0, concat_axis=0, tiled=T...  3.63 us
    all_to_all x1, waiting for transfers between devices, shards(): lax.all_to_all(result, ('gy', 'gz'), split_axis=0, concat_axis=0, tiled=T...  3.53 us
    pallas_call x1, Pallas kernels, shards(): call(first_kernel, [(FIELDS - GRID, rows, depth), (rows, depth), (8, buck...  3.09 us
  transfers between devices with their start and end apart: 9, of which 5 were waited for; matrix products, arithmetic and copies ran while one was open for 0% of the time, Pallas kernels for 7%

profile of v3, /device:TPU:0, one launch (start us, length us, event | category | flops | bytes accessed | tf_op | source)
XLA Modules:
  0.0 54.3 jit_solution(15150519271626116024)
XLA Ops:
  0.6 1.5 %shard_map.121 = f32[8,13,128]{2,1,0:T(8,128)} custom-call(s32[1,8,128]{2,1,0:T(8,128)} %index.1, f32[2,3,1,8,128]{4,3,2,1,0:T(8,128)} %polar.1, f32[2,1,8,128]{3,2,1,0:T(8,128)} %popul.1, f32[1,8,128]{2,1,0:T(8,128)} %freq.1, f32[1,8,128]{2,1,0:T(8,128)} %dephase.1, f32[1,8,128]{2,1,0:T(8,128)} %strength.1, f32[1,8,128]{2,1,0:T(8,128)} %pumping.1), custom_call_target="tpu_custom_call" | custom-call | tf_op jit(solution)/shard_map/pallas_call | solution.py:480
  2.1 5.2 %all-to-all-start = ((f32[8,13,128]{2,1,0:T(8,128)}), f32[8,13,128]{2,1,0:T(8,128)S(1)}, u32[]{:S(2)}, u32[]{:S(2)}) async-start(f32[8,13,128]{2,1,0:T(8,128)} %shard_map.121), calls=%async_computation | async-start | bytes 131072 | tf_op jit(solution)/shard_map/all_to_all | solution.py:490
  7.3 1.1 %shard_map.120 = (f32[4,128,128]{2,1,0:T(8,128)S(1)}, bf16[384,256]{1,0:T(8,128)(2,1)S(1)}) custom-call(f32[3,8,16,128]{3,2,1,0:T(8,128)} %electric.1, s32[8,16,128]{2,1,0:T(8,128)} %classes.1), custom_call_target="tpu_custom_call" | custom-call | tf_op jit(solution)/shard_map/pallas_call | solution.py:484
  8.3 3.9 %all-to-all-done.arrived = f32[8,13,128]{2,1,0:T(8,128)S(1)} async-done(((f32[8,13,128]{2,1,0:T(8,128)}), f32[8,13,128]{2,1,0:T(8,128)S(1)}, u32[]{:S(2)}, u32[]{:S(2)}) %all-to-all-start) | async-done | bytes 53280 | tf_op jit(solution)/shard_map/all_to_all | solution.py:490
  12.3 3.1 %shard_map.122 = (f32[16,128,128]{2,1,0:T(8,128)S(1)}, f32[128,128]{1,0:T(8,128)S(1)}, f32[8,8,128]{2,1,0:T(8,128)S(1)}, bf16[256,1024]{1,0:T(8,128)(2,1)S(1)}, bf16[128,1024]{1,0:T(8,128)(2,1)S(1)}) custom-call(f32[8,13,128]{2,1,0:T(8,128)S(1)} %all-to-all-done.arrived, f32[4,128,128]{2,1,0:T(8,128)S(1)} %get-tuple-element.29.base, ...), custom_call_target="tpu_custom_call" | custom-call | tf_op jit(solution)/shard_map/pallas_call | solution.py:493
  15.4 0.1 collective-permute-start
  15.5 1.2 %collective-permute-done.from_low.from_high = f32[128,128]{1,0:T(8,128)S(1)} collective-permute-done((f32[128,128]{1,0:T(8,128)S(1)}, f32[128,128]{1,0:T(8,128)S(1)}, u32[]{:S(2)}, u32[]{:S(2)}) %collective-permute-start) | collective-permute-done | bytes 65568 | tf_op jit(solution)/shard_map/ppermute | solution.py:500
  16.7 0.2 shard_map.123
  16.9 3.5 %collective-permute-start.1 = (f32[45,16,128]{2,1,0:T(8,128)S(1)}, f32[45,16,128]{2,1,0:T(8,128)S(1)}, u32[]{:S(2)}, u32[]{:S(2)}) collective-permute-start(f32[45,16,128]{2,1,0:T(8,128)S(1)} %get-tuple-element.33), channel_id=1, source_target_pairs={{0,8},{8,16},{16,24},{1,9},{9,17},{17,25},{2,10},{10,18},{18,26},{... | collective-permute-start | bytes 1105928 | tf_op jit(solution)/shard_map/ppermute | solution.py:465
  20.4 1.3 %collective-permute-start.2 = (f32[41,16,128]{2,1,0:T(8,128)S(1)}, f32[41,16,128]{2,1,0:T(8,128)S(1)}, u32[]{:S(2)}, u32[]{:S(2)}) collective-permute-start(f32[41,16,128]{2,1,0:T(8,128)S(1)} %get-tuple-element.34), channel_id=1, source_target_pairs={{8,0},{16,8},{24,16},{9,1},{17,9},{25,17},{10,2},{18,10},{26,18},{... | collective-permute-start | bytes 1007624 | tf_op jit(solution)/shard_map/ppermute | solution.py:465
  21.7 2.5 %collective-permute-start.5 = (f32[45,8,128]{2,1,0:T(8,128)S(1)}, f32[45,8,128]{2,1,0:T(8,128)S(1)}, u32[]{:S(2)}, u32[]{:S(2)}) collective-permute-start(f32[45,8,128]{2,1,0:T(8,128)S(1)} %get-tuple-element.38), channel_id=1, source_target_pairs={{0,2},{2,4},{4,6},{1,3},{3,5},{5,7},{8,10},{10,12},{12,14},{9,11},... | collective-permute-start | bytes 552968 | tf_op jit(solution)/shard_map/ppermute | solution.py:465
  24.2 1.3 %collective-permute-start.6 = (f32[41,8,128]{2,1,0:T(8,128)S(1)}, f32[41,8,128]{2,1,0:T(8,128)S(1)}, u32[]{:S(2)}, u32[]{:S(2)}) collective-permute-start(f32[41,8,128]{2,1,0:T(8,128)S(1)} %get-tuple-element.39), channel_id=1, source_target_pairs={{2,0},{4,2},{6,4},{3,1},{5,3},{7,5},{10,8},{12,10},{14,12},{11,9},... | collective-permute-start | bytes 503816 | tf_op jit(solution)/shard_map/ppermute | solution.py:465
  25.5 6.5 %collective-permute-done.2.halo_high.x_high = f32[41,16,128]{2,1,0:T(8,128)S(1)} collective-permute-done((f32[41,16,128]{2,1,0:T(8,128)S(1)}, f32[41,16,128]{2,1,0:T(8,128)S(1)}, u32[]{:S(2)}, u32[]{:S(2)}) %collective-permute-start.2) | collective-permute-done | bytes 335904 | tf_op jit(solution)/shard_map/ppermute | solution.py:465
  32.0 0.0 collective-permute-done.1.halo_low.x_low
  32.0 0.1 shard_map.124
  32.0 2.5 %collective-permute-start.3 = (f32[128,128]{1,0:T(8,128)S(1)}, f32[128,128]{1,0:T(8,128)S(1)}, u32[]{:S(2)}, u32[]{:S(2)}) collective-permute-start(f32[128,128]{1,0:T(8,128)S(1)} %get-tuple-element.35), channel_id=1, source_target_pairs={{0,2},{2,4},{4,6},{1,3},{3,5},{5,7},{8,10},{10,12},{12,14},{9,11},... | collective-permute-start | bytes 196616 | tf_op jit(solution)/shard_map/ppermute | solution.py:465
  34.5 1.3 %collective-permute-start.4 = (f32[128,128]{1,0:T(8,128)S(1)}, f32[128,128]{1,0:T(8,128)S(1)}, u32[]{:S(2)}, u32[]{:S(2)}) collective-permute-start(f32[128,128]{1,0:T(8,128)S(1)} %get-tuple-element.36), channel_id=1, source_target_pairs={{2,0},{4,2},{6,4},{3,1},{5,3},{7,5},{10,8},{12,10},{14,12},{11,9},... | collective-permute-start | bytes 196616 | tf_op jit(solution)/shard_map/ppermute | solution.py:465
  35.8 0.0 collective-permute-done.6.y_high
  35.8 0.0 collective-permute-done.5.y_low
  35.8 1.3 %shard_map.125 = (f32[3,16,24,256]{3,2,1,0:T(8,128)S(1)}, f32[17,16,24,256]{3,2,1,0:T(8,128)S(1)}, f32[16,24,128]{2,1,0:T(8,128)S(1)}) custom-call(f32[4,128,128]{2,1,0:T(8,128)S(1)} %get-tuple-element.29.base, f32[16,128,128]{2,1,0:T(8,128)S(1)} %get-tuple-element.31.coefs, f32[128,128]{1,0:T(8,128)S(1)} %get-tuple-element.37.strip, ...), custom_call_target="tpu_custom_call" | custom-call | tf_op jit(solution)/shard_map/pallas_call | solution.py:523
  37.2 0.0 collective-permute-done.3.c_low
  37.2 3.5 %collective-permute-done.4.c_high = f32[128,128]{1,0:T(8,128)S(1)} collective-permute-done((f32[128,128]{1,0:T(8,128)S(1)}, f32[128,128]{1,0:T(8,128)S(1)}, u32[]{:S(2)}, u32[]{:S(2)}) %collective-permute-start.4) | collective-permute-done | bytes 65568 | tf_op jit(solution)/shard_map/ppermute | solution.py:465
  40.7 4.5 %shard_map.126 = (f32[3,16,24,256]{3,2,1,0:T(8,128)S(1)}, f32[17,16,24,256]{3,2,1,0:T(8,128)S(1)}, f32[3,16,24,256]{3,2,1,0:T(8,128)S(1)}, f32[8,8,128]{2,1,0:T(8,128)}, f32[3,8,128]{2,1,0:T(8,128)S(1)}) custom-call(f32[128,128]{1,0:T(8,128)S(1)} %collective-permute-done.3.c_low, ...), custom_call_target="tpu_custom_call", output_to_operand_aliasing={{0}: (2, {}), {1}: (3, {})} | custom-call | tf_op jit(solution)/shard_map/pallas_call | solution.py:528
  45.2 3.6 %all-to-all-start.1 = ((f32[8,8,128]{2,1,0:T(8,128)}), f32[8,8,128]{2,1,0:T(8,128)S(1)}, u32[]{:S(2)}, u32[]{:S(2)}) async-start(f32[8,8,128]{2,1,0:T(8,128)} %get-tuple-element.51), calls=%async_computation.1 | async-start | bytes 65536 | tf_op jit(solution)/shard_map/all_to_all | solution.py:540
  48.8 1.3 %shard_map.127 = (f32[3,8,16,128]{3,2,1,0:T(8,128)}, f32[3,8,16,128]{3,2,1,0:T(8,128)}) custom-call(f32[3,16,24,256]{3,2,1,0:T(8,128)S(1)} %get-tuple-element.46.cells, f32[4,128,128]{2,1,0:T(8,128)S(1)} %get-tuple-element.29.base, f32[3,16,24,256]{3,2,1,0:T(8,128)S(1)} %get-tuple-element.47.field, f32[3,8,128]{2,1,0:T(8,128)S(1)} %get-tuple-element.48.changes, ...), custom_call_target="tpu_custom_call" | custom-call | tf_op jit(solution)/shard_map/pallas_call | solution.py:541
  50.1 3.5 %all-to-all-done.1.home = f32[8,8,128]{2,1,0:T(8,128)S(1)} async-done(((f32[8,8,128]{2,1,0:T(8,128)}), f32[8,8,128]{2,1,0:T(8,128)S(1)}, u32[]{:S(2)}, u32[]{:S(2)}) %all-to-all-start.1) | async-done | bytes 32800 | tf_op jit(solution)/shard_map/all_to_all | solution.py:540
  53.7 0.6 %shard_map.128 = (f32[2,3,1,8,128]{4,3,2,1,0:T(8,128)}, f32[2,1,8,128]{3,2,1,0:T(8,128)}) custom-call(f32[8,8,128]{2,1,0:T(8,128)S(1)} %all-to-all-done.1.home), custom_call_target="tpu_custom_call" | custom-call | tf_op jit(solution)/shard_map/pallas_call | solution.py:544
Async XLA Ops:
  2.1 10.2 %all-to-all-start = ((f32[8,13,128]{2,1,0:T(8,128)}), f32[8,13,128]{2,1,0:T(8,128)S(1)}, u32[]{:S(2)}, u32[]{:S(2)}) async-start(f32[8,13,128]{2,1,0:T(8,128)} %shard_map.121), calls=%async_computation | async-start | bytes 131072 | tf_op jit(solution)/shard_map/all_to_all | solution.py:490
  15.4 1.3 %collective-permute-start = (f32[128,128]{1,0:T(8,128)S(1)}, f32[128,128]{1,0:T(8,128)S(1)}, u32[]{:S(2)}, u32[]{:S(2)}) collective-permute-start(f32[128,128]{1,0:T(8,128)S(1)} %get-tuple-element.32), channel_id=1, source_target_pairs={{0,1},{1,0},{2,3},{3,2},{4,5},{5,4},{6,7},{7,6},{8,9},{9,8},{10,11... | collective-permute-start | bytes 196616 | tf_op jit(solution)/shard_map/ppermute | solution.py:500
  16.9 15.1 %collective-permute-start.1 = (f32[45,16,128]{2,1,0:T(8,128)S(1)}, f32[45,16,128]{2,1,0:T(8,128)S(1)}, u32[]{:S(2)}, u32[]{:S(2)}) collective-permute-start(f32[45,16,128]{2,1,0:T(8,128)S(1)} %get-tuple-element.33), channel_id=1, source_target_pairs={{0,8},{8,16},{16,24},{1,9},{9,17},{17,25},{2,10},{10,18},{18,26},{... | collective-permute-start | bytes 1105928 | tf_op jit(solution)/shard_map/ppermute | solution.py:465
  20.4 11.6 %collective-permute-start.2 = (f32[41,16,128]{2,1,0:T(8,128)S(1)}, f32[41,16,128]{2,1,0:T(8,128)S(1)}, u32[]{:S(2)}, u32[]{:S(2)}) collective-permute-start(f32[41,16,128]{2,1,0:T(8,128)S(1)} %get-tuple-element.34), channel_id=1, source_target_pairs={{8,0},{16,8},{24,16},{9,1},{17,9},{25,17},{10,2},{18,10},{26,18},{... | collective-permute-start | bytes 1007624 | tf_op jit(solution)/shard_map/ppermute | solution.py:465
  21.7 14.1 %collective-permute-start.5 = (f32[45,8,128]{2,1,0:T(8,128)S(1)}, f32[45,8,128]{2,1,0:T(8,128)S(1)}, u32[]{:S(2)}, u32[]{:S(2)}) collective-permute-start(f32[45,8,128]{2,1,0:T(8,128)S(1)} %get-tuple-element.38), channel_id=1, source_target_pairs={{0,2},{2,4},{4,6},{1,3},{3,5},{5,7},{8,10},{10,12},{12,14},{9,11},... | collective-permute-start | bytes 552968 | tf_op jit(solution)/shard_map/ppermute | solution.py:465
  24.2 11.7 %collective-permute-start.6 = (f32[41,8,128]{2,1,0:T(8,128)S(1)}, f32[41,8,128]{2,1,0:T(8,128)S(1)}, u32[]{:S(2)}, u32[]{:S(2)}) collective-permute-start(f32[41,8,128]{2,1,0:T(8,128)S(1)} %get-tuple-element.39), channel_id=1, source_target_pairs={{2,0},{4,2},{6,4},{3,1},{5,3},{7,5},{10,8},{12,10},{14,12},{11,9},... | collective-permute-start | bytes 503816 | tf_op jit(solution)/shard_map/ppermute | solution.py:465
  32.0 5.1 %collective-permute-start.3 = (f32[128,128]{1,0:T(8,128)S(1)}, f32[128,128]{1,0:T(8,128)S(1)}, u32[]{:S(2)}, u32[]{:S(2)}) collective-permute-start(f32[128,128]{1,0:T(8,128)S(1)} %get-tuple-element.35), channel_id=1, source_target_pairs={{0,2},{2,4},{4,6},{1,3},{3,5},{5,7},{8,10},{10,12},{12,14},{9,11},... | collective-permute-start | bytes 196616 | tf_op jit(solution)/shard_map/ppermute | solution.py:465
  34.5 6.2 %collective-permute-start.4 = (f32[128,128]{1,0:T(8,128)S(1)}, f32[128,128]{1,0:T(8,128)S(1)}, u32[]{:S(2)}, u32[]{:S(2)}) collective-permute-start(f32[128,128]{1,0:T(8,128)S(1)} %get-tuple-element.36), channel_id=1, source_target_pairs={{2,0},{4,2},{6,4},{3,1},{5,3},{7,5},{10,8},{12,10},{14,12},{11,9},... | collective-permute-start | bytes 196616 | tf_op jit(solution)/shard_map/ppermute | solution.py:465
  45.2 8.5 %all-to-all-start.1 = ((f32[8,8,128]{2,1,0:T(8,128)}), f32[8,8,128]{2,1,0:T(8,128)S(1)}, u32[]{:S(2)}, u32[]{:S(2)}) async-start(f32[8,8,128]{2,1,0:T(8,128)} %get-tuple-element.51), calls=%async_computation.1 | async-start | bytes 65536 | tf_op jit(solution)/shard_map/all_to_all | solution.py:540

commit v4 on v3

--- a/solution.py
+++ b/solution.py
@@ -20,7 +20,8 @@
 ALL_WIDTHS = WIDTHS + (STEPS,)
 VECTORS = (0, 4, 7, 11)
 LANE_BASES = tuple(2 * sum(WIDTHS[:i]) for i in range(FIELDS))
-LANES = 128
+FOLDS = 2
+LONG = pl.CostEstimate(flops=20_000_000_000, bytes_accessed=100_000_000, transcendentals=0)
 VMEM_LIMIT = 24 * 1024 * 1024
 HIGH_LIMIT = 56 * 1024 * 1024
 
@@ -39,14 +40,17 @@
 
 def corner_rows(layers, halo_sign):
     out = []
+    furthest = 0 if halo_sign < 0 else 1
     for f, d in layers:
         width = ALL_WIDTHS[f]
         for side in (-1, 1):
-            reach = width - d if side != halo_sign else width - 1 - d
-            for e in range(reach):
-                known = LAYERS_HIGH if side < 0 else LAYERS_LOW[0]
-                if (f, e) in known:
-                    out.append((f, d, side, e))
+            reach = width - d
+            if side == halo_sign or any(
+                f in (v, v + 1, v + 2) and f != v + furthest for v in VECTORS
+            ):
+                reach -= 1
+            known = LAYERS_HIGH if side < 0 else LAYERS_LOW[1]
+            out += [(f, d, side, e) for e in range(reach) if (f, e) in known]
     return out
 
 
@@ -68,39 +72,48 @@
 
 
 def write_one_hots(index, row_hot, depth_hot, rows, depth):
+    fold = depth // FOLDS
     shift = depth.bit_length() - 1
     buckets, slots = index.shape
+    live = index < rows * depth
+    part = lax.shift_right_logical(lax.bitwise_and(index, depth - 1), fold.bit_length() - 1)
+    row = lax.shift_right_logical(index, shift) + part * rows
+    row = jnp.where(live, row, -1)
+    deep = lax.bitwise_and(index, fold - 1)
+    rows_at = lax.broadcasted_iota(jnp.int32, (FOLDS * rows, slots), 0)
+    deep_at = lax.broadcasted_iota(jnp.int32, (fold, slots), 0)
     for b in range(buckets):
-        row = lax.shift_right_logical(index[b : b + 1], shift)
-        deep = lax.bitwise_and(index[b : b + 1], depth - 1)
-        rows_at = lax.broadcasted_iota(jnp.int32, (rows, slots), 0)
-        deep_at = lax.broadcasted_iota(jnp.int32, (depth, slots), 0)
-        hot = jnp.where(rows_at == row, 1.0, 0.0).astype(jnp.bfloat16)
         span = slice(b * slots, (b + 1) * slots)
-        row_hot[0:rows, span] = hot
-        row_hot[rows : 2 * rows, span] = hot
-        depth_hot[:, span] = jnp.where(deep_at == deep, 1.0, 0.0).astype(jnp.bfloat16)
+        row_hot[:, span] = jnp.where(rows_at == row[b : b + 1], 1.0, 0.0).astype(jnp.bfloat16)
+        depth_hot[:, span] = jnp.where(deep_at == deep[b : b + 1], 1.0, 0.0).astype(jnp.bfloat16)
 
 
 def cell_halves(cells):
     parts = []
     for block in cells:
-        parts.append(jnp.concatenate(halves(block.T), axis=1))
+        turned = block.T
+        fold = turned.shape[0] // FOLDS
+        turned = [turned[i * fold : (i + 1) * fold] for i in range(FOLDS)]
+        parts += halves(jnp.concatenate(turned, axis=1))
     return jnp.concatenate(parts, axis=0)
 
 
 def gather_cells(left, index, row_hot, depth):
     buckets, slots = index.shape
+    fold = depth // FOLDS
+    size = 2 * fold
     samples = [[], [], []]
     group = 2 if buckets % 2 == 0 else 1
+    place_at = lax.broadcasted_iota(jnp.int32, (size, slots), 0)
+    place_at = lax.bitwise_and(place_at, fold - 1)
     for start in range(0, buckets, group):
         span = slice(start * slots, (start + group) * slots)
         picked = jnp.dot(left, row_hot[:, span], preferred_element_type=jnp.float32)
         for b in range(start, start + group):
-            deep = lax.bitwise_and(index[b : b + 1], depth - 1)
-            hit = lax.broadcasted_iota(jnp.int32, (depth, slots), 0) == deep
+            hit = place_at == lax.bitwise_and(index[b : b + 1], fold - 1)
+            lanes = slice((b - start) * slots, (b - start + 1) * slots)
             for c in range(3):
-                part = picked[c * depth : (c + 1) * depth, (b - start) * slots : (b - start + 1) * slots]
+                part = picked[c * size : (c + 1) * size, lanes]
                 samples[c].append(jnp.sum(jnp.where(hit, part, 0.0), axis=0, keepdims=True))
     return [jnp.concatenate(rows, axis=0) for rows in samples]
 
@@ -110,19 +123,23 @@
     return jnp.concatenate([value[b : b + 1] for b in range(buckets)], axis=1)
 
 
-def scatter_cells(values, row_hot, depth_hot, rows):
-    hot = row_hot[0:rows, :]
-    hot = jnp.concatenate([hot, hot], axis=1)
+def scatter_cells(values, row_hot, depth_hot, rows, group=4):
+    hot = row_hot[...]
     deep = depth_hot[...]
+    fold = deep.shape[0]
     out = []
-    for value in values:
-        high, low = halves(flat_row(value))
-        spread = jnp.concatenate([deep * high, deep * low], axis=1)
-        out.append(
-            lax.dot_general(
-                hot, spread, (((1,), (1,)), ((), ())), preferred_element_type=jnp.float32
+    for start in range(0, len(values), group):
+        some = [halves(flat_row(value)) for value in values[start : start + group]]
+        total = 0.0
+        for part in range(2):
+            spread = jnp.concatenate([deep * pair[part] for pair in some], axis=0)
+            total = total + lax.dot_general(
+                spread, hot, (((1,), (1,)), ((), ())), preferred_element_type=jnp.float32
             )
-        )
+        for i in range(len(some)):
+            block = total[i * fold : (i + 1) * fold]
+            block = [block[:, j * rows : (j + 1) * rows] for j in range(FOLDS)]
+            out.append(jnp.concatenate(block, axis=0).T)
     return out
 
 
@@ -247,14 +264,14 @@
 
 
 def corners_kernel(halo_low, halo_high, low, high):
-    ny = halo_low.shape[1]
-    for face, layers, sign in ((low, LAYERS_LOW[1], -1), (high, LAYERS_HIGH, 1)):
+    nx = halo_low.shape[1]
+    for face, layers, sign in ((low, LAYERS_LOW[0], -1), (high, LAYERS_HIGH, 1)):
         for row, (f, d, side, e) in enumerate(corner_rows(layers, -sign)):
-            y = d if sign < 0 else ny - 1 - d
+            x = d if sign < 0 else nx - 1 - d
             if side < 0:
-                value = halo_low[LAYERS_HIGH.index((f, e)), y : y + 1, :]
+                value = halo_low[LAYERS_HIGH.index((f, e)), x : x + 1, :]
             else:
-                value = halo_high[LAYERS_LOW[0].index((f, e)), y : y + 1, :]
+                value = halo_high[LAYERS_LOW[1].index((f, e)), x : x + 1, :]
             face[row : row + 1, :] = value
 
 
@@ -264,32 +281,61 @@
     return wide.at[f - 3] if f < FIELDS else wide_strip
 
 
+def spread_strip(cells, wide, wide_strip, x, y, count, fields):
+    depth = wide_strip.shape[2]
+    value = wide_strip[x, y : y + count]
+    for f in fields:
+        place(cells, wide, wide_strip, f)[x, y : y + count, depth : 2 * depth] = pltpu.roll(
+            value, (-(LANE_BASES[f] + WIDTHS[f])) % depth, 1
+        )
+
+
 def assemble_kernel(
-    base, coefs, strip, x_low, x_high, y_low, y_high, cells, wide, wide_strip
+    base, coefs, strip, y_low, y_high, cells, wide, wide_strip, field, snaps
 ):
-    _, ny, depth = x_low.shape
-    nx = y_low.shape[1]
-    ex, ey, ez = nx + 2 * STEPS, ny + 2 * STEPS, 2 * depth
+    _, nx, depth = y_low.shape
+    _, ex, ey, ez = cells.shape
+    ny = ey - 2 * STEPS
     for f in range(FIELDS + 1):
         source = source_of(base, coefs, strip, f)
         target = place(cells, wide, wide_strip, f)
         target[STEPS : STEPS + nx, 0:ny, 0:depth] = source[...].reshape(nx, ny, depth)
-        target[:, ny:ey, 0:depth] = jnp.zeros((ex, 2 * STEPS, depth), jnp.float32)
-    for at, (f, d) in enumerate(LAYERS_HIGH):
-        place(cells, wide, wide_strip, f)[STEPS - 1 - d, 0:ny, 0:depth] = x_low[at]
-    for at, (f, d) in enumerate(LAYERS_LOW[0]):
-        place(cells, wide, wide_strip, f)[STEPS + nx + d, 0:ny, 0:depth] = x_high[at]
+        target[STEPS : STEPS + nx, ny:ey, 0:depth] = jnp.zeros((nx, 2 * STEPS, depth), jnp.float32)
     for halo, layers, sign in ((y_low, LAYERS_HIGH, -1), (y_high, LAYERS_LOW[1], 1)):
         for at, (f, d) in enumerate(layers):
             y = ey - 1 - d if sign < 0 else ny + d
             for x in range(nx):
                 place(cells, wide, wide_strip, f)[STEPS + x, y : y + 1, 0:depth] = halo[at, x : x + 1, :]
-    for x in range(ex):
-        value = wide_strip[x]
-        for f, width in enumerate(WIDTHS):
-            place(cells, wide, wide_strip, f)[x, :, depth:ez] = pltpu.roll(
-                value, (-(LANE_BASES[f] + width)) % depth, 1
-            )
+    for x in range(STEPS, STEPS + nx):
+        spread_strip(cells, wide, wide_strip, x, 0, ey, range(FIELDS))
+    inside = inside_mask(ey, ez)
+    for step in range(1, STEPS):
+        for x in range(STEPS + step - 1, STEPS + nx - step):
+            advance_magnetic(cells, field, inside, step, x)
+            if x >= STEPS + step:
+                advance_electric(cells, wide, field, snaps, step, x)
+
+
+def side_slabs(nx):
+    for d in range(STEPS):
+        fields = [f for f in range(FIELDS) if WIDTHS[f] > d]
+        yield STEPS - 1 - d, fields
+        yield STEPS + nx + d, fields
+
+
+def sides_kernel(x_low, x_high, _cells, _wide, _strip, cells, wide, wide_strip):
+    _, ny, depth = x_low.shape
+    _, ex, ey, _ = cells.shape
+    nx = ex - 2 * STEPS
+    for at, (f, d) in enumerate(LAYERS_HIGH):
+        place(cells, wide, wide_strip, f)[STEPS - 1 - d, 0:ny, 0:depth] = x_low[at]
+    for at, (f, d) in enumerate(LAYERS_LOW[0]):
+        place(cells, wide, wide_strip, f)[STEPS + nx + d, 0:ny, 0:depth] = x_high[at]
+    for x, fields in side_slabs(nx):
+        for f in (*fields, FIELDS):
+            target = place(cells, wide, wide_strip, f)
+            target[x, ny:ey, :] = jnp.zeros((2 * STEPS, target.shape[2]), jnp.float32)
+        spread_strip(cells, wide, wide_strip, x, 0, ny, fields)
 
 
 def rolls(ey, ez):
@@ -340,7 +386,7 @@
     )
 
 
-def advance_electric(cells, wide, field, step, x):
+def advance_electric(cells, wide, field, snaps, step, x):
     curl = backward_curl(field, x)
     old = [cells[c, x] for c in range(3)]
     if step == 2:
@@ -362,28 +408,31 @@
     else:
         source = [wide[1 + c, x] for c in range(3)]
     scale = wide[0, x]
+    _, rows, depth = snaps.shape
+    ny = cells.shape[2] - 2 * STEPS
+    at = (x - STEPS) * ny
     for c in range(3):
-        cells[c, x] = old[c] + scale * (curl[c] + source[c])
+        new = old[c] + scale * (curl[c] + source[c])
+        cells[c, x] = new
+        if 0 <= at < rows:
+            snaps[(step - 1) * 3 + c, at : at + ny, :] = new[0:ny, 0:depth]
 
 
 def steps_kernel(
-    c_low, c_high, _cells, _wide, wide_strip, row_hot, depth_hot, arrived, states,
-    cells, wide, field, result, changes,
+    c_low, c_high, _cells, _wide, _field, _snaps, wide_strip, row_hot, depth_hot,
+    arrived, states, cells, wide, field, snaps, result, changes,
 ):
     _, ex, ey, ez = wide.shape
     nx, ny, depth = ex - 2 * STEPS, ey - 2 * STEPS, ez // 2
     rows = nx * ny
-    for corner, layers, sign in ((c_low, LAYERS_HIGH, -1), (c_high, LAYERS_LOW[1], 1)):
+    for corner, layers, sign in ((c_low, LAYERS_HIGH, -1), (c_high, LAYERS_LOW[0], 1)):
         for row, (f, d, side, e) in enumerate(corner_rows(layers, sign)):
-            y = ey - 1 - d if sign < 0 else ny + d
-            x = STEPS - 1 - e if side < 0 else STEPS + nx + e
+            x = STEPS - 1 - d if sign < 0 else STEPS + nx + d
+            y = ey - 1 - e if side < 0 else ny + e
             place(cells, wide, wide_strip, f)[x, y : y + 1, 0:depth] = corner[row : row + 1, :]
-    for x in (*range(STEPS), *range(STEPS + nx, ex)):
-        value = wide_strip[x, ny:ey]
-        for f, width in enumerate(WIDTHS):
-            place(cells, wide, wide_strip, f)[x, ny:ey, depth:ez] = pltpu.roll(
-                value, (-(LANE_BASES[f] + width)) % depth, 1
-            )
+    for x, fields in side_slabs(nx):
+        fields = [f for f in fields if WIDTHS[f] > 1]
+        spread_strip(cells, wide, wide_strip, x, ny, 2 * STEPS, fields)
     inside = inside_mask(ey, ez)
     index = arrived[:, 12, :].astype(jnp.int32)
     constants = emitter_constants(arrived)
@@ -393,9 +442,7 @@
     pumped = states[7]
     for step in range(1, STEPS + 1):
         if step > 1:
-            own = [
-                cells[c, STEPS : STEPS + nx, 0:ny, 0:depth].reshape(rows, depth) for c in range(3)
-            ]
+            own = [snaps[(step - 2) * 3 + c] for c in range(3)]
             sample = gather_cells(cell_halves(own), index, row_hot, depth)
             advanced, previous, upper, pumped = bloch_step(
                 sample, current, previous, upper, pumped, constants
@@ -406,10 +453,12 @@
                 ]
             current = advanced
         if step < STEPS:
-            advance_magnetic(cells, field, inside, step, step - 1)
-            for x in range(step, ex - step):
-                advance_magnetic(cells, field, inside, step, x)
-                advance_electric(cells, wide, field, step, x)
+            done = range(STEPS + step, STEPS + nx - step)
+            for x in range(step - 1, ex - step):
+                if x not in done and x + 1 not in done:
+                    advance_magnetic(cells, field, inside, step, x)
+                if x not in done and x >= step:
+                    advance_electric(cells, wide, field, snaps, step, x)
     for c in range(3):
         result[:, c, :] = current[c]
         result[:, 3 + c, :] = previous[c]
@@ -444,13 +493,14 @@
         popul[i, 0] = home[:, 6 + i, :]
 
 
-def call(kernel, outs, final=(), aliases=None, limit=VMEM_LIMIT):
+def call(kernel, outs, final=(), aliases=None, limit=VMEM_LIMIT, cost=None):
     shapes = [pltpu.VMEM(s[:-1], s[-1]) if isinstance(s[-1], type) else pltpu.VMEM(s, jnp.float32) for s in outs]
     shapes += [jax.ShapeDtypeStruct(s, jnp.float32) for s in final]
     return pl.pallas_call(
         kernel,
         out_shape=shapes,
         input_output_aliases=aliases or {},
+        cost_estimate=cost,
         compiler_params=pltpu.CompilerParams(vmem_limit_bytes=limit),
     )
 
@@ -474,8 +524,8 @@
     _, buckets, slots = cell_index.shape
     ex, ey, ez = nx + 2 * STEPS, ny + 2 * STEPS, 2 * depth
     hots = [
-        (2 * rows, buckets * slots, jnp.bfloat16),
-        (depth, buckets * slots, jnp.bfloat16),
+        (FOLDS * rows, buckets * slots, jnp.bfloat16),
+        (depth // FOLDS, buckets * slots, jnp.bfloat16),
     ]
     (packed,) = call(pack_kernel, [(buckets, 13, slots)], limit=HIGH_LIMIT)(
         cell_index, polarization, populations, resonance, dephasing, coupling, pump_rate
@@ -483,7 +533,7 @@
     base, left = near(
         *call(
             base_kernel,
-            [(GRID, rows, depth), (3 * depth, 2 * rows, jnp.bfloat16)],
+            [(GRID, rows, depth), (6 * depth // FOLDS, FOLDS * rows, jnp.bfloat16)],
             limit=HIGH_LIMIT,
         )(electric, permittivity_class)
     )
@@ -516,26 +566,43 @@
     y_low, y_high = near(shifted(faces[3], "gy", 1), shifted(faces[2], "gy", -1))
     low, high = call(
         corners_kernel,
-        [corner_shape(LAYERS_LOW[1], 1, depth), corner_shape(LAYERS_HIGH, -1, depth)],
-    )(x_low, x_high)
-    c_low, c_high = near(shifted(high, "gy", 1), shifted(low, "gy", -1))
+        [corner_shape(LAYERS_LOW[0], 1, depth), corner_shape(LAYERS_HIGH, -1, depth)],
+        cost=LONG,
+    )(y_low, y_high)
+    c_low, c_high = near(shifted(high, "gx", 1), shifted(low, "gx", -1))
+    state = near(
+        *call(
+            assemble_kernel,
+            [
+                (3, ex, ey, ez),
+                (FIELDS - 3, ex, ey, ez),
+                (ex, ey, depth),
+                (3, ex, ey, ez),
+                (3 * (STEPS - 1), rows, depth),
+            ],
+        )(base, coefs, strip, y_low, y_high)
+    )
+    cells, wide, wide_strip, field, snaps = state
     cells, wide, wide_strip = near(
         *call(
-            assemble_kernel, [(3, ex, ey, ez), (FIELDS - 3, ex, ey, ez), (ex, ey, depth)]
-        )(base, coefs, strip, x_low, x_high, y_low, y_high)
-    )
-    cells, _, field, result, changes = near(
+            sides_kernel,
+            [cells.shape, wide.shape, wide_strip.shape],
+            aliases={2: 0, 3: 1, 4: 2},
+        )(x_low, x_high, cells, wide, wide_strip)
+    )
+    cells, _, field, _, result, changes = near(
         *call(
             steps_kernel,
             [
                 cells.shape,
                 wide.shape,
-                (3, ex, ey, ez),
+                field.shape,
+                snaps.shape,
                 (buckets, 8, slots),
                 (3, buckets, slots),
             ],
-            aliases={2: 0, 3: 1},
-        )(c_low, c_high, cells, wide, wide_strip, row_hot, depth_hot, arrived, states)
+            aliases={2: 0, 3: 1, 4: 2, 5: 3},
+        )(c_low, c_high, cells, wide, field, snaps, wide_strip, row_hot, depth_hot, arrived, states)
     )
     home = lax.all_to_all(result, ("gy", "gz"), split_axis=0, concat_axis=0, tiled=True)
     electric, magnetic = call(last_kernel, [], [electric.shape, electric.shape])(

time: 54.8 us -> 50.1 us (0.914)
  waiting for transfers between devices: 18.7 us -> 13.9 us
  starting transfers between devices: 21.2 us -> 23 us
  Pallas kernels: 13.7 us -> 12.1 us
    ppermute x6, waiting for transfers between devices: 9.98 us -> 5.32 us  [shifted(): return lax.ppermute(value, axis, pairs)]
    ppermute x6, starting transfers between devices: 12.3 us -> 14.4 us  [shifted(): return lax.ppermute(value, axis, pairs)]
    pallas_call x3 -> x4, Pallas kernels: 5.67 us -> 4.55 us  [the longest x1 3.13 us: shards(): call(steps_kernel, [cells.shape, wide.shape, field.shape, snaps.shape, (b...]
    pallas_call x1, Pallas kernels: 3.09 us -> 2.15 us  [shards(): call(first_kernel, [(FIELDS - GRID, rows, depth), (rows, depth), (8, buck...]
  transfers between devices with their start and end apart: 9 -> 9, of which waited for: 5 -> 5; matrix products, arithmetic and copies ran while one was open for 0% -> 0% of each run, Pallas kernels for 7% -> 9%
where the time goes in v4:
time: 50.1 us; the launch traced here: 49.7 us
  starting transfers between devices  23 us (46%)
  waiting for transfers between devices  13.9 us (28%)
  Pallas kernels  12.1 us (24%)
  between operations  0.75 us (1%)
    ppermute x6, starting transfers between devices, shifted(): return lax.ppermute(value, axis, pairs)  14.4 us
    ppermute x6, waiting for transfers between devices, shifted(): return lax.ppermute(value, axis, pairs)  5.32 us
    all_to_all x1, starting transfers between devices, shards(): lax.all_to_all(packed, ('gy', 'gz'), split_axis=0, concat_axis=0, tiled=T...  5.17 us
    all_to_all x1, waiting for transfers between devices, shards(): lax.all_to_all(packed, ('gy', 'gz'), split_axis=0, concat_axis=0, tiled=T...  3.94 us
    all_to_all x1, waiting for transfers between devices, shards(): lax.all_to_all(result, ('gy', 'gz'), split_axis=0, concat_axis=0, tiled=T...  3.35 us
    all_to_all x1, starting transfers between devices, shards(): lax.all_to_all(result, ('gy', 'gz'), split_axis=0, concat_axis=0, tiled=T...  3.33 us
    pallas_call x1, Pallas kernels, shards(): call(steps_kernel, [cells.shape, wide.shape, field.shape, snaps.shape, (b...  3.13 us
    pallas_call x1, Pallas kernels, shards(): call(first_kernel, [(FIELDS - GRID, rows, depth), (rows, depth), (8, buck...  2.15 us
  transfers between devices with their start and end apart: 9, of which 5 were waited for; matrix products, arithmetic and copies ran while one was open for 0% of the time, Pallas kernels for 9%

profile of v4, /device:TPU:0, one launch (start us, length us, event | category | flops | bytes accessed | tf_op | source)
XLA Modules:
  0.0 49.7 jit_solution(3663806876711384322)
XLA Ops:
  0.6 1.5 %shard_map.121 = f32[8,13,128]{2,1,0:T(8,128)} custom-call(s32[1,8,128]{2,1,0:T(8,128)} %index.1, f32[2,3,1,8,128]{4,3,2,1,0:T(8,128)} %polar.1, f32[2,1,8,128]{3,2,1,0:T(8,128)} %popul.1, f32[1,8,128]{2,1,0:T(8,128)} %freq.1, f32[1,8,128]{2,1,0:T(8,128)} %dephase.1, f32[1,8,128]{2,1,0:T(8,128)} %strength.1, f32[1,8,128]{2,1,0:T(8,128)} %pumping.1), custom_call_target="tpu_custom_call" | custom-call | tf_op jit(solution)/shard_map/pallas_call | solution.py:530
  2.1 5.2 %all-to-all-start = ((f32[8,13,128]{2,1,0:T(8,128)}), f32[8,13,128]{2,1,0:T(8,128)S(1)}, u32[]{:S(2)}, u32[]{:S(2)}) async-start(f32[8,13,128]{2,1,0:T(8,128)} %shard_map.121), calls=%async_computation | async-start | bytes 131072 | tf_op jit(solution)/shard_map/all_to_all | solution.py:540
  7.3 1.1 %shard_map.120 = (f32[4,128,128]{2,1,0:T(8,128)S(1)}, bf16[384,256]{1,0:T(8,128)(2,1)S(1)}) custom-call(f32[3,8,16,128]{3,2,1,0:T(8,128)} %electric.1, s32[8,16,128]{2,1,0:T(8,128)} %classes.1), custom_call_target="tpu_custom_call" | custom-call | tf_op jit(solution)/shard_map/pallas_call | solution.py:534
  8.3 3.9 %all-to-all-done.arrived = f32[8,13,128]{2,1,0:T(8,128)S(1)} async-done(((f32[8,13,128]{2,1,0:T(8,128)}), f32[8,13,128]{2,1,0:T(8,128)S(1)}, u32[]{:S(2)}, u32[]{:S(2)}) %all-to-all-start) | async-done | bytes 53280 | tf_op jit(solution)/shard_map/all_to_all | solution.py:540
  12.3 2.2 %shard_map.122 = (f32[16,128,128]{2,1,0:T(8,128)S(1)}, f32[128,128]{1,0:T(8,128)S(1)}, f32[8,8,128]{2,1,0:T(8,128)S(1)}, bf16[256,1024]{1,0:T(8,128)(2,1)S(1)}, bf16[64,1024]{1,0:T(8,128)(2,1)S(1)}) custom-call(f32[8,13,128]{2,1,0:T(8,128)S(1)} %all-to-all-done.arrived, f32[4,128,128]{2,1,0:T(8,128)S(1)} %get-tuple-element.34.base, ...), custom_call_target="tpu_custom_call" | custom-call | tf_op jit(solution)/shard_map/pallas_call | solution.py:543
  14.4 0.1 collective-permute-start
  14.5 1.2 %collective-permute-done.from_low.from_high = f32[128,128]{1,0:T(8,128)S(1)} collective-permute-done((f32[128,128]{1,0:T(8,128)S(1)}, f32[128,128]{1,0:T(8,128)S(1)}, u32[]{:S(2)}, u32[]{:S(2)}) %collective-permute-start) | collective-permute-done | bytes 65568 | tf_op jit(solution)/shard_map/ppermute | solution.py:550
  15.8 0.2 shard_map.123
  15.9 2.5 %collective-permute-start.1 = (f32[45,8,128]{2,1,0:T(8,128)S(1)}, f32[45,8,128]{2,1,0:T(8,128)S(1)}, u32[]{:S(2)}, u32[]{:S(2)}) collective-permute-start(f32[45,8,128]{2,1,0:T(8,128)S(1)} %get-tuple-element.38), channel_id=1, source_target_pairs={{0,2},{2,4},{4,6},{1,3},{3,5},{5,7},{8,10},{10,12},{12,14},{9,11},... | collective-permute-start | bytes 552968 | tf_op jit(solution)/shard_map/ppermute | solution.py:515
  18.4 1.3 %collective-permute-start.2 = (f32[41,8,128]{2,1,0:T(8,128)S(1)}, f32[41,8,128]{2,1,0:T(8,128)S(1)}, u32[]{:S(2)}, u32[]{:S(2)}) collective-permute-start(f32[41,8,128]{2,1,0:T(8,128)S(1)} %get-tuple-element.39), channel_id=1, source_target_pairs={{2,0},{4,2},{6,4},{3,1},{5,3},{7,5},{10,8},{12,10},{14,12},{11,9},... | collective-permute-start | bytes 503816 | tf_op jit(solution)/shard_map/ppermute | solution.py:515
  19.7 1.3 %collective-permute-start.6 = (f32[41,16,128]{2,1,0:T(8,128)S(1)}, f32[41,16,128]{2,1,0:T(8,128)S(1)}, u32[]{:S(2)}, u32[]{:S(2)}) collective-permute-start(f32[41,16,128]{2,1,0:T(8,128)S(1)} %get-tuple-element.43), channel_id=1, source_target_pairs={{8,0},{16,8},{24,16},{9,1},{17,9},{25,17},{10,2},{18,10},{26,18},{... | collective-permute-start | bytes 1007624 | tf_op jit(solution)/shard_map/ppermute | solution.py:515
  21.0 4.6 %collective-permute-start.5 = (f32[45,16,128]{2,1,0:T(8,128)S(1)}, f32[45,16,128]{2,1,0:T(8,128)S(1)}, u32[]{:S(2)}, u32[]{:S(2)}) collective-permute-start(f32[45,16,128]{2,1,0:T(8,128)S(1)} %get-tuple-element.42), channel_id=1, source_target_pairs={{0,8},{8,16},{16,24},{1,9},{9,17},{17,25},{2,10},{10,18},{18,26},{... | collective-permute-start | bytes 1105928 | tf_op jit(solution)/shard_map/ppermute | solution.py:515
  25.6 2.5 %collective-permute-done.2.halo_high.y_high = f32[41,8,128]{2,1,0:T(8,128)S(1)} collective-permute-done((f32[41,8,128]{2,1,0:T(8,128)S(1)}, f32[41,8,128]{2,1,0:T(8,128)S(1)}, u32[]{:S(2)}, u32[]{:S(2)}) %collective-permute-start.2) | collective-permute-done | bytes 167968 | tf_op jit(solution)/shard_map/ppermute | solution.py:515
  28.1 0.0 collective-permute-done.1.halo_low.y_low
  28.1 0.1 shard_map.124
  28.2 3.5 %collective-permute-start.3 = (f32[112,128]{1,0:T(8,128)S(1)}, f32[112,128]{1,0:T(8,128)S(1)}, u32[]{:S(2)}, u32[]{:S(2)}) collective-permute-start(f32[112,128]{1,0:T(8,128)S(1)} %get-tuple-element.40), channel_id=1, source_target_pairs={{0,8},{8,16},{16,24},{1,9},{9,17},{17,25},{2,10},{10,18},{18,26},{... | collective-permute-start | bytes 172040 | tf_op jit(solution)/shard_map/ppermute | solution.py:515
  31.7 1.3 %collective-permute-start.4 = (f32[112,128]{1,0:T(8,128)S(1)}, f32[112,128]{1,0:T(8,128)S(1)}, u32[]{:S(2)}, u32[]{:S(2)}) collective-permute-start(f32[112,128]{1,0:T(8,128)S(1)} %get-tuple-element.41), channel_id=1, source_target_pairs={{8,0},{16,8},{24,16},{9,1},{17,9},{25,17},{10,2},{18,10},{26,18},{... | collective-permute-start | bytes 172040 | tf_op jit(solution)/shard_map/ppermute | solution.py:515
  33.0 1.7 %shard_map.125 = (f32[3,16,24,256]{3,2,1,0:T(8,128)S(1)}, f32[17,16,24,256]{3,2,1,0:T(8,128)S(1)}, f32[16,24,128]{2,1,0:T(8,128)S(1)}, f32[3,16,24,256]{3,2,1,0:T(8,128)S(1)}, f32[9,128,128]{2,1,0:T(8,128)S(1)}) custom-call(f32[4,128,128]{2,1,0:T(8,128)S(1)} %get-tuple-element.34.base, f32[16,128,128]{2,1,0:T(8,128)S(1)} %get-tuple-element.36.coefs, ...), custom_call_target="tpu_custom_call" | custom-call | tf_op jit(solution)/shard_map/pallas_call | solution.py:574
  34.7 0.0 collective-permute-done.6.x_high
  34.7 0.0 collective-permute-done.5.x_low
  34.7 0.3 shard_map.126
  35.0 0.0 collective-permute-done.3.c_low
  35.0 2.8 %collective-permute-done.4.c_high = f32[112,128]{1,0:T(8,128)S(1)} collective-permute-done((f32[112,128]{1,0:T(8,128)S(1)}, f32[112,128]{1,0:T(8,128)S(1)}, u32[]{:S(2)}, u32[]{:S(2)}) %collective-permute-start.4) | collective-permute-done | bytes 57376 | tf_op jit(solution)/shard_map/ppermute | solution.py:515
  37.8 3.1 %shard_map.127 = (f32[3,16,24,256]{3,2,1,0:T(8,128)S(1)}, f32[17,16,24,256]{3,2,1,0:T(8,128)S(1)}, f32[3,16,24,256]{3,2,1,0:T(8,128)S(1)}, f32[9,128,128]{2,1,0:...) custom-call(f32[112,128]{1,0:T(8,128)S(1)} %collective-permute-done., ...), custom_call_target="tpu_custom_call", output_to_operand_aliasing={{0}: (2, {}), {1}: (3, {}), {2}: (4, {}), {3}: (5, {})} | custom-call | tf_op jit(solution)/shard_map/pallas_call | solution.py:594
  40.9 3.3 %all-to-all-start.1 = ((f32[8,8,128]{2,1,0:T(8,128)}), f32[8,8,128]{2,1,0:T(8,128)S(1)}, u32[]{:S(2)}, u32[]{:S(2)}) async-start(f32[8,8,128]{2,1,0:T(8,128)} %get-tuple-element.61), calls=%async_computation.1 | async-start | bytes 65536 | tf_op jit(solution)/shard_map/all_to_all | solution.py:607
  44.2 1.4 %shard_map.128 = (f32[3,8,16,128]{3,2,1,0:T(8,128)}, f32[3,8,16,128]{3,2,1,0:T(8,128)}) custom-call(f32[3,16,24,256]{3,2,1,0:T(8,128)S(1)} %get-tuple-element.56.cells, f32[4,128,128]{2,1,0:T(8,128)S(1)} %get-tuple-element.34.base, f32[3,16,24,256]{3,2,1,0:T(8,128)S(1)} %get-tuple-element.57.field, f32[3,8,128]{2,1,0:T(8,128)S(1)} %get-tuple-element.58.changes, ...), custom_call_target="tpu_custom_call" | custom-call | tf_op jit(solution)/shard_map/pallas_call | solution.py:608
  45.7 3.3 %all-to-all-done.1.home = f32[8,8,128]{2,1,0:T(8,128)S(1)} async-done(((f32[8,8,128]{2,1,0:T(8,128)}), f32[8,8,128]{2,1,0:T(8,128)S(1)}, u32[]{:S(2)}, u32[]{:S(2)}) %all-to-all-start.1) | async-done | bytes 32800 | tf_op jit(solution)/shard_map/all_to_all | solution.py:607
  49.0 0.6 %shard_map.129 = (f32[2,3,1,8,128]{4,3,2,1,0:T(8,128)}, f32[2,1,8,128]{3,2,1,0:T(8,128)}) custom-call(f32[8,8,128]{2,1,0:T(8,128)S(1)} %all-to-all-done.1.home), custom_call_target="tpu_custom_call" | custom-call | tf_op jit(solution)/shard_map/pallas_call | solution.py:611
Async XLA Ops:
  2.1 10.2 %all-to-all-start = ((f32[8,13,128]{2,1,0:T(8,128)}), f32[8,13,128]{2,1,0:T(8,128)S(1)}, u32[]{:S(2)}, u32[]{:S(2)}) async-start(f32[8,13,128]{2,1,0:T(8,128)} %shard_map.121), calls=%async_computation | async-start | bytes 131072 | tf_op jit(solution)/shard_map/all_to_all | solution.py:540
  14.4 1.3 %collective-permute-start = (f32[128,128]{1,0:T(8,128)S(1)}, f32[128,128]{1,0:T(8,128)S(1)}, u32[]{:S(2)}, u32[]{:S(2)}) collective-permute-start(f32[128,128]{1,0:T(8,128)S(1)} %get-tuple-element.37), channel_id=1, source_target_pairs={{0,1},{1,0},{2,3},{3,2},{4,5},{5,4},{6,7},{7,6},{8,9},{9,8},{10,11... | collective-permute-start | bytes 196616 | tf_op jit(solution)/shard_map/ppermute | solution.py:550
  15.9 12.2 %collective-permute-start.1 = (f32[45,8,128]{2,1,0:T(8,128)S(1)}, f32[45,8,128]{2,1,0:T(8,128)S(1)}, u32[]{:S(2)}, u32[]{:S(2)}) collective-permute-start(f32[45,8,128]{2,1,0:T(8,128)S(1)} %get-tuple-element.38), channel_id=1, source_target_pairs={{0,2},{2,4},{4,6},{1,3},{3,5},{5,7},{8,10},{10,12},{12,14},{9,11},... | collective-permute-start | bytes 552968 | tf_op jit(solution)/shard_map/ppermute | solution.py:515
  18.4 9.7 %collective-permute-start.2 = (f32[41,8,128]{2,1,0:T(8,128)S(1)}, f32[41,8,128]{2,1,0:T(8,128)S(1)}, u32[]{:S(2)}, u32[]{:S(2)}) collective-permute-start(f32[41,8,128]{2,1,0:T(8,128)S(1)} %get-tuple-element.39), channel_id=1, source_target_pairs={{2,0},{4,2},{6,4},{3,1},{5,3},{7,5},{10,8},{12,10},{14,12},{11,9},... | collective-permute-start | bytes 503816 | tf_op jit(solution)/shard_map/ppermute | solution.py:515
  19.7 15.0 %collective-permute-start.6 = (f32[41,16,128]{2,1,0:T(8,128)S(1)}, f32[41,16,128]{2,1,0:T(8,128)S(1)}, u32[]{:S(2)}, u32[]{:S(2)}) collective-permute-start(f32[41,16,128]{2,1,0:T(8,128)S(1)} %get-tuple-element.43), channel_id=1, source_target_pairs={{8,0},{16,8},{24,16},{9,1},{17,9},{25,17},{10,2},{18,10},{26,18},{... | collective-permute-start | bytes 1007624 | tf_op jit(solution)/shard_map/ppermute | solution.py:515
  21.0 13.7 %collective-permute-start.5 = (f32[45,16,128]{2,1,0:T(8,128)S(1)}, f32[45,16,128]{2,1,0:T(8,128)S(1)}, u32[]{:S(2)}, u32[]{:S(2)}) collective-permute-start(f32[45,16,128]{2,1,0:T(8,128)S(1)} %get-tuple-element.42), channel_id=1, source_target_pairs={{0,8},{8,16},{16,24},{1,9},{9,17},{17,25},{2,10},{10,18},{18,26},{... | collective-permute-start | bytes 1105928 | tf_op jit(solution)/shard_map/ppermute | solution.py:515
  28.2 6.8 %collective-permute-start.3 = (f32[112,128]{1,0:T(8,128)S(1)}, f32[112,128]{1,0:T(8,128)S(1)}, u32[]{:S(2)}, u32[]{:S(2)}) collective-permute-start(f32[112,128]{1,0:T(8,128)S(1)} %get-tuple-element.40), channel_id=1, source_target_pairs={{0,8},{8,16},{16,24},{1,9},{9,17},{17,25},{2,10},{10,18},{18,26},{... | collective-permute-start | bytes 172040 | tf_op jit(solution)/shard_map/ppermute | solution.py:515
  31.7 6.1 %collective-permute-start.4 = (f32[112,128]{1,0:T(8,128)S(1)}, f32[112,128]{1,0:T(8,128)S(1)}, u32[]{:S(2)}, u32[]{:S(2)}) collective-permute-start(f32[112,128]{1,0:T(8,128)S(1)} %get-tuple-element.41), channel_id=1, source_target_pairs={{8,0},{16,8},{24,16},{9,1},{17,9},{25,17},{10,2},{18,10},{26,18},{... | collective-permute-start | bytes 172040 | tf_op jit(solution)/shard_map/ppermute | solution.py:515
  40.9 8.1 %all-to-all-start.1 = ((f32[8,8,128]{2,1,0:T(8,128)}), f32[8,8,128]{2,1,0:T(8,128)S(1)}, u32[]{:S(2)}, u32[]{:S(2)}) async-start(f32[8,8,128]{2,1,0:T(8,128)} %get-tuple-element.61), calls=%async_computation.1 | async-start | bytes 65536 | tf_op jit(solution)/shard_map/all_to_all | solution.py:607

commit v5 on v4

--- a/solution.py
+++ b/solution.py
@@ -17,45 +17,71 @@
 WIDTHS = (STEPS,) * 3 + (STEPS - 1,) * 4 + (STEPS - 2,) * 4 + (STEPS - 3,) * 9
 FIELDS = len(WIDTHS)
 GRID = 4
-ALL_WIDTHS = WIDTHS + (STEPS,)
 VECTORS = (0, 4, 7, 11)
-LANE_BASES = tuple(2 * sum(WIDTHS[:i]) for i in range(FIELDS))
+LANE_BASES = tuple(sum(WIDTHS[:i]) for i in range(FIELDS))
+LAYER_LANES = tuple(sum(w for w in WIDTHS if w > d) for d in range(STEPS))
+LAYER_BASES = tuple(sum(LAYER_LANES[:d]) for d in range(STEPS + 1))
 FOLDS = 2
 LONG = pl.CostEstimate(flops=20_000_000_000, bytes_accessed=100_000_000, transcendentals=0)
 VMEM_LIMIT = 24 * 1024 * 1024
 HIGH_LIMIT = 56 * 1024 * 1024
 
 
-def layer_list(skip_axis):
+def layer_list(skip_axis, strips):
     layers = []
-    for f, width in enumerate(ALL_WIDTHS):
+    for f, width in enumerate(WIDTHS):
         unused = skip_axis is not None and f - skip_axis in VECTORS
         layers += [(f, d) for d in range(width - 1 if unused else width)]
-    return layers
-
-
-LAYERS_LOW = (layer_list(0), layer_list(1))
-LAYERS_HIGH = layer_list(None)
-
-
-def corner_rows(layers, halo_sign):
+    return layers + [(FIELDS + i, 0) for i in range(strips)]
+
+
+def low_layers(axis, strips):
+    return layer_list(axis, strips)
+
+
+def high_layers(strips):
+    return layer_list(None, strips)
+
+
+def corner_rows(halo_sign, strips):
     out = []
     furthest = 0 if halo_sign < 0 else 1
-    for f, d in layers:
-        width = ALL_WIDTHS[f]
-        for side in (-1, 1):
-            reach = width - d
-            if side == halo_sign or any(
-                f in (v, v + 1, v + 2) and f != v + furthest for v in VECTORS
-            ):
-                reach -= 1
-            known = LAYERS_HIGH if side < 0 else LAYERS_LOW[1]
-            out += [(f, d, side, e) for e in range(reach) if (f, e) in known]
+    known_x = high_layers(0) if halo_sign < 0 else low_layers(0, 0)
+    for f, width in enumerate(WIDTHS + (STEPS,) * strips):
+        for d in range(width):
+            if f < FIELDS and (f, d) not in known_x:
+                continue
+            for side in (-1, 1):
+                reach = width - d
+                if side == halo_sign or any(
+                    f in (v, v + 1, v + 2) and f != v + furthest for v in VECTORS
+                ):
+                    reach -= 1
+                known = high_layers(0) if side < 0 else low_layers(1, 0)
+                out += [
+                    (f, d, side, e)
+                    for e in range(reach)
+                    if f >= FIELDS or (f, e) in known
+                ]
     return out
 
 
-def corner_shape(layers, halo_sign, depth):
-    return (-(-len(corner_rows(layers, halo_sign)) // 8) * 8, depth)
+def corner_shape(halo_sign, strips, depth):
+    return (-(-len(corner_rows(halo_sign, strips)) // 8) * 8, depth)
+
+
+def share_lanes(layers):
+    lane = lax.broadcasted_iota(jnp.int32, layers[0].shape, 1)
+    out = layers[0]
+    for d in range(1, STEPS):
+        turned = pltpu.roll(layers[d], LAYER_BASES[d], 1)
+        out = jnp.where(lane >= LAYER_BASES[d], turned, out)
+    return out
+
+
+def layer_of_shared(shared, d):
+    depth = shared.shape[1]
+    return pltpu.roll(shared, depth - LAYER_BASES[d], 1) if d else shared
 
 
 def inverse_permittivity(classes):
@@ -168,7 +194,9 @@
     return advanced, current, upper_next, pumped_next
 
 
-def pack_kernel(index, polar, popul, freq, dephase, strength, pumping, out):
+def pack_kernel(
+    electric, classes, index, polar, popul, freq, dephase, strength, pumping, out, base, left
+):
     for i in range(2):
         for c in range(3):
             out[:, 3 * i + c, :] = polar[i, c, 0]
@@ -177,15 +205,6 @@
     for f, source in enumerate((freq, dephase, strength, pumping)):
         out[:, 8 + f, :] = source[0]
     out[:, 12, :] = index[0].astype(jnp.float32)
-
-
-def source_of(base, coefs, strip, f):
-    if f < GRID:
-        return base.at[f]
-    return coefs.at[f - GRID] if f < FIELDS else strip
-
-
-def base_kernel(electric, classes, base, left):
     _, nx, ny, depth = electric.shape
     rows = nx * ny
     for c in range(3):
@@ -194,7 +213,13 @@
     left[...] = cell_halves([base[c] for c in range(3)])
 
 
-def first_kernel(arrived, base, left, coefs, strip, states, row_hot, depth_hot):
+def source_of(base, coefs, strip, f):
+    if f < GRID:
+        return base.at[f]
+    return coefs.at[f - GRID] if f < FIELDS else strip.at[f - FIELDS]
+
+
+def first_kernel(arrived, base, left, coefs, states, row_hot, depth_hot, *strip):
     _, rows, depth = base.shape
     index = arrived[:, 12, :].astype(jnp.int32)
     write_one_hots(index, row_hot, depth_hot, rows, depth)
@@ -228,66 +253,82 @@
     for number, block in enumerate(scatter_cells(values, row_hot, depth_hot, rows)):
         coefs[number] = block
     lane = lax.broadcasted_iota(jnp.int32, (rows, depth), 1)
-    packed = jnp.zeros((rows, depth), jnp.float32)
-    for f, width in enumerate(WIDTHS):
-        at = LANE_BASES[f]
-        turned = pltpu.roll(source_of(base, coefs, strip, f)[...], (at + width) % depth, 1)
-        packed = jnp.where((lane >= at) & (lane < at + 2 * width), turned, packed)
-    strip[...] = packed
-
-
-def faces_kernel(nx, ny, count_z, base, coefs, from_low, from_high, strip, x_low, x_high, y_low, y_high):
-    rows, depth = strip.shape
-    lane = lax.broadcasted_iota(jnp.int32, (rows, depth), 1)
-    top = jnp.zeros((rows, depth), jnp.bool_)
-    for f, width in enumerate(WIDTHS):
-        at = LANE_BASES[f]
-        top = top | ((lane >= at) & (lane < at + width))
-    me = lax.axis_index("gz")
-    strip[...] = jnp.where(
-        top,
-        jnp.where(me > 0, from_low[...], 0.0),
-        jnp.where(me < count_z - 1, from_high[...], 0.0),
-    )
-
-    def source(f):
-        return source_of(base, coefs, strip, f)
-
-    for at, (f, d) in enumerate(LAYERS_LOW[0]):
-        x_low[at] = source(f)[d * ny : (d + 1) * ny, :]
-    for at, (f, d) in enumerate(LAYERS_HIGH):
-        x_high[at] = source(f)[(nx - 1 - d) * ny : (nx - d) * ny, :]
-    for at, (f, d) in enumerate(LAYERS_LOW[1]):
-        y_low[at] = source(f)[pl.ds(d, nx, stride=ny), :]
-    for at, (f, d) in enumerate(LAYERS_HIGH):
-        y_high[at] = source(f)[pl.ds(ny - 1 - d, nx, stride=ny), :]
-
-
-def corners_kernel(halo_low, halo_high, low, high):
+    strips = len(strip)
+    for i in range(strips):
+        top = 1 - i if strips > 1 else jnp.where(lax.axis_index("gz") == 0, 1, 0)
+        packed = jnp.zeros((rows, depth), jnp.float32)
+        for f, width in enumerate(WIDTHS):
+            at = LANE_BASES[f]
+            turned = pltpu.roll(source_of(base, coefs, None, f)[...], at + width * top, 1)
+            packed = jnp.where((lane >= at) & (lane < at + width), turned, packed)
+        strip[i][0] = packed
+
+
+def join_kernel(first, second, out):
+    out[0] = first[0]
+    out[1] = second[0]
+
+
+def faces_kernel(nx, ny, base, coefs, strip, y_low, y_high, x_low, x_high):
+    strips = strip.shape[0]
+    for face, layers, sign, axis in (
+        (y_low, low_layers(1, strips), -1, 1),
+        (y_high, high_layers(strips), 1, 1),
+        (x_low, low_layers(0, strips), -1, 0),
+        (x_high, high_layers(strips), 1, 0),
+    ):
+
+        def layer(f, d):
+            source = source_of(base, coefs, strip, f)
+            at = d if sign < 0 else (nx, ny)[axis] - 1 - d
+            if axis == 1:
+                return source[pl.ds(at, nx, stride=ny), :]
+            return source[at * ny : (at + 1) * ny, :]
+
+        for at, (f, d) in enumerate(layers):
+            if f < FIELDS:
+                face[at] = layer(f, d)
+            else:
+                face[at] = share_lanes([layer(f, i) for i in range(STEPS)])
+
+
+def corners_kernel(strips, halo_low, halo_high, low, high):
     nx = halo_low.shape[1]
-    for face, layers, sign in ((low, LAYERS_LOW[0], -1), (high, LAYERS_HIGH, 1)):
-        for row, (f, d, side, e) in enumerate(corner_rows(layers, -sign)):
+    for face, sign in ((low, -1), (high, 1)):
+        for row, (f, d, side, e) in enumerate(corner_rows(-sign, strips)):
             x = d if sign < 0 else nx - 1 - d
-            if side < 0:
-                value = halo_low[LAYERS_HIGH.index((f, e)), x : x + 1, :]
-            else:
-                value = halo_high[LAYERS_LOW[1].index((f, e)), x : x + 1, :]
-            face[row : row + 1, :] = value
+            halo = halo_low if side < 0 else halo_high
+            layers = high_layers(strips) if side < 0 else low_layers(1, strips)
+            at = layers.index((f, e if f < FIELDS else 0))
+            value = halo[at, x : x + 1, :]
+            face[row : row + 1, :] = value if f < FIELDS else layer_of_shared(value, e)
 
 
 def place(cells, wide, wide_strip, f):
     if f < 3:
         return cells.at[f]
-    return wide.at[f - 3] if f < FIELDS else wide_strip
+    return wide.at[f - 3] if f < FIELDS else wide_strip.at[f - FIELDS]
 
 
 def spread_strip(cells, wide, wide_strip, x, y, count, fields):
-    depth = wide_strip.shape[2]
-    value = wide_strip[x, y : y + count]
+    strips, _, _, depth = wide_strip.shape
+    values = [wide_strip[i, x, y : y + count] for i in range(strips)]
+    upper = lax.broadcasted_iota(jnp.int32, (count, depth), 1) >= depth // 2
+    low = lax.axis_index("gz") > 0
     for f in fields:
-        place(cells, wide, wide_strip, f)[x, y : y + count, depth : 2 * depth] = pltpu.roll(
-            value, (-(LANE_BASES[f] + WIDTHS[f])) % depth, 1
-        )
+        at, width = LANE_BASES[f], WIDTHS[f]
+        if strips == 1:
+            shift = lax.bitwise_and(depth - at - jnp.where(low, width, 0), depth - 1)
+            value = pltpu.roll(values[0], shift, 1)
+            if f < GRID:
+                value = jnp.where(upper == low, value, 0.0)
+        else:
+            value = jnp.where(
+                upper,
+                pltpu.roll(values[0], (depth - at - width) % depth, 1),
+                pltpu.roll(values[1], (depth - at) % depth, 1),
+            )
+        place(cells, wide, wide_strip, f)[x, y : y + count, depth : 2 * depth] = value
 
 
 def assemble_kernel(
@@ -296,16 +337,23 @@
     _, nx, depth = y_low.shape
     _, ex, ey, ez = cells.shape
     ny = ey - 2 * STEPS
-    for f in range(FIELDS + 1):
+    strips = strip.shape[0]
+    for f in range(FIELDS + strips):
         source = source_of(base, coefs, strip, f)
         target = place(cells, wide, wide_strip, f)
         target[STEPS : STEPS + nx, 0:ny, 0:depth] = source[...].reshape(nx, ny, depth)
         target[STEPS : STEPS + nx, ny:ey, 0:depth] = jnp.zeros((nx, 2 * STEPS, depth), jnp.float32)
-    for halo, layers, sign in ((y_low, LAYERS_HIGH, -1), (y_high, LAYERS_LOW[1], 1)):
-        for at, (f, d) in enumerate(layers):
-            y = ey - 1 - d if sign < 0 else ny + d
-            for x in range(nx):
-                place(cells, wide, wide_strip, f)[STEPS + x, y : y + 1, 0:depth] = halo[at, x : x + 1, :]
+    for halo, layers, sign in (
+        (y_low, high_layers(strips), -1),
+        (y_high, low_layers(1, strips), 1),
+    ):
+        for at, (f, first) in enumerate(layers):
+            target = place(cells, wide, wide_strip, f)
+            for d in range(STEPS) if f >= FIELDS else (first,):
+                y = ey - 1 - d if sign < 0 else ny + d
+                value = halo[at] if f < FIELDS else layer_of_shared(halo[at], d)
+                for x in range(nx):
+                    target[STEPS + x, y : y + 1, 0:depth] = value[x : x + 1]
     for x in range(STEPS, STEPS + nx):
         spread_strip(cells, wide, wide_strip, x, 0, ey, range(FIELDS))
     inside = inside_mask(ey, ez)
@@ -327,12 +375,18 @@
     _, ny, depth = x_low.shape
     _, ex, ey, _ = cells.shape
     nx = ex - 2 * STEPS
-    for at, (f, d) in enumerate(LAYERS_HIGH):
-        place(cells, wide, wide_strip, f)[STEPS - 1 - d, 0:ny, 0:depth] = x_low[at]
-    for at, (f, d) in enumerate(LAYERS_LOW[0]):
-        place(cells, wide, wide_strip, f)[STEPS + nx + d, 0:ny, 0:depth] = x_high[at]
+    strips = wide_strip.shape[0]
+    for halo, layers, sign in (
+        (x_low, high_layers(strips), -1),
+        (x_high, low_layers(0, strips), 1),
+    ):
+        for at, (f, first) in enumerate(layers):
+            for d in range(STEPS) if f >= FIELDS else (first,):
+                x = STEPS - 1 - d if sign < 0 else STEPS + nx + d
+                value = halo[at] if f < FIELDS else layer_of_shared(halo[at], d)
+                place(cells, wide, wide_strip, f)[x, 0:ny, 0:depth] = value
     for x, fields in side_slabs(nx):
-        for f in (*fields, FIELDS):
+        for f in (*fields, *range(FIELDS, FIELDS + strips)):
             target = place(cells, wide, wide_strip, f)
             target[x, ny:ey, :] = jnp.zeros((2 * STEPS, target.shape[2]), jnp.float32)
         spread_strip(cells, wide, wide_strip, x, 0, ny, fields)
@@ -425,8 +479,8 @@
     _, ex, ey, ez = wide.shape
     nx, ny, depth = ex - 2 * STEPS, ey - 2 * STEPS, ez // 2
     rows = nx * ny
-    for corner, layers, sign in ((c_low, LAYERS_HIGH, -1), (c_high, LAYERS_LOW[0], 1)):
-        for row, (f, d, side, e) in enumerate(corner_rows(layers, sign)):
+    for corner, sign in ((c_low, -1), (c_high, 1)):
+        for row, (f, d, side, e) in enumerate(corner_rows(sign, wide_strip.shape[0])):
             x = STEPS - 1 - d if sign < 0 else STEPS + nx + d
             y = ey - 1 - e if side < 0 else ny + e
             place(cells, wide, wide_strip, f)[x, y : y + 1, 0:depth] = corner[row : row + 1, :]
@@ -527,46 +581,54 @@
         (FOLDS * rows, buckets * slots, jnp.bfloat16),
         (depth // FOLDS, buckets * slots, jnp.bfloat16),
     ]
-    (packed,) = call(pack_kernel, [(buckets, 13, slots)], limit=HIGH_LIMIT)(
-        cell_index, polarization, populations, resonance, dephasing, coupling, pump_rate
-    )
-    base, left = near(
+    packed, base, left = near(
         *call(
-            base_kernel,
-            [(GRID, rows, depth), (6 * depth // FOLDS, FOLDS * rows, jnp.bfloat16)],
+            pack_kernel,
+            [
+                (buckets, 13, slots),
+                (GRID, rows, depth),
+                (6 * depth // FOLDS, FOLDS * rows, jnp.bfloat16),
+            ],
             limit=HIGH_LIMIT,
-        )(electric, permittivity_class)
+        )(
+            electric, permittivity_class, cell_index, polarization, populations,
+            resonance, dephasing, coupling, pump_rate,
+        )
     )
     arrived = lax.all_to_all(packed, ("gy", "gz"), split_axis=0, concat_axis=0, tiled=True)
     (arrived,) = near(arrived)
-    coefs, strip, states, row_hot, depth_hot = near(
+    strips = 1 if lax.axis_size("gz") == 2 else 2
+    coefs, states, row_hot, depth_hot, *strip = near(
         *call(
             first_kernel,
-            [(FIELDS - GRID, rows, depth), (rows, depth), (8, buckets, slots), *hots],
+            [
+                (FIELDS - GRID, rows, depth),
+                (8, buckets, slots),
+                *hots,
+                *[(1, rows, depth)] * strips,
+            ],
         )(arrived, base, left)
     )
-    count_z = lax.axis_size("gz")
-    if count_z == 2:
-        from_low = from_high = lax.ppermute(strip, "gz", [(0, 1), (1, 0)])
+    if strips == 1:
+        (strip,) = near(lax.ppermute(strip[0], "gz", [(0, 1), (1, 0)]))
     else:
-        from_low = shifted(strip, "gz", 1)
-        from_high = shifted(strip, "gz", -1)
-    strip, *faces = call(
-        functools.partial(faces_kernel, nx, ny, count_z),
+        strip = near(shifted(strip[0], "gz", 1), shifted(strip[1], "gz", -1))
+        (strip,) = near(*call(join_kernel, [(strips, rows, depth)])(*strip))
+    high = len(high_layers(strips))
+    faces = call(
+        functools.partial(faces_kernel, nx, ny),
         [
-            (rows, depth),
-            (len(LAYERS_LOW[0]), ny, depth),
-            (len(LAYERS_HIGH), ny, depth),
-            (len(LAYERS_LOW[1]), nx, depth),
-            (len(LAYERS_HIGH), nx, depth),
+            (len(low_layers(1, strips)), nx, depth),
+            (high, nx, depth),
+            (len(low_layers(0, strips)), ny, depth),
+            (high, ny, depth),
         ],
-    )(base, coefs, *near(from_low, from_high))
-    (strip,) = near(strip)
-    x_low, x_high = near(shifted(faces[1], "gx", 1), shifted(faces[0], "gx", -1))
-    y_low, y_high = near(shifted(faces[3], "gy", 1), shifted(faces[2], "gy", -1))
+    )(base, coefs, strip)
+    y_low, y_high = near(shifted(faces[1], "gy", 1), shifted(faces[0], "gy", -1))
+    x_low, x_high = near(shifted(faces[3], "gx", 1), shifted(faces[2], "gx", -1))
     low, high = call(
-        corners_kernel,
-        [corner_shape(LAYERS_LOW[0], 1, depth), corner_shape(LAYERS_HIGH, -1, depth)],
+        functools.partial(corners_kernel, strips),
+        [corner_shape(1, strips, depth), corner_shape(-1, strips, depth)],
         cost=LONG,
     )(y_low, y_high)
     c_low, c_high = near(shifted(high, "gx", 1), shifted(low, "gx", -1))
@@ -576,7 +638,7 @@
             [
                 (3, ex, ey, ez),
                 (FIELDS - 3, ex, ey, ez),
-                (ex, ey, depth),
+                (strips, ex, ey, depth),
                 (3, ex, ey, ez),
                 (3 * (STEPS - 1), rows, depth),
             ],

time: 50.1 us -> 48.7 us (0.972)
  blocking collectives: 0 us -> 9.99 us
  starting transfers between devices: 23 us -> 17.8 us
  waiting for transfers between devices: 13.9 us -> 9.42 us
  Pallas kernels: 12.1 us -> 10.3 us
    all_to_all x0 -> x1, blocking collectives: none -> 9.99 us  [shards(): lax.all_to_all(packed, ('gy', 'gz'), split_axis=0, concat_axis=0, tiled=T...]
    all_to_all x1 -> x0, starting transfers between devices: 5.17 us -> none  [shards(): lax.all_to_all(packed, ('gy', 'gz'), split_axis=0, concat_axis=0, tiled=T...]
    all_to_all x1 -> x0, waiting for transfers between devices: 3.94 us -> none  [shards(): lax.all_to_all(packed, ('gy', 'gz'), split_axis=0, concat_axis=0, tiled=T...]
    pallas_call x6 -> x5, Pallas kernels: 6.62 us -> 5.19 us  [the longest x1 2.16 us: shards(): call(first_kernel, [(FIELDS - GRID, rows, depth), (8, buckets, slots), *h...]
  transfers between devices with their start and end apart: 9 -> 8, of which waited for: 5 -> 4; matrix products, arithmetic and copies ran while one was open for 0% -> 0% of each run, Pallas kernels for 9% -> 7%
where the time goes in v5:
time: 48.7 us; the launch traced here: 48.3 us
  starting transfers between devices  17.8 us (37%)
  Pallas kernels  10.3 us (21%)
  blocking collectives  9.99 us (21%)
  waiting for transfers between devices  9.42 us (19%)
  between operations  0.75 us (2%)
    ppermute x6, starting transfers between devices, shifted(): return lax.ppermute(value, axis, pairs)  14.4 us
    all_to_all x1, blocking collectives, shards(): lax.all_to_all(packed, ('gy', 'gz'), split_axis=0, concat_axis=0, tiled=T...  9.99 us
    ppermute x6, waiting for transfers between devices, shifted(): return lax.ppermute(value, axis, pairs)  4.83 us
    all_to_all x1, waiting for transfers between devices, shards(): lax.all_to_all(result, ('gy', 'gz'), split_axis=0, concat_axis=0, tiled=T...  3.35 us
    all_to_all x1, starting transfers between devices, shards(): lax.all_to_all(result, ('gy', 'gz'), split_axis=0, concat_axis=0, tiled=T...  3.33 us
    pallas_call x1, Pallas kernels, shards(): call(steps_kernel, [cells.shape, wide.shape, field.shape, snaps.shape, (b...  2.81 us
    pallas_call x1, Pallas kernels, shards(): call(first_kernel, [(FIELDS - GRID, rows, depth), (8, buckets, slots), *h...  2.16 us
    pallas_call x1, Pallas kernels, shards(): call(assemble_kernel, [(3, ex, ey, ez), (FIELDS - 3, ex, ey, ez), (strips...  1.61 us
  transfers between devices with their start and end apart: 8, of which 4 were waited for; matrix products, arithmetic and copies ran while one was open for 0% of the time, Pallas kernels for 7%

profile of v5, /device:TPU:0, one launch (start us, length us, event | category | flops | bytes accessed | tf_op | source)
XLA Modules:
  0.0 48.3 jit_solution(5187302346245660822)
XLA Ops:
  0.6 1.2 %shard_map.120 = (f32[8,13,128]{2,1,0:T(8,128)S(1)}, f32[4,128,128]{2,1,0:T(8,128)S(1)}, bf16[384,256]{1,0:T(8,128)(2,1)S(1)}) custom-call(f32[3,8,16,128]{3,2,1,0:T(8,128)} %electric.1, s32[8,16,128]{2,1,0:T(8,128)} %classes.1, s32[1,8,128]{2,1,0:T(8,128)} %index.1, f32[2,3,1,8,128]{4,3,2,1,0:T(8,128)} %polar.1, f32[2,1,8,128]{3,2,1,0:T(8,128)} %popul.1, ...), custom_call_target="tpu_custom_call" | custom-call | tf_op jit(solution)/shard_map/pallas_call | solution.py:585
  1.8 10.0 %all_to_all.10.arrived = f32[8,13,128]{2,1,0:T(8,128)S(1)} all-to-all(f32[8,13,128]{2,1,0:T(8,128)S(1)} %get-tuple-element.35), channel_id=1, replica_groups=mesh['gx'=4,'gy'=4,'gz'=2] {'gy','gz'}, dimensions={0} | all-to-all | bytes 106496 | tf_op jit(solution)/shard_map/all_to_all | solution.py:598
  11.8 2.2 %shard_map.121 = (f32[16,128,128]{2,1,0:T(8,128)S(1)}, f32[8,8,128]{2,1,0:T(8,128)S(1)}, bf16[256,1024]{1,0:T(8,128)(2,1)S(1)}, bf16[64,1024]{1,0:T(8,128)(2,1)S(1)}, f32[1,128,128]{2,1,0:T(8,128)S(1)}) custom-call(f32[8,13,128]{2,1,0:T(8,128)S(1)} %all_to_all.10.arrived, f32[4,128,128]{2,1,0:T(8,128)S(1)} %get-tuple-element.34.base, ...), custom_call_target="tpu_custom_call" | custom-call | tf_op jit(solution)/shard_map/pallas_call | solution.py:602
  14.0 0.1 collective-permute-start
  14.0 1.2 %collective-permute-done.strip = f32[1,128,128]{2,1,0:T(8,128)S(1)} collective-permute-done((f32[1,128,128]{2,1,0:T(8,128)S(1)}, f32[1,128,128]{2,1,0:T(8,128)S(1)}, u32[]{:S(2)}, u32[]{:S(2)}) %collective-permute-start) | collective-permute-done | bytes 65568 | tf_op jit(solution)/shard_map/ppermute | solution.py:613
  15.3 0.1 shard_map.122
  15.4 2.5 %collective-permute-start.1 = (f32[42,8,128]{2,1,0:T(8,128)S(1)}, f32[42,8,128]{2,1,0:T(8,128)S(1)}, u32[]{:S(2)}, u32[]{:S(2)}) collective-permute-start(f32[42,8,128]{2,1,0:T(8,128)S(1)} %get-tuple-element.39), channel_id=1, source_target_pairs={{0,2},{2,4},{4,6},{1,3},{3,5},{5,7},{8,10},{10,12},{12,14},{9,11},... | collective-permute-start | bytes 516104 | tf_op jit(solution)/shard_map/ppermute | solution.py:569
  17.9 1.3 %collective-permute-start.2 = (f32[38,8,128]{2,1,0:T(8,128)S(1)}, f32[38,8,128]{2,1,0:T(8,128)S(1)}, u32[]{:S(2)}, u32[]{:S(2)}) collective-permute-start(f32[38,8,128]{2,1,0:T(8,128)S(1)} %get-tuple-element.40), channel_id=1, source_target_pairs={{2,0},{4,2},{6,4},{3,1},{5,3},{7,5},{10,8},{12,10},{14,12},{11,9},... | collective-permute-start | bytes 466952 | tf_op jit(solution)/shard_map/ppermute | solution.py:569
  19.2 1.3 %collective-permute-start.6 = (f32[38,16,128]{2,1,0:T(8,128)S(1)}, f32[38,16,128]{2,1,0:T(8,128)S(1)}, u32[]{:S(2)}, u32[]{:S(2)}) collective-permute-start(f32[38,16,128]{2,1,0:T(8,128)S(1)} %get-tuple-element.44), channel_id=1, source_target_pairs={{8,0},{16,8},{24,16},{9,1},{17,9},{25,17},{10,2},{18,10},{26,18},{... | collective-permute-start | bytes 933896 | tf_op jit(solution)/shard_map/ppermute | solution.py:569
  20.5 4.6 %collective-permute-start.5 = (f32[42,16,128]{2,1,0:T(8,128)S(1)}, f32[42,16,128]{2,1,0:T(8,128)S(1)}, u32[]{:S(2)}, u32[]{:S(2)}) collective-permute-start(f32[42,16,128]{2,1,0:T(8,128)S(1)} %get-tuple-element.43), channel_id=1, source_target_pairs={{0,8},{8,16},{16,24},{1,9},{9,17},{17,25},{2,10},{10,18},{18,26},{... | collective-permute-start | bytes 1032200 | tf_op jit(solution)/shard_map/ppermute | solution.py:569
  25.1 2.0 %collective-permute-done.2.halo_high.y_high = f32[38,8,128]{2,1,0:T(8,128)S(1)} collective-permute-done((f32[38,8,128]{2,1,0:T(8,128)S(1)}, f32[38,8,128]{2,1,0:T(8,128)S(1)}, u32[]{:S(2)}, u32[]{:S(2)}) %collective-permute-start.2) | collective-permute-done | bytes 155680 | tf_op jit(solution)/shard_map/ppermute | solution.py:569
  27.1 0.0 collective-permute-done.1.halo_low.y_low
  27.1 0.1 shard_map.123
  27.2 3.5 %collective-permute-start.3 = (f32[112,128]{1,0:T(8,128)S(1)}, f32[112,128]{1,0:T(8,128)S(1)}, u32[]{:S(2)}, u32[]{:S(2)}) collective-permute-start(f32[112,128]{1,0:T(8,128)S(1)} %get-tuple-element.41), channel_id=1, source_target_pairs={{0,8},{8,16},{16,24},{1,9},{9,17},{17,25},{2,10},{10,18},{18,26},{... | collective-permute-start | bytes 172040 | tf_op jit(solution)/shard_map/ppermute | solution.py:569
  30.7 1.3 %collective-permute-start.4 = (f32[112,128]{1,0:T(8,128)S(1)}, f32[112,128]{1,0:T(8,128)S(1)}, u32[]{:S(2)}, u32[]{:S(2)}) collective-permute-start(f32[112,128]{1,0:T(8,128)S(1)} %get-tuple-element.42), channel_id=1, source_target_pairs={{8,0},{16,8},{24,16},{9,1},{17,9},{25,17},{10,2},{18,10},{26,18},{... | collective-permute-start | bytes 172040 | tf_op jit(solution)/shard_map/ppermute | solution.py:569
  32.0 1.6 %shard_map.124 = (f32[3,16,24,256]{3,2,1,0:T(8,128)S(1)}, f32[17,16,24,256]{3,2,1,0:T(8,128)S(1)}, f32[1,16,24,128]{3,2,1,0:T(8,128)S(1)}, f32[3,16,24,256]{3,2,1,0:T(8,128)S(1)}, f32[9,128,128]{2,1,0:T(8,128)S(1)}) custom-call(f32[4,128,128]{2,1,0:T(8,128)S(1)} %get-tuple-element.34.base, f32[16,128,128]{2,1,0:T(8,128)S(1)} %get-tuple-element.37.coefs, ...), custom_call_target="tpu_custom_call" | custom-call | tf_op jit(solution)/shard_map/pallas_call | solution.py:636
  33.6 0.0 collective-permute-done.6.x_high
  33.6 0.0 collective-permute-done.5.x_low
  33.6 0.3 shard_map.125
  33.9 0.0 collective-permute-done.3.c_low
  33.9 2.8 %collective-permute-done.4.c_high = f32[112,128]{1,0:T(8,128)S(1)} collective-permute-done((f32[112,128]{1,0:T(8,128)S(1)}, f32[112,128]{1,0:T(8,128)S(1)}, u32[]{:S(2)}, u32[]{:S(2)}) %collective-permute-start.4) | collective-permute-done | bytes 57376 | tf_op jit(solution)/shard_map/ppermute | solution.py:569
  36.8 2.8 %shard_map.126 = (f32[3,16,24,256]{3,2,1,0:T(8,128)S(1)}, f32[17,16,24,256]{3,2,1,0:T(8,128)S(1)}, f32[3,16,24,256]{3,2,1,0:T(8,128)S(1)}, f32[9,128,128]{2,1,0:...) custom-call(f32[112,128]{1,0:T(8,128)S(1)} %collective-permute-done., ...), custom_call_target="tpu_custom_call", output_to_operand_aliasing={{0}: (2, {}), {1}: (3, {}), {2}: (4, {}), {3}: (5, {})} | custom-call | tf_op jit(solution)/shard_map/pallas_call | solution.py:656
  39.6 3.3 %all-to-all-start.1 = ((f32[8,8,128]{2,1,0:T(8,128)}), f32[8,8,128]{2,1,0:T(8,128)S(1)}, u32[]{:S(2)}, u32[]{:S(2)}) async-start(f32[8,8,128]{2,1,0:T(8,128)} %get-tuple-element.61), calls=%async_computation.1 | async-start | bytes 65536 | tf_op jit(solution)/shard_map/all_to_all | solution.py:669
  42.9 1.4 %shard_map.127 = (f32[3,8,16,128]{3,2,1,0:T(8,128)}, f32[3,8,16,128]{3,2,1,0:T(8,128)}) custom-call(f32[3,16,24,256]{3,2,1,0:T(8,128)S(1)} %get-tuple-element.56.cells, f32[4,128,128]{2,1,0:T(8,128)S(1)} %get-tuple-element.34.base, f32[3,16,24,256]{3,2,1,0:T(8,128)S(1)} %get-tuple-element.57.field, f32[3,8,128]{2,1,0:T(8,128)S(1)} %get-tuple-element.58.changes, ...), custom_call_target="tpu_custom_call" | custom-call | tf_op jit(solution)/shard_map/pallas_call | solution.py:670
  44.3 3.4 %all-to-all-done.1.home = f32[8,8,128]{2,1,0:T(8,128)S(1)} async-done(((f32[8,8,128]{2,1,0:T(8,128)}), f32[8,8,128]{2,1,0:T(8,128)S(1)}, u32[]{:S(2)}, u32[]{:S(2)}) %all-to-all-start.1) | async-done | bytes 32800 | tf_op jit(solution)/shard_map/all_to_all | solution.py:669
  47.7 0.6 %shard_map.128 = (f32[2,3,1,8,128]{4,3,2,1,0:T(8,128)}, f32[2,1,8,128]{3,2,1,0:T(8,128)}) custom-call(f32[8,8,128]{2,1,0:T(8,128)S(1)} %all-to-all-done.1.home), custom_call_target="tpu_custom_call" | custom-call | tf_op jit(solution)/shard_map/pallas_call | solution.py:673
Async XLA Ops:
  14.0 1.3 %collective-permute-start = (f32[1,128,128]{2,1,0:T(8,128)S(1)}, f32[1,128,128]{2,1,0:T(8,128)S(1)}, u32[]{:S(2)}, u32[]{:S(2)}) collective-permute-start(f32[1,128,128]{2,1,0:T(8,128)S(1)} %get-tuple-element.38), channel_id=1, source_target_pairs={{0,1},{1,0},{2,3},{3,2},{4,5},{5,4},{6,7},{7,6},{8,9},{9,8},{10,11... | collective-permute-start | bytes 196616 | tf_op jit(solution)/shard_map/ppermute | solution.py:613
  15.4 11.7 %collective-permute-start.1 = (f32[42,8,128]{2,1,0:T(8,128)S(1)}, f32[42,8,128]{2,1,0:T(8,128)S(1)}, u32[]{:S(2)}, u32[]{:S(2)}) collective-permute-start(f32[42,8,128]{2,1,0:T(8,128)S(1)} %get-tuple-element.39), channel_id=1, source_target_pairs={{0,2},{2,4},{4,6},{1,3},{3,5},{5,7},{8,10},{10,12},{12,14},{9,11},... | collective-permute-start | bytes 516104 | tf_op jit(solution)/shard_map/ppermute | solution.py:569
  17.9 9.2 %collective-permute-start.2 = (f32[38,8,128]{2,1,0:T(8,128)S(1)}, f32[38,8,128]{2,1,0:T(8,128)S(1)}, u32[]{:S(2)}, u32[]{:S(2)}) collective-permute-start(f32[38,8,128]{2,1,0:T(8,128)S(1)} %get-tuple-element.40), channel_id=1, source_target_pairs={{2,0},{4,2},{6,4},{3,1},{5,3},{7,5},{10,8},{12,10},{14,12},{11,9},... | collective-permute-start | bytes 466952 | tf_op jit(solution)/shard_map/ppermute | solution.py:569
  19.2 14.4 %collective-permute-start.6 = (f32[38,16,128]{2,1,0:T(8,128)S(1)}, f32[38,16,128]{2,1,0:T(8,128)S(1)}, u32[]{:S(2)}, u32[]{:S(2)}) collective-permute-start(f32[38,16,128]{2,1,0:T(8,128)S(1)} %get-tuple-element.44), channel_id=1, source_target_pairs={{8,0},{16,8},{24,16},{9,1},{17,9},{25,17},{10,2},{18,10},{26,18},{... | collective-permute-start | bytes 933896 | tf_op jit(solution)/shard_map/ppermute | solution.py:569
  20.5 13.1 %collective-permute-start.5 = (f32[42,16,128]{2,1,0:T(8,128)S(1)}, f32[42,16,128]{2,1,0:T(8,128)S(1)}, u32[]{:S(2)}, u32[]{:S(2)}) collective-permute-start(f32[42,16,128]{2,1,0:T(8,128)S(1)} %get-tuple-element.43), channel_id=1, source_target_pairs={{0,8},{8,16},{16,24},{1,9},{9,17},{17,25},{2,10},{10,18},{18,26},{... | collective-permute-start | bytes 1032200 | tf_op jit(solution)/shard_map/ppermute | solution.py:569
  27.2 6.7 %collective-permute-start.3 = (f32[112,128]{1,0:T(8,128)S(1)}, f32[112,128]{1,0:T(8,128)S(1)}, u32[]{:S(2)}, u32[]{:S(2)}) collective-permute-start(f32[112,128]{1,0:T(8,128)S(1)} %get-tuple-element.41), channel_id=1, source_target_pairs={{0,8},{8,16},{16,24},{1,9},{9,17},{17,25},{2,10},{10,18},{18,26},{... | collective-permute-start | bytes 172040 | tf_op jit(solution)/shard_map/ppermute | solution.py:569
  30.7 6.1 %collective-permute-start.4 = (f32[112,128]{1,0:T(8,128)S(1)}, f32[112,128]{1,0:T(8,128)S(1)}, u32[]{:S(2)}, u32[]{:S(2)}) collective-permute-start(f32[112,128]{1,0:T(8,128)S(1)} %get-tuple-element.42), channel_id=1, source_target_pairs={{8,0},{16,8},{24,16},{9,1},{17,9},{25,17},{10,2},{18,10},{26,18},{... | collective-permute-start | bytes 172040 | tf_op jit(solution)/shard_map/ppermute | solution.py:569
  39.6 8.1 %all-to-all-start.1 = ((f32[8,8,128]{2,1,0:T(8,128)}), f32[8,8,128]{2,1,0:T(8,128)S(1)}, u32[]{:S(2)}, u32[]{:S(2)}) async-start(f32[8,8,128]{2,1,0:T(8,128)} %get-tuple-element.61), calls=%async_computation.1 | async-start | bytes 65536 | tf_op jit(solution)/shard_map/all_to_all | solution.py:669

commit v6 on v5

--- a/solution.py
+++ b/solution.py
@@ -53,7 +53,7 @@
                 continue
             for side in (-1, 1):
                 reach = width - d
-                if side == halo_sign or any(
+                if f >= FIELDS or side == halo_sign or any(
                     f in (v, v + 1, v + 2) and f != v + furthest for v in VECTORS
                 ):
                     reach -= 1
@@ -286,21 +286,22 @@
             return source[at * ny : (at + 1) * ny, :]
 
         for at, (f, d) in enumerate(layers):
+            count = nx if axis == 1 else ny
             if f < FIELDS:
-                face[at] = layer(f, d)
+                value = layer(f, d)
             else:
-                face[at] = share_lanes([layer(f, i) for i in range(STEPS)])
-
-
-def corners_kernel(strips, halo_low, halo_high, low, high):
-    nx = halo_low.shape[1]
+                value = share_lanes([layer(f, i) for i in range(STEPS)])
+            face[at * count : (at + 1) * count, :] = value
+
+
+def corners_kernel(nx, strips, halo_low, halo_high, low, high):
     for face, sign in ((low, -1), (high, 1)):
         for row, (f, d, side, e) in enumerate(corner_rows(-sign, strips)):
             x = d if sign < 0 else nx - 1 - d
             halo = halo_low if side < 0 else halo_high
             layers = high_layers(strips) if side < 0 else low_layers(1, strips)
             at = layers.index((f, e if f < FIELDS else 0))
-            value = halo[at, x : x + 1, :]
+            value = halo[at * nx + x : at * nx + x + 1, :]
             face[row : row + 1, :] = value if f < FIELDS else layer_of_shared(value, e)
 
 
@@ -334,9 +335,8 @@
 def assemble_kernel(
     base, coefs, strip, y_low, y_high, cells, wide, wide_strip, field, snaps
 ):
-    _, nx, depth = y_low.shape
     _, ex, ey, ez = cells.shape
-    ny = ey - 2 * STEPS
+    nx, ny, depth = ex - 2 * STEPS, ey - 2 * STEPS, ez // 2
     strips = strip.shape[0]
     for f in range(FIELDS + strips):
         source = source_of(base, coefs, strip, f)
@@ -349,9 +349,10 @@
     ):
         for at, (f, first) in enumerate(layers):
             target = place(cells, wide, wide_strip, f)
+            rows = halo[at * nx : (at + 1) * nx, :]
             for d in range(STEPS) if f >= FIELDS else (first,):
                 y = ey - 1 - d if sign < 0 else ny + d
-                value = halo[at] if f < FIELDS else layer_of_shared(halo[at], d)
+                value = rows if f < FIELDS else layer_of_shared(rows, d)
                 for x in range(nx):
                     target[STEPS + x, y : y + 1, 0:depth] = value[x : x + 1]
     for x in range(STEPS, STEPS + nx):
@@ -372,18 +373,18 @@
 
 
 def sides_kernel(x_low, x_high, _cells, _wide, _strip, cells, wide, wide_strip):
-    _, ny, depth = x_low.shape
-    _, ex, ey, _ = cells.shape
-    nx = ex - 2 * STEPS
+    _, ex, ey, ez = cells.shape
+    nx, ny, depth = ex - 2 * STEPS, ey - 2 * STEPS, ez // 2
     strips = wide_strip.shape[0]
     for halo, layers, sign in (
         (x_low, high_layers(strips), -1),
         (x_high, low_layers(0, strips), 1),
     ):
         for at, (f, first) in enumerate(layers):
+            rows = halo[at * ny : (at + 1) * ny, :]
             for d in range(STEPS) if f >= FIELDS else (first,):
                 x = STEPS - 1 - d if sign < 0 else STEPS + nx + d
-                value = halo[at] if f < FIELDS else layer_of_shared(halo[at], d)
+                value = rows if f < FIELDS else layer_of_shared(rows, d)
                 place(cells, wide, wide_strip, f)[x, 0:ny, 0:depth] = value
     for x, fields in side_slabs(nx):
         for f in (*fields, *range(FIELDS, FIELDS + strips)):
@@ -618,16 +619,16 @@
     faces = call(
         functools.partial(faces_kernel, nx, ny),
         [
-            (len(low_layers(1, strips)), nx, depth),
-            (high, nx, depth),
-            (len(low_layers(0, strips)), ny, depth),
-            (high, ny, depth),
+            (len(low_layers(1, strips)) * nx, depth),
+            (high * nx, depth),
+            (len(low_layers(0, strips)) * ny, depth),
+            (high * ny, depth),
         ],
     )(base, coefs, strip)
     y_low, y_high = near(shifted(faces[1], "gy", 1), shifted(faces[0], "gy", -1))
     x_low, x_high = near(shifted(faces[3], "gx", 1), shifted(faces[2], "gx", -1))
     low, high = call(
-        functools.partial(corners_kernel, strips),
+        functools.partial(corners_kernel, nx, strips),
         [corner_shape(1, strips, depth), corner_shape(-1, strips, depth)],
         cost=LONG,
     )(y_low, y_high)

time: 48.7 us -> 48.6 us (level)
  no operation moved by 1% of the time
where the time goes in v6:
time: 48.6 us; the launch traced here: 48.3 us
  starting transfers between devices  17.8 us (37%)
  Pallas kernels  10.3 us (21%)
  blocking collectives  9.99 us (21%)
  waiting for transfers between devices  9.38 us (19%)
  between operations  0.75 us (2%)
    ppermute x6, starting transfers between devices, shifted(): return lax.ppermute(value, axis, pairs)  14.4 us
    all_to_all x1, blocking collectives, shards(): lax.all_to_all(packed, ('gy', 'gz'), split_axis=0, concat_axis=0, tiled=T...  9.99 us
    ppermute x6, waiting for transfers between devices, shifted(): return lax.ppermute(value, axis, pairs)  4.79 us
    all_to_all x1, waiting for transfers between devices, shards(): lax.all_to_all(result, ('gy', 'gz'), split_axis=0, concat_axis=0, tiled=T...  3.35 us
    all_to_all x1, starting transfers between devices, shards(): lax.all_to_all(result, ('gy', 'gz'), split_axis=0, concat_axis=0, tiled=T...  3.33 us
    pallas_call x1, Pallas kernels, shards(): call(steps_kernel, [cells.shape, wide.shape, field.shape, snaps.shape, (b...  2.81 us
    pallas_call x1, Pallas kernels, shards(): call(first_kernel, [(FIELDS - GRID, rows, depth), (8, buckets, slots), *h...  2.16 us
    pallas_call x1, Pallas kernels, shards(): call(assemble_kernel, [(3, ex, ey, ez), (FIELDS - 3, ex, ey, ez), (strips...  1.61 us
  transfers between devices with their start and end apart: 8, of which 4 were waited for; matrix products, arithmetic and copies ran while one was open for 0% of the time, Pallas kernels for 7%

profile of v6, /device:TPU:0, one launch (start us, length us, event | category | flops | bytes accessed | tf_op | source)
XLA Modules:
  0.0 48.3 jit_solution(8174990262050264268)
XLA Ops:
  0.6 1.2 %shard_map.120 = (f32[8,13,128]{2,1,0:T(8,128)S(1)}, f32[4,128,128]{2,1,0:T(8,128)S(1)}, bf16[384,256]{1,0:T(8,128)(2,1)S(1)}) custom-call(f32[3,8,16,128]{3,2,1,0:T(8,128)} %electric.1, s32[8,16,128]{2,1,0:T(8,128)} %classes.1, s32[1,8,128]{2,1,0:T(8,128)} %index.1, f32[2,3,1,8,128]{4,3,2,1,0:T(8,128)} %polar.1, f32[2,1,8,128]{3,2,1,0:T(8,128)} %popul.1, ...), custom_call_target="tpu_custom_call" | custom-call | tf_op jit(solution)/shard_map/pallas_call | solution.py:586
  1.8 10.0 %all_to_all.10.arrived = f32[8,13,128]{2,1,0:T(8,128)S(1)} all-to-all(f32[8,13,128]{2,1,0:T(8,128)S(1)} %get-tuple-element.35), channel_id=1, replica_groups=mesh['gx'=4,'gy'=4,'gz'=2] {'gy','gz'}, dimensions={0} | all-to-all | bytes 106496 | tf_op jit(solution)/shard_map/all_to_all | solution.py:599
  11.8 2.2 %shard_map.121 = (f32[16,128,128]{2,1,0:T(8,128)S(1)}, f32[8,8,128]{2,1,0:T(8,128)S(1)}, bf16[256,1024]{1,0:T(8,128)(2,1)S(1)}, bf16[64,1024]{1,0:T(8,128)(2,1)S(1)}, f32[1,128,128]{2,1,0:T(8,128)S(1)}) custom-call(f32[8,13,128]{2,1,0:T(8,128)S(1)} %all_to_all.10.arrived, f32[4,128,128]{2,1,0:T(8,128)S(1)} %get-tuple-element.34.base, ...), custom_call_target="tpu_custom_call" | custom-call | tf_op jit(solution)/shard_map/pallas_call | solution.py:603
  14.0 0.1 collective-permute-start
  14.0 1.2 %collective-permute-done.strip = f32[1,128,128]{2,1,0:T(8,128)S(1)} collective-permute-done((f32[1,128,128]{2,1,0:T(8,128)S(1)}, f32[1,128,128]{2,1,0:T(8,128)S(1)}, u32[]{:S(2)}, u32[]{:S(2)}) %collective-permute-start) | collective-permute-done | bytes 65568 | tf_op jit(solution)/shard_map/ppermute | solution.py:614
  15.3 0.1 shard_map.122
  15.4 2.5 %collective-permute-start.1 = (f32[336,128]{1,0:T(8,128)S(1)}, f32[336,128]{1,0:T(8,128)S(1)}, u32[]{:S(2)}, u32[]{:S(2)}) collective-permute-start(f32[336,128]{1,0:T(8,128)S(1)} %get-tuple-element.39), channel_id=1, source_target_pairs={{0,2},{2,4},{4,6},{1,3},{3,5},{5,7},{8,10},{10,12},{12,14},{9,11},... | collective-permute-start | bytes 516104 | tf_op jit(solution)/shard_map/ppermute | solution.py:570
  17.9 1.3 %collective-permute-start.2 = (f32[304,128]{1,0:T(8,128)S(1)}, f32[304,128]{1,0:T(8,128)S(1)}, u32[]{:S(2)}, u32[]{:S(2)}) collective-permute-start(f32[304,128]{1,0:T(8,128)S(1)} %get-tuple-element.40), channel_id=1, source_target_pairs={{2,0},{4,2},{6,4},{3,1},{5,3},{7,5},{10,8},{12,10},{14,12},{11,9},... | collective-permute-start | bytes 466952 | tf_op jit(solution)/shard_map/ppermute | solution.py:570
  19.2 1.3 %collective-permute-start.6 = (f32[608,128]{1,0:T(8,128)S(1)}, f32[608,128]{1,0:T(8,128)S(1)}, u32[]{:S(2)}, u32[]{:S(2)}) collective-permute-start(f32[608,128]{1,0:T(8,128)S(1)} %get-tuple-element.44), channel_id=1, source_target_pairs={{8,0},{16,8},{24,16},{9,1},{17,9},{25,17},{10,2},{18,10},{26,18},{... | collective-permute-start | bytes 933896 | tf_op jit(solution)/shard_map/ppermute | solution.py:570
  20.5 4.6 %collective-permute-start.5 = (f32[672,128]{1,0:T(8,128)S(1)}, f32[672,128]{1,0:T(8,128)S(1)}, u32[]{:S(2)}, u32[]{:S(2)}) collective-permute-start(f32[672,128]{1,0:T(8,128)S(1)} %get-tuple-element.43), channel_id=1, source_target_pairs={{0,8},{8,16},{16,24},{1,9},{9,17},{17,25},{2,10},{10,18},{18,26},{... | collective-permute-start | bytes 1032200 | tf_op jit(solution)/shard_map/ppermute | solution.py:570
  25.1 2.0 %collective-permute-done.2.halo_high.y_high = f32[304,128]{1,0:T(8,128)S(1)} collective-permute-done((f32[304,128]{1,0:T(8,128)S(1)}, f32[304,128]{1,0:T(8,128)S(1)}, u32[]{:S(2)}, u32[]{:S(2)}) %collective-permute-start.2) | collective-permute-done | bytes 155680 | tf_op jit(solution)/shard_map/ppermute | solution.py:570
  27.1 0.0 collective-permute-done.1.halo_low.y_low
  27.1 0.1 shard_map.123
  27.2 3.5 %collective-permute-start.3 = (f32[104,128]{1,0:T(8,128)S(1)}, f32[104,128]{1,0:T(8,128)S(1)}, u32[]{:S(2)}, u32[]{:S(2)}) collective-permute-start(f32[104,128]{1,0:T(8,128)S(1)} %get-tuple-element.41), channel_id=1, source_target_pairs={{0,8},{8,16},{16,24},{1,9},{9,17},{17,25},{2,10},{10,18},{18,26},{... | collective-permute-start | bytes 159752 | tf_op jit(solution)/shard_map/ppermute | solution.py:570
  30.7 1.3 %collective-permute-start.4 = (f32[104,128]{1,0:T(8,128)S(1)}, f32[104,128]{1,0:T(8,128)S(1)}, u32[]{:S(2)}, u32[]{:S(2)}) collective-permute-start(f32[104,128]{1,0:T(8,128)S(1)} %get-tuple-element.42), channel_id=1, source_target_pairs={{8,0},{16,8},{24,16},{9,1},{17,9},{25,17},{10,2},{18,10},{26,18},{... | collective-permute-start | bytes 159752 | tf_op jit(solution)/shard_map/ppermute | solution.py:570
  32.0 1.6 %shard_map.124 = (f32[3,16,24,256]{3,2,1,0:T(8,128)S(1)}, f32[17,16,24,256]{3,2,1,0:T(8,128)S(1)}, f32[1,16,24,128]{3,2,1,0:T(8,128)S(1)}, f32[3,16,24,256]{3,2,1,0:T(8,128)S(1)}, f32[9,128,128]{2,1,0:T(8,128)S(1)}) custom-call(f32[4,128,128]{2,1,0:T(8,128)S(1)} %get-tuple-element.34.base, f32[16,128,128]{2,1,0:T(8,128)S(1)} %get-tuple-element.37.coefs, ...), custom_call_target="tpu_custom_call" | custom-call | tf_op jit(solution)/shard_map/pallas_call | solution.py:637
  33.6 0.0 collective-permute-done.6.x_high
  33.6 0.0 collective-permute-done.5.x_low
  33.6 0.3 shard_map.125
  33.9 0.0 collective-permute-done.3.c_low
  33.9 2.8 %collective-permute-done.4.c_high = f32[104,128]{1,0:T(8,128)S(1)} collective-permute-done((f32[104,128]{1,0:T(8,128)S(1)}, f32[104,128]{1,0:T(8,128)S(1)}, u32[]{:S(2)}, u32[]{:S(2)}) %collective-permute-start.4) | collective-permute-done | bytes 53280 | tf_op jit(solution)/shard_map/ppermute | solution.py:570
  36.7 2.8 %shard_map.126 = (f32[3,16,24,256]{3,2,1,0:T(8,128)S(1)}, f32[17,16,24,256]{3,2,1,0:T(8,128)S(1)}, f32[3,16,24,256]{3,2,1,0:T(8,128)S(1)}, f32[9,128,128]{2,1,0:...) custom-call(f32[104,128]{1,0:T(8,128)S(1)} %collective-permute-done., ...), custom_call_target="tpu_custom_call", output_to_operand_aliasing={{0}: (2, {}), {1}: (3, {}), {2}: (4, {}), {3}: (5, {})} | custom-call | tf_op jit(solution)/shard_map/pallas_call | solution.py:657
  39.5 3.3 %all-to-all-start.1 = ((f32[8,8,128]{2,1,0:T(8,128)}), f32[8,8,128]{2,1,0:T(8,128)S(1)}, u32[]{:S(2)}, u32[]{:S(2)}) async-start(f32[8,8,128]{2,1,0:T(8,128)} %get-tuple-element.61), calls=%async_computation.1 | async-start | bytes 65536 | tf_op jit(solution)/shard_map/all_to_all | solution.py:670
  42.9 1.4 %shard_map.127 = (f32[3,8,16,128]{3,2,1,0:T(8,128)}, f32[3,8,16,128]{3,2,1,0:T(8,128)}) custom-call(f32[3,16,24,256]{3,2,1,0:T(8,128)S(1)} %get-tuple-element.56.cells, f32[4,128,128]{2,1,0:T(8,128)S(1)} %get-tuple-element.34.base, f32[3,16,24,256]{3,2,1,0:T(8,128)S(1)} %get-tuple-element.57.field, f32[3,8,128]{2,1,0:T(8,128)S(1)} %get-tuple-element.58.changes, ...), custom_call_target="tpu_custom_call" | custom-call | tf_op jit(solution)/shard_map/pallas_call | solution.py:671
  44.3 3.4 %all-to-all-done.1.home = f32[8,8,128]{2,1,0:T(8,128)S(1)} async-done(((f32[8,8,128]{2,1,0:T(8,128)}), f32[8,8,128]{2,1,0:T(8,128)S(1)}, u32[]{:S(2)}, u32[]{:S(2)}) %all-to-all-start.1) | async-done | bytes 32800 | tf_op jit(solution)/shard_map/all_to_all | solution.py:670
  47.6 0.6 %shard_map.128 = (f32[2,3,1,8,128]{4,3,2,1,0:T(8,128)}, f32[2,1,8,128]{3,2,1,0:T(8,128)}) custom-call(f32[8,8,128]{2,1,0:T(8,128)S(1)} %all-to-all-done.1.home), custom_call_target="tpu_custom_call" | custom-call | tf_op jit(solution)/shard_map/pallas_call | solution.py:674
Async XLA Ops:
  14.0 1.3 %collective-permute-start = (f32[1,128,128]{2,1,0:T(8,128)S(1)}, f32[1,128,128]{2,1,0:T(8,128)S(1)}, u32[]{:S(2)}, u32[]{:S(2)}) collective-permute-start(f32[1,128,128]{2,1,0:T(8,128)S(1)} %get-tuple-element.38), channel_id=1, source_target_pairs={{0,1},{1,0},{2,3},{3,2},{4,5},{5,4},{6,7},{7,6},{8,9},{9,8},{10,11... | collective-permute-start | bytes 196616 | tf_op jit(solution)/shard_map/ppermute | solution.py:614
  15.4 11.7 %collective-permute-start.1 = (f32[336,128]{1,0:T(8,128)S(1)}, f32[336,128]{1,0:T(8,128)S(1)}, u32[]{:S(2)}, u32[]{:S(2)}) collective-permute-start(f32[336,128]{1,0:T(8,128)S(1)} %get-tuple-element.39), channel_id=1, source_target_pairs={{0,2},{2,4},{4,6},{1,3},{3,5},{5,7},{8,10},{10,12},{12,14},{9,11},... | collective-permute-start | bytes 516104 | tf_op jit(solution)/shard_map/ppermute | solution.py:570
  17.9 9.2 %collective-permute-start.2 = (f32[304,128]{1,0:T(8,128)S(1)}, f32[304,128]{1,0:T(8,128)S(1)}, u32[]{:S(2)}, u32[]{:S(2)}) collective-permute-start(f32[304,128]{1,0:T(8,128)S(1)} %get-tuple-element.40), channel_id=1, source_target_pairs={{2,0},{4,2},{6,4},{3,1},{5,3},{7,5},{10,8},{12,10},{14,12},{11,9},... | collective-permute-start | bytes 466952 | tf_op jit(solution)/shard_map/ppermute | solution.py:570
  19.2 14.4 %collective-permute-start.6 = (f32[608,128]{1,0:T(8,128)S(1)}, f32[608,128]{1,0:T(8,128)S(1)}, u32[]{:S(2)}, u32[]{:S(2)}) collective-permute-start(f32[608,128]{1,0:T(8,128)S(1)} %get-tuple-element.44), channel_id=1, source_target_pairs={{8,0},{16,8},{24,16},{9,1},{17,9},{25,17},{10,2},{18,10},{26,18},{... | collective-permute-start | bytes 933896 | tf_op jit(solution)/shard_map/ppermute | solution.py:570
  20.5 13.1 %collective-permute-start.5 = (f32[672,128]{1,0:T(8,128)S(1)}, f32[672,128]{1,0:T(8,128)S(1)}, u32[]{:S(2)}, u32[]{:S(2)}) collective-permute-start(f32[672,128]{1,0:T(8,128)S(1)} %get-tuple-element.43), channel_id=1, source_target_pairs={{0,8},{8,16},{16,24},{1,9},{9,17},{17,25},{2,10},{10,18},{18,26},{... | collective-permute-start | bytes 1032200 | tf_op jit(solution)/shard_map/ppermute | solution.py:570
  27.2 6.7 %collective-permute-start.3 = (f32[104,128]{1,0:T(8,128)S(1)}, f32[104,128]{1,0:T(8,128)S(1)}, u32[]{:S(2)}, u32[]{:S(2)}) collective-permute-start(f32[104,128]{1,0:T(8,128)S(1)} %get-tuple-element.41), channel_id=1, source_target_pairs={{0,8},{8,16},{16,24},{1,9},{9,17},{17,25},{2,10},{10,18},{18,26},{... | collective-permute-start | bytes 159752 | tf_op jit(solution)/shard_map/ppermute | solution.py:570
  30.7 6.0 %collective-permute-start.4 = (f32[104,128]{1,0:T(8,128)S(1)}, f32[104,128]{1,0:T(8,128)S(1)}, u32[]{:S(2)}, u32[]{:S(2)}) collective-permute-start(f32[104,128]{1,0:T(8,128)S(1)} %get-tuple-element.42), channel_id=1, source_target_pairs={{8,0},{16,8},{24,16},{9,1},{17,9},{25,17},{10,2},{18,10},{26,18},{... | collective-permute-start | bytes 159752 | tf_op jit(solution)/shard_map/ppermute | solution.py:570
  39.5 8.1 %all-to-all-start.1 = ((f32[8,8,128]{2,1,0:T(8,128)}), f32[8,8,128]{2,1,0:T(8,128)S(1)}, u32[]{:S(2)}, u32[]{:S(2)}) async-start(f32[8,8,128]{2,1,0:T(8,128)} %get-tuple-element.61), calls=%async_computation.1 | async-start | bytes 65536 | tf_op jit(solution)/shard_map/all_to_all | solution.py:670

commit v7 on v6

--- a/solution.py
+++ b/solution.py
@@ -269,29 +269,42 @@
     out[1] = second[0]
 
 
-def faces_kernel(nx, ny, base, coefs, strip, y_low, y_high, x_low, x_high):
-    strips = strip.shape[0]
-    for face, layers, sign, axis in (
+def face_plans(strips, y_low, y_high, x_low, x_high):
+    return (
         (y_low, low_layers(1, strips), -1, 1),
         (y_high, high_layers(strips), 1, 1),
         (x_low, low_layers(0, strips), -1, 0),
         (x_high, high_layers(strips), 1, 0),
-    ):
-
-        def layer(f, d):
-            source = source_of(base, coefs, strip, f)
-            at = d if sign < 0 else (nx, ny)[axis] - 1 - d
-            if axis == 1:
-                return source[pl.ds(at, nx, stride=ny), :]
-            return source[at * ny : (at + 1) * ny, :]
-
+    )
+
+
+def face_layer(source, nx, ny, axis, sign, d):
+    at = d if sign < 0 else (nx, ny)[axis] - 1 - d
+    if axis == 1:
+        return source[pl.ds(at, nx, stride=ny), :]
+    return source[at * ny : (at + 1) * ny, :]
+
+
+def faces_kernel(nx, ny, strips, base, coefs, *faces):
+    for face, layers, sign, axis in face_plans(strips, *faces):
+        count = nx if axis == 1 else ny
         for at, (f, d) in enumerate(layers):
-            count = nx if axis == 1 else ny
             if f < FIELDS:
-                value = layer(f, d)
-            else:
-                value = share_lanes([layer(f, i) for i in range(STEPS)])
-            face[at * count : (at + 1) * count, :] = value
+                source = source_of(base, coefs, None, f)
+                face[at * count : (at + 1) * count, :] = face_layer(source, nx, ny, axis, sign, d)
+
+
+def face_strips_kernel(nx, ny, strip, *faces):
+    strips = strip.shape[0]
+    for face, layers, sign, axis in face_plans(strips, *faces[4:]):
+        count = nx if axis == 1 else ny
+        for at, (f, _) in enumerate(layers):
+            if f >= FIELDS:
+                source = strip.at[f - FIELDS]
+                value = share_lanes(
+                    [face_layer(source, nx, ny, axis, sign, d) for d in range(STEPS)]
+                )
+                face[at * count : (at + 1) * count, :] = value
 
 
 def corners_kernel(nx, strips, halo_low, halo_high, low, high):
@@ -610,21 +623,24 @@
             ],
         )(arrived, base, left)
     )
+    high = len(high_layers(strips))
+    shapes = [
+        (len(low_layers(1, strips)) * nx, depth),
+        (high * nx, depth),
+        (len(low_layers(0, strips)) * ny, depth),
+        (high * ny, depth),
+    ]
+    faces = near(*call(functools.partial(faces_kernel, nx, ny, strips), shapes)(base, coefs))
     if strips == 1:
         (strip,) = near(lax.ppermute(strip[0], "gz", [(0, 1), (1, 0)]))
     else:
         strip = near(shifted(strip[0], "gz", 1), shifted(strip[1], "gz", -1))
         (strip,) = near(*call(join_kernel, [(strips, rows, depth)])(*strip))
-    high = len(high_layers(strips))
     faces = call(
-        functools.partial(faces_kernel, nx, ny),
-        [
-            (len(low_layers(1, strips)) * nx, depth),
-            (high * nx, depth),
-            (len(low_layers(0, strips)) * ny, depth),
-            (high * ny, depth),
-        ],
-    )(base, coefs, strip)
+        functools.partial(face_strips_kernel, nx, ny),
+        shapes,
+        aliases={1: 0, 2: 1, 3: 2, 4: 3},
+    )(strip, *faces)
     y_low, y_high = near(shifted(faces[1], "gy", 1), shifted(faces[0], "gy", -1))
     x_low, x_high = near(shifted(faces[3], "gx", 1), shifted(faces[2], "gx", -1))
     low, high = call(

time: 48.6 us -> 48.6 us (level)
  no operation moved by 1% of the time
where the time goes in v7:
time: 48.6 us; the launch traced here: 48.2 us
  starting transfers between devices  17.8 us (37%)
  Pallas kernels  10.4 us (21%)
  blocking collectives  9.99 us (21%)
  waiting for transfers between devices  9.23 us (19%)
  between operations  0.76 us (2%)
    ppermute x6, starting transfers between devices, shifted(): return lax.ppermute(value, axis, pairs)  14.4 us
    all_to_all x1, blocking collectives, shards(): lax.all_to_all(packed, ('gy', 'gz'), split_axis=0, concat_axis=0, tiled=T...  9.99 us
    ppermute x6, waiting for transfers between devices, shifted(): return lax.ppermute(value, axis, pairs)  4.79 us
    all_to_all x1, waiting for transfers between devices, shards(): lax.all_to_all(result, ('gy', 'gz'), split_axis=0, concat_axis=0, tiled=T...  3.35 us
    all_to_all x1, starting transfers between devices, shards(): lax.all_to_all(result, ('gy', 'gz'), split_axis=0, concat_axis=0, tiled=T...  3.33 us
    pallas_call x1, Pallas kernels, shards(): call(steps_kernel, [cells.shape, wide.shape, field.shape, snaps.shape, (b...  2.83 us
    pallas_call x1, Pallas kernels, shards(): call(first_kernel, [(FIELDS - GRID, rows, depth), (8, buckets, slots), *h...  2.16 us
    pallas_call x1, Pallas kernels, shards(): call(assemble_kernel, [(3, ex, ey, ez), (FIELDS - 3, ex, ey, ez), (strips...  1.61 us
  transfers between devices with their start and end apart: 8, of which 4 were waited for; matrix products, arithmetic and copies ran while one was open for 0% of the time, Pallas kernels for 7%

profile of v7, /device:TPU:0, one launch (start us, length us, event | category | flops | bytes accessed | tf_op | source)
XLA Modules:
  0.0 48.2 jit_solution(18215755128252123228)
XLA Ops:
  0.6 1.2 %shard_map.120 = (f32[8,13,128]{2,1,0:T(8,128)S(1)}, f32[4,128,128]{2,1,0:T(8,128)S(1)}, bf16[384,256]{1,0:T(8,128)(2,1)S(1)}) custom-call(f32[3,8,16,128]{3,2,1,0:T(8,128)} %electric.1, s32[8,16,128]{2,1,0:T(8,128)} %classes.1, s32[1,8,128]{2,1,0:T(8,128)} %index.1, f32[2,3,1,8,128]{4,3,2,1,0:T(8,128)} %polar.1, f32[2,1,8,128]{3,2,1,0:T(8,128)} %popul.1, ...), custom_call_target="tpu_custom_call" | custom-call | tf_op jit(solution)/shard_map/pallas_call | solution.py:599
  1.8 10.0 %all_to_all.10.arrived = f32[8,13,128]{2,1,0:T(8,128)S(1)} all-to-all(f32[8,13,128]{2,1,0:T(8,128)S(1)} %get-tuple-element.38), channel_id=1, replica_groups=mesh['gx'=4,'gy'=4,'gz'=2] {'gy','gz'}, dimensions={0} | all-to-all | bytes 106496 | tf_op jit(solution)/shard_map/all_to_all | solution.py:612
  11.8 2.2 %shard_map.121 = (f32[16,128,128]{2,1,0:T(8,128)S(1)}, f32[8,8,128]{2,1,0:T(8,128)S(1)}, bf16[256,1024]{1,0:T(8,128)(2,1)S(1)}, bf16[64,1024]{1,0:T(8,128)(2,1)S(1)}, f32[1,128,128]{2,1,0:T(8,128)S(1)}) custom-call(f32[8,13,128]{2,1,0:T(8,128)S(1)} %all_to_all.10.arrived, f32[4,128,128]{2,1,0:T(8,128)S(1)} %get-tuple-element.39.base, ...), custom_call_target="tpu_custom_call" | custom-call | tf_op jit(solution)/shard_map/pallas_call | solution.py:616
  14.0 0.1 collective-permute-start
  14.0 0.1 shard_map.122
  14.2 1.1 %collective-permute-done.strip = f32[1,128,128]{2,1,0:T(8,128)S(1)} collective-permute-done((f32[1,128,128]{2,1,0:T(8,128)S(1)}, f32[1,128,128]{2,1,0:T(8,128)S(1)}, u32[]{:S(2)}, u32[]{:S(2)}) %collective-permute-start) | collective-permute-done | bytes 65568 | tf_op jit(solution)/shard_map/ppermute | solution.py:635
  15.3 0.1 shard_map.123
  15.4 2.5 %collective-permute-start.1 = (f32[336,128]{1,0:T(8,128)S(1)}, f32[336,128]{1,0:T(8,128)S(1)}, u32[]{:S(2)}, u32[]{:S(2)}) collective-permute-start(f32[336,128]{1,0:T(8,128)S(1)} %get-tuple-element.47), channel_id=1, source_target_pairs={{0,2},{2,4},{4,6},{1,3},{3,5},{5,7},{8,10},{10,12},{12,14},{9,11},... | collective-permute-start | bytes 516104 | tf_op jit(solution)/shard_map/ppermute | solution.py:583
  17.8 1.3 %collective-permute-start.2 = (f32[304,128]{1,0:T(8,128)S(1)}, f32[304,128]{1,0:T(8,128)S(1)}, u32[]{:S(2)}, u32[]{:S(2)}) collective-permute-start(f32[304,128]{1,0:T(8,128)S(1)} %get-tuple-element.48), channel_id=1, source_target_pairs={{2,0},{4,2},{6,4},{3,1},{5,3},{7,5},{10,8},{12,10},{14,12},{11,9},... | collective-permute-start | bytes 466952 | tf_op jit(solution)/shard_map/ppermute | solution.py:583
  19.1 1.3 %collective-permute-start.6 = (f32[608,128]{1,0:T(8,128)S(1)}, f32[608,128]{1,0:T(8,128)S(1)}, u32[]{:S(2)}, u32[]{:S(2)}) collective-permute-start(f32[608,128]{1,0:T(8,128)S(1)} %get-tuple-element.52), channel_id=1, source_target_pairs={{8,0},{16,8},{24,16},{9,1},{17,9},{25,17},{10,2},{18,10},{26,18},{... | collective-permute-start | bytes 933896 | tf_op jit(solution)/shard_map/ppermute | solution.py:583
  20.4 4.6 %collective-permute-start.5 = (f32[672,128]{1,0:T(8,128)S(1)}, f32[672,128]{1,0:T(8,128)S(1)}, u32[]{:S(2)}, u32[]{:S(2)}) collective-permute-start(f32[672,128]{1,0:T(8,128)S(1)} %get-tuple-element.51), channel_id=1, source_target_pairs={{0,8},{8,16},{16,24},{1,9},{9,17},{17,25},{2,10},{10,18},{18,26},{... | collective-permute-start | bytes 1032200 | tf_op jit(solution)/shard_map/ppermute | solution.py:583
  25.0 2.0 %collective-permute-done.2.halo_high.y_high = f32[304,128]{1,0:T(8,128)S(1)} collective-permute-done((f32[304,128]{1,0:T(8,128)S(1)}, f32[304,128]{1,0:T(8,128)S(1)}, u32[]{:S(2)}, u32[]{:S(2)}) %collective-permute-start.2) | collective-permute-done | bytes 155680 | tf_op jit(solution)/shard_map/ppermute | solution.py:583
  27.0 0.0 collective-permute-done.1.halo_low.y_low
  27.0 0.1 shard_map.124
  27.1 3.5 %collective-permute-start.3 = (f32[104,128]{1,0:T(8,128)S(1)}, f32[104,128]{1,0:T(8,128)S(1)}, u32[]{:S(2)}, u32[]{:S(2)}) collective-permute-start(f32[104,128]{1,0:T(8,128)S(1)} %get-tuple-element.49), channel_id=1, source_target_pairs={{0,8},{8,16},{16,24},{1,9},{9,17},{17,25},{2,10},{10,18},{18,26},{... | collective-permute-start | bytes 159752 | tf_op jit(solution)/shard_map/ppermute | solution.py:583
  30.6 1.3 %collective-permute-start.4 = (f32[104,128]{1,0:T(8,128)S(1)}, f32[104,128]{1,0:T(8,128)S(1)}, u32[]{:S(2)}, u32[]{:S(2)}) collective-permute-start(f32[104,128]{1,0:T(8,128)S(1)} %get-tuple-element.50), channel_id=1, source_target_pairs={{8,0},{16,8},{24,16},{9,1},{17,9},{25,17},{10,2},{18,10},{26,18},{... | collective-permute-start | bytes 159752 | tf_op jit(solution)/shard_map/ppermute | solution.py:583
  31.9 1.6 %shard_map.125 = (f32[3,16,24,256]{3,2,1,0:T(8,128)S(1)}, f32[17,16,24,256]{3,2,1,0:T(8,128)S(1)}, f32[1,16,24,128]{3,2,1,0:T(8,128)S(1)}, f32[3,16,24,256]{3,2,1,0:T(8,128)S(1)}, f32[9,128,128]{2,1,0:T(8,128)S(1)}) custom-call(f32[4,128,128]{2,1,0:T(8,128)S(1)} %get-tuple-element.39.base, f32[16,128,128]{2,1,0:T(8,128)S(1)} %get-tuple-element.42.coefs, ...), custom_call_target="tpu_custom_call" | custom-call | tf_op jit(solution)/shard_map/pallas_call | solution.py:653
  33.5 0.0 collective-permute-done.6.x_high
  33.5 0.0 collective-permute-done.5.x_low
  33.6 0.3 shard_map.126
  33.8 0.0 collective-permute-done.3.c_low
  33.9 2.8 %collective-permute-done.4.c_high = f32[104,128]{1,0:T(8,128)S(1)} collective-permute-done((f32[104,128]{1,0:T(8,128)S(1)}, f32[104,128]{1,0:T(8,128)S(1)}, u32[]{:S(2)}, u32[]{:S(2)}) %collective-permute-start.4) | collective-permute-done | bytes 53280 | tf_op jit(solution)/shard_map/ppermute | solution.py:583
  36.6 2.8 %shard_map.127 = (f32[3,16,24,256]{3,2,1,0:T(8,128)S(1)}, f32[17,16,24,256]{3,2,1,0:T(8,128)S(1)}, f32[3,16,24,256]{3,2,1,0:T(8,128)S(1)}, f32[9,128,128]{2,1,0:...) custom-call(f32[104,128]{1,0:T(8,128)S(1)} %collective-permute-done., ...), custom_call_target="tpu_custom_call", output_to_operand_aliasing={{0}: (2, {}), {1}: (3, {}), {2}: (4, {}), {3}: (5, {})} | custom-call | tf_op jit(solution)/shard_map/pallas_call | solution.py:673
  39.5 3.3 %all-to-all-start.1 = ((f32[8,8,128]{2,1,0:T(8,128)}), f32[8,8,128]{2,1,0:T(8,128)S(1)}, u32[]{:S(2)}, u32[]{:S(2)}) async-start(f32[8,8,128]{2,1,0:T(8,128)} %get-tuple-element.69), calls=%async_computation.1 | async-start | bytes 65536 | tf_op jit(solution)/shard_map/all_to_all | solution.py:686
  42.8 1.4 %shard_map.128 = (f32[3,8,16,128]{3,2,1,0:T(8,128)}, f32[3,8,16,128]{3,2,1,0:T(8,128)}) custom-call(f32[3,16,24,256]{3,2,1,0:T(8,128)S(1)} %get-tuple-element.64.cells, f32[4,128,128]{2,1,0:T(8,128)S(1)} %get-tuple-element.39.base, f32[3,16,24,256]{3,2,1,0:T(8,128)S(1)} %get-tuple-element.65.field, f32[3,8,128]{2,1,0:T(8,128)S(1)} %get-tuple-element.66.changes, ...), custom_call_target="tpu_custom_call" | custom-call | tf_op jit(solution)/shard_map/pallas_call | solution.py:687
  44.2 3.4 %all-to-all-done.1.home = f32[8,8,128]{2,1,0:T(8,128)S(1)} async-done(((f32[8,8,128]{2,1,0:T(8,128)}), f32[8,8,128]{2,1,0:T(8,128)S(1)}, u32[]{:S(2)}, u32[]{:S(2)}) %all-to-all-start.1) | async-done | bytes 32800 | tf_op jit(solution)/shard_map/all_to_all | solution.py:686
  47.6 0.6 %shard_map.129 = (f32[2,3,1,8,128]{4,3,2,1,0:T(8,128)}, f32[2,1,8,128]{3,2,1,0:T(8,128)}) custom-call(f32[8,8,128]{2,1,0:T(8,128)S(1)} %all-to-all-done.1.home), custom_call_target="tpu_custom_call" | custom-call | tf_op jit(solution)/shard_map/pallas_call | solution.py:690
Async XLA Ops:
  14.0 1.3 %collective-permute-start = (f32[1,128,128]{2,1,0:T(8,128)S(1)}, f32[1,128,128]{2,1,0:T(8,128)S(1)}, u32[]{:S(2)}, u32[]{:S(2)}) collective-permute-start(f32[1,128,128]{2,1,0:T(8,128)S(1)} %get-tuple-element.41), channel_id=1, source_target_pairs={{0,1},{1,0},{2,3},{3,2},{4,5},{5,4},{6,7},{7,6},{8,9},{9,8},{10,11... | collective-permute-start | bytes 196616 | tf_op jit(solution)/shard_map/ppermute | solution.py:635
  15.4 11.7 %collective-permute-start.1 = (f32[336,128]{1,0:T(8,128)S(1)}, f32[336,128]{1,0:T(8,128)S(1)}, u32[]{:S(2)}, u32[]{:S(2)}) collective-permute-start(f32[336,128]{1,0:T(8,128)S(1)} %get-tuple-element.47), channel_id=1, source_target_pairs={{0,2},{2,4},{4,6},{1,3},{3,5},{5,7},{8,10},{10,12},{12,14},{9,11},... | collective-permute-start | bytes 516104 | tf_op jit(solution)/shard_map/ppermute | solution.py:583
  17.8 9.2 %collective-permute-start.2 = (f32[304,128]{1,0:T(8,128)S(1)}, f32[304,128]{1,0:T(8,128)S(1)}, u32[]{:S(2)}, u32[]{:S(2)}) collective-permute-start(f32[304,128]{1,0:T(8,128)S(1)} %get-tuple-element.48), channel_id=1, source_target_pairs={{2,0},{4,2},{6,4},{3,1},{5,3},{7,5},{10,8},{12,10},{14,12},{11,9},... | collective-permute-start | bytes 466952 | tf_op jit(solution)/shard_map/ppermute | solution.py:583
  19.1 14.4 %collective-permute-start.6 = (f32[608,128]{1,0:T(8,128)S(1)}, f32[608,128]{1,0:T(8,128)S(1)}, u32[]{:S(2)}, u32[]{:S(2)}) collective-permute-start(f32[608,128]{1,0:T(8,128)S(1)} %get-tuple-element.52), channel_id=1, source_target_pairs={{8,0},{16,8},{24,16},{9,1},{17,9},{25,17},{10,2},{18,10},{26,18},{... | collective-permute-start | bytes 933896 | tf_op jit(solution)/shard_map/ppermute | solution.py:583
  20.4 13.1 %collective-permute-start.5 = (f32[672,128]{1,0:T(8,128)S(1)}, f32[672,128]{1,0:T(8,128)S(1)}, u32[]{:S(2)}, u32[]{:S(2)}) collective-permute-start(f32[672,128]{1,0:T(8,128)S(1)} %get-tuple-element.51), channel_id=1, source_target_pairs={{0,8},{8,16},{16,24},{1,9},{9,17},{17,25},{2,10},{10,18},{18,26},{... | collective-permute-start | bytes 1032200 | tf_op jit(solution)/shard_map/ppermute | solution.py:583
  27.1 6.7 %collective-permute-start.3 = (f32[104,128]{1,0:T(8,128)S(1)}, f32[104,128]{1,0:T(8,128)S(1)}, u32[]{:S(2)}, u32[]{:S(2)}) collective-permute-start(f32[104,128]{1,0:T(8,128)S(1)} %get-tuple-element.49), channel_id=1, source_target_pairs={{0,8},{8,16},{16,24},{1,9},{9,17},{17,25},{2,10},{10,18},{18,26},{... | collective-permute-start | bytes 159752 | tf_op jit(solution)/shard_map/ppermute | solution.py:583
  30.6 6.0 %collective-permute-start.4 = (f32[104,128]{1,0:T(8,128)S(1)}, f32[104,128]{1,0:T(8,128)S(1)}, u32[]{:S(2)}, u32[]{:S(2)}) collective-permute-start(f32[104,128]{1,0:T(8,128)S(1)} %get-tuple-element.50), channel_id=1, source_target_pairs={{8,0},{16,8},{24,16},{9,1},{17,9},{25,17},{10,2},{18,10},{26,18},{... | collective-permute-start | bytes 159752 | tf_op jit(solution)/shard_map/ppermute | solution.py:583
  39.5 8.1 %all-to-all-start.1 = ((f32[8,8,128]{2,1,0:T(8,128)}), f32[8,8,128]{2,1,0:T(8,128)S(1)}, u32[]{:S(2)}, u32[]{:S(2)}) async-start(f32[8,8,128]{2,1,0:T(8,128)} %get-tuple-element.69), calls=%async_computation.1 | async-start | bytes 65536 | tf_op jit(solution)/shard_map/all_to_all | solution.py:686

commit v8 on v7

--- a/solution.py
+++ b/solution.py
@@ -488,7 +488,7 @@
 
 def steps_kernel(
     c_low, c_high, _cells, _wide, _field, _snaps, wide_strip, row_hot, depth_hot,
-    arrived, states, cells, wide, field, snaps, result, changes,
+    arrived, states, cells, wide, field, snaps, result, changes, edges,
 ):
     _, ex, ey, ez = wide.shape
     nx, ny, depth = ex - 2 * STEPS, ey - 2 * STEPS, ez // 2
@@ -522,10 +522,11 @@
             current = advanced
         if step < STEPS:
             done = range(STEPS + step, STEPS + nx - step)
-            for x in range(step - 1, ex - step):
+            spare = step == STEPS - 1
+            for x in range(step - 1 + spare, ex - step - spare):
                 if x not in done and x + 1 not in done:
                     advance_magnetic(cells, field, inside, step, x)
-                if x not in done and x >= step:
+                if x not in done and x >= step + spare:
                     advance_electric(cells, wide, field, snaps, step, x)
     for c in range(3):
         result[:, c, :] = current[c]
@@ -534,14 +535,24 @@
     result[:, 7, :] = pumped
     for c in range(3):
         changes[c] = change[c]
-
-
-def last_kernel(cells, base, field, changes, row_hot, depth_hot, electric, magnetic):
+    for i, x in enumerate((STEPS - 1, STEPS + nx)):
+        for c in range(3):
+            edges[i, c] = wide[8 + c, x] + wide[12, x] * cells[c, x]
+        edges[i, 3] = wide[0, x]
+
+
+def last_kernel(cells, base, field, changes, edges, row_hot, depth_hot, electric, magnetic):
     _, nx, ny, depth = electric.shape
     rows = nx * ny
     ey, ez = cells.shape[2:]
     sources = scatter_cells([changes[c] for c in range(3)], row_hot, depth_hot, rows)
     inside = inside_mask(ey, ez)
+    for x in (STEPS - 2, STEPS + nx):
+        advance_magnetic(cells, field, inside, STEPS - 1, x)
+    for i, x in enumerate((STEPS - 1, STEPS + nx)):
+        curl = backward_curl(field, x)
+        for c in range(3):
+            cells[c, x] = cells[c, x] + edges[i, 3] * (curl[c] + edges[i, c])
     advance_magnetic(cells, field, inside, STEPS, STEPS - 1)
     for x in range(STEPS, STEPS + nx):
         advance_magnetic(cells, field, inside, STEPS, x)
@@ -669,7 +680,7 @@
             aliases={2: 0, 3: 1, 4: 2},
         )(x_low, x_high, cells, wide, wide_strip)
     )
-    cells, _, field, _, result, changes = near(
+    cells, _, field, _, result, changes, edges = near(
         *call(
             steps_kernel,
             [
@@ -679,13 +690,14 @@
                 snaps.shape,
                 (buckets, 8, slots),
                 (3, buckets, slots),
+                (2, 4, ey, ez),
             ],
             aliases={2: 0, 3: 1, 4: 2, 5: 3},
         )(c_low, c_high, cells, wide, field, snaps, wide_strip, row_hot, depth_hot, arrived, states)
     )
     home = lax.all_to_all(result, ("gy", "gz"), split_axis=0, concat_axis=0, tiled=True)
     electric, magnetic = call(last_kernel, [], [electric.shape, electric.shape])(
-        cells, base, field, changes, row_hot, depth_hot
+        cells, base, field, changes, edges, row_hot, depth_hot
     )
     polar_out, popul_out = call(unpack_kernel, [], [polarization.shape, populations.shape])(
         *near(home)

time: 48.6 us -> 48.4 us (level)
  transfers between devices with their start and end apart: 8 -> 8, of which waited for: 4 -> 4; matrix products, arithmetic and copies ran while one was open for 0% -> 0% of each run, Pallas kernels for 7% -> 8%
where the time goes in v8:
time: 48.4 us; the launch traced here: 48 us
  starting transfers between devices  17.8 us (37%)
  Pallas kernels  10.4 us (21%)
  blocking collectives  9.99 us (21%)
  waiting for transfers between devices  9.11 us (19%)
  between operations  0.76 us (2%)
    ppermute x6, starting transfers between devices, shifted(): return lax.ppermute(value, axis, pairs)  14.4 us
    all_to_all x1, blocking collectives, shards(): lax.all_to_all(packed, ('gy', 'gz'), split_axis=0, concat_axis=0, tiled=T...  9.99 us
    ppermute x6, waiting for transfers between devices, shifted(): return lax.ppermute(value, axis, pairs)  4.79 us
    all_to_all x1, starting transfers between devices, shards(): lax.all_to_all(result, ('gy', 'gz'), split_axis=0, concat_axis=0, tiled=T...  3.33 us
    all_to_all x1, waiting for transfers between devices, shards(): lax.all_to_all(result, ('gy', 'gz'), split_axis=0, concat_axis=0, tiled=T...  3.23 us
    pallas_call x1, Pallas kernels, shards(): call(steps_kernel, [cells.shape, wide.shape, field.shape, snaps.shape, (b...  2.66 us
    pallas_call x1, Pallas kernels, shards(): call(first_kernel, [(FIELDS - GRID, rows, depth), (8, buckets, slots), *h...  2.16 us
    pallas_call x1, Pallas kernels, shards(): call(assemble_kernel, [(3, ex, ey, ez), (FIELDS - 3, ex, ey, ez), (strips...  1.61 us
  transfers between devices with their start and end apart: 8, of which 4 were waited for; matrix products, arithmetic and copies ran while one was open for 0% of the time, Pallas kernels for 8%

profile of v8, /device:TPU:0, one launch (start us, length us, event | category | flops | bytes accessed | tf_op | source)
XLA Modules:
  0.0 48.0 jit_solution(7570675497521900172)
XLA Ops:
  0.6 1.2 %shard_map.120 = (f32[8,13,128]{2,1,0:T(8,128)S(1)}, f32[4,128,128]{2,1,0:T(8,128)S(1)}, bf16[384,256]{1,0:T(8,128)(2,1)S(1)}) custom-call(f32[3,8,16,128]{3,2,1,0:T(8,128)} %electric.1, s32[8,16,128]{2,1,0:T(8,128)} %classes.1, s32[1,8,128]{2,1,0:T(8,128)} %index.1, f32[2,3,1,8,128]{4,3,2,1,0:T(8,128)} %polar.1, f32[2,1,8,128]{3,2,1,0:T(8,128)} %popul.1, ...), custom_call_target="tpu_custom_call" | custom-call | tf_op jit(solution)/shard_map/pallas_call | solution.py:610
  1.8 10.0 %all_to_all.10.arrived = f32[8,13,128]{2,1,0:T(8,128)S(1)} all-to-all(f32[8,13,128]{2,1,0:T(8,128)S(1)} %get-tuple-element.39), channel_id=1, replica_groups=mesh['gx'=4,'gy'=4,'gz'=2] {'gy','gz'}, dimensions={0} | all-to-all | bytes 106496 | tf_op jit(solution)/shard_map/all_to_all | solution.py:623
  11.8 2.2 %shard_map.121 = (f32[16,128,128]{2,1,0:T(8,128)S(1)}, f32[8,8,128]{2,1,0:T(8,128)S(1)}, bf16[256,1024]{1,0:T(8,128)(2,1)S(1)}, bf16[64,1024]{1,0:T(8,128)(2,1)S(1)}, f32[1,128,128]{2,1,0:T(8,128)S(1)}) custom-call(f32[8,13,128]{2,1,0:T(8,128)S(1)} %all_to_all.10.arrived, f32[4,128,128]{2,1,0:T(8,128)S(1)} %get-tuple-element.40.base, ...), custom_call_target="tpu_custom_call" | custom-call | tf_op jit(solution)/shard_map/pallas_call | solution.py:627
  14.0 0.1 collective-permute-start
  14.0 0.1 shard_map.122
  14.2 1.1 %collective-permute-done.strip = f32[1,128,128]{2,1,0:T(8,128)S(1)} collective-permute-done((f32[1,128,128]{2,1,0:T(8,128)S(1)}, f32[1,128,128]{2,1,0:T(8,128)S(1)}, u32[]{:S(2)}, u32[]{:S(2)}) %collective-permute-start) | collective-permute-done | bytes 65568 | tf_op jit(solution)/shard_map/ppermute | solution.py:646
  15.3 0.1 shard_map.123
  15.4 2.5 %collective-permute-start.1 = (f32[336,128]{1,0:T(8,128)S(1)}, f32[336,128]{1,0:T(8,128)S(1)}, u32[]{:S(2)}, u32[]{:S(2)}) collective-permute-start(f32[336,128]{1,0:T(8,128)S(1)} %get-tuple-element.48), channel_id=1, source_target_pairs={{0,2},{2,4},{4,6},{1,3},{3,5},{5,7},{8,10},{10,12},{12,14},{9,11},... | collective-permute-start | bytes 516104 | tf_op jit(solution)/shard_map/ppermute | solution.py:594
  17.8 1.3 %collective-permute-start.2 = (f32[304,128]{1,0:T(8,128)S(1)}, f32[304,128]{1,0:T(8,128)S(1)}, u32[]{:S(2)}, u32[]{:S(2)}) collective-permute-start(f32[304,128]{1,0:T(8,128)S(1)} %get-tuple-element.49), channel_id=1, source_target_pairs={{2,0},{4,2},{6,4},{3,1},{5,3},{7,5},{10,8},{12,10},{14,12},{11,9},... | collective-permute-start | bytes 466952 | tf_op jit(solution)/shard_map/ppermute | solution.py:594
  19.1 1.3 %collective-permute-start.6 = (f32[608,128]{1,0:T(8,128)S(1)}, f32[608,128]{1,0:T(8,128)S(1)}, u32[]{:S(2)}, u32[]{:S(2)}) collective-permute-start(f32[608,128]{1,0:T(8,128)S(1)} %get-tuple-element.53), channel_id=1, source_target_pairs={{8,0},{16,8},{24,16},{9,1},{17,9},{25,17},{10,2},{18,10},{26,18},{... | collective-permute-start | bytes 933896 | tf_op jit(solution)/shard_map/ppermute | solution.py:594
  20.4 4.6 %collective-permute-start.5 = (f32[672,128]{1,0:T(8,128)S(1)}, f32[672,128]{1,0:T(8,128)S(1)}, u32[]{:S(2)}, u32[]{:S(2)}) collective-permute-start(f32[672,128]{1,0:T(8,128)S(1)} %get-tuple-element.52), channel_id=1, source_target_pairs={{0,8},{8,16},{16,24},{1,9},{9,17},{17,25},{2,10},{10,18},{18,26},{... | collective-permute-start | bytes 1032200 | tf_op jit(solution)/shard_map/ppermute | solution.py:594
  25.0 2.0 %collective-permute-done.2.halo_high.y_high = f32[304,128]{1,0:T(8,128)S(1)} collective-permute-done((f32[304,128]{1,0:T(8,128)S(1)}, f32[304,128]{1,0:T(8,128)S(1)}, u32[]{:S(2)}, u32[]{:S(2)}) %collective-permute-start.2) | collective-permute-done | bytes 155680 | tf_op jit(solution)/shard_map/ppermute | solution.py:594
  27.0 0.0 collective-permute-done.1.halo_low.y_low
  27.0 0.1 shard_map.124
  27.1 3.5 %collective-permute-start.3 = (f32[104,128]{1,0:T(8,128)S(1)}, f32[104,128]{1,0:T(8,128)S(1)}, u32[]{:S(2)}, u32[]{:S(2)}) collective-permute-start(f32[104,128]{1,0:T(8,128)S(1)} %get-tuple-element.50), channel_id=1, source_target_pairs={{0,8},{8,16},{16,24},{1,9},{9,17},{17,25},{2,10},{10,18},{18,26},{... | collective-permute-start | bytes 159752 | tf_op jit(solution)/shard_map/ppermute | solution.py:594
  30.6 1.3 %collective-permute-start.4 = (f32[104,128]{1,0:T(8,128)S(1)}, f32[104,128]{1,0:T(8,128)S(1)}, u32[]{:S(2)}, u32[]{:S(2)}) collective-permute-start(f32[104,128]{1,0:T(8,128)S(1)} %get-tuple-element.51), channel_id=1, source_target_pairs={{8,0},{16,8},{24,16},{9,1},{17,9},{25,17},{10,2},{18,10},{26,18},{... | collective-permute-start | bytes 159752 | tf_op jit(solution)/shard_map/ppermute | solution.py:594
  31.9 1.6 %shard_map.125 = (f32[3,16,24,256]{3,2,1,0:T(8,128)S(1)}, f32[17,16,24,256]{3,2,1,0:T(8,128)S(1)}, f32[1,16,24,128]{3,2,1,0:T(8,128)S(1)}, f32[3,16,24,256]{3,2,1,0:T(8,128)S(1)}, f32[9,128,128]{2,1,0:T(8,128)S(1)}) custom-call(f32[4,128,128]{2,1,0:T(8,128)S(1)} %get-tuple-element.40.base, f32[16,128,128]{2,1,0:T(8,128)S(1)} %get-tuple-element.43.coefs, ...), custom_call_target="tpu_custom_call" | custom-call | tf_op jit(solution)/shard_map/pallas_call | solution.py:664
  33.5 0.0 collective-permute-done.6.x_high
  33.5 0.0 collective-permute-done.5.x_low
  33.6 0.3 shard_map.126
  33.8 0.0 collective-permute-done.3.c_low
  33.9 2.8 %collective-permute-done.4.c_high = f32[104,128]{1,0:T(8,128)S(1)} collective-permute-done((f32[104,128]{1,0:T(8,128)S(1)}, f32[104,128]{1,0:T(8,128)S(1)}, u32[]{:S(2)}, u32[]{:S(2)}) %collective-permute-start.4) | collective-permute-done | bytes 53280 | tf_op jit(solution)/shard_map/ppermute | solution.py:594
  36.6 2.7 %shard_map.127 = (f32[3,16,24,256]{3,2,1,0:T(8,128)S(1)}, f32[17,16,24,256]{3,2,1,0:T(8,128)S(1)}, f32[3,16,24,256]{3,2,1,0:T(8,128)S(1)}, f32[9,128,128]{2,1,0:...) custom-call(f32[104,128]{1,0:T(8,128)S(1)} %collective-permute-done., ...), custom_call_target="tpu_custom_call", output_to_operand_aliasing={{0}: (2, {}), {1}: (3, {}), {2}: (4, {}), {3}: (5, {})} | custom-call | tf_op jit(solution)/shard_map/pallas_call | solution.py:684
  39.3 3.3 %all-to-all-start.1 = ((f32[8,8,128]{2,1,0:T(8,128)}), f32[8,8,128]{2,1,0:T(8,128)S(1)}, u32[]{:S(2)}, u32[]{:S(2)}) async-start(f32[8,8,128]{2,1,0:T(8,128)} %get-tuple-element.71), calls=%async_computation.1 | async-start | bytes 65536 | tf_op jit(solution)/shard_map/all_to_all | solution.py:698
  42.6 1.5 %shard_map.128 = (f32[3,8,16,128]{3,2,1,0:T(8,128)}, f32[3,8,16,128]{3,2,1,0:T(8,128)}) custom-call(f32[3,16,24,256]{3,2,1,0:T(8,128)S(1)} %get-tuple-element.65.cells, f32[4,128,128]{2,1,0:T(8,128)S(1)} %get-tuple-element.40.base, f32[3,16,24,256]{3,2,1,0:T(8,128)S(1)} %get-tuple-element.66.field, f32[3,8,128]{2,1,0:T(8,128)S(1)} %get-tuple-element.67.changes, ...), custom_call_target="tpu_custom_call" | custom-call | tf_op jit(solution)/shard_map/pallas_call | solution.py:699
  44.2 3.2 %all-to-all-done.1.home = f32[8,8,128]{2,1,0:T(8,128)S(1)} async-done(((f32[8,8,128]{2,1,0:T(8,128)}), f32[8,8,128]{2,1,0:T(8,128)S(1)}, u32[]{:S(2)}, u32[]{:S(2)}) %all-to-all-start.1) | async-done | bytes 32800 | tf_op jit(solution)/shard_map/all_to_all | solution.py:698
  47.4 0.6 %shard_map.129 = (f32[2,3,1,8,128]{4,3,2,1,0:T(8,128)}, f32[2,1,8,128]{3,2,1,0:T(8,128)}) custom-call(f32[8,8,128]{2,1,0:T(8,128)S(1)} %all-to-all-done.1.home), custom_call_target="tpu_custom_call" | custom-call | tf_op jit(solution)/shard_map/pallas_call | solution.py:702
Async XLA Ops:
  14.0 1.3 %collective-permute-start = (f32[1,128,128]{2,1,0:T(8,128)S(1)}, f32[1,128,128]{2,1,0:T(8,128)S(1)}, u32[]{:S(2)}, u32[]{:S(2)}) collective-permute-start(f32[1,128,128]{2,1,0:T(8,128)S(1)} %get-tuple-element.42), channel_id=1, source_target_pairs={{0,1},{1,0},{2,3},{3,2},{4,5},{5,4},{6,7},{7,6},{8,9},{9,8},{10,11... | collective-permute-start | bytes 196616 | tf_op jit(solution)/shard_map/ppermute | solution.py:646
  15.4 11.7 %collective-permute-start.1 = (f32[336,128]{1,0:T(8,128)S(1)}, f32[336,128]{1,0:T(8,128)S(1)}, u32[]{:S(2)}, u32[]{:S(2)}) collective-permute-start(f32[336,128]{1,0:T(8,128)S(1)} %get-tuple-element.48), channel_id=1, source_target_pairs={{0,2},{2,4},{4,6},{1,3},{3,5},{5,7},{8,10},{10,12},{12,14},{9,11},... | collective-permute-start | bytes 516104 | tf_op jit(solution)/shard_map/ppermute | solution.py:594
  17.8 9.2 %collective-permute-start.2 = (f32[304,128]{1,0:T(8,128)S(1)}, f32[304,128]{1,0:T(8,128)S(1)}, u32[]{:S(2)}, u32[]{:S(2)}) collective-permute-start(f32[304,128]{1,0:T(8,128)S(1)} %get-tuple-element.49), channel_id=1, source_target_pairs={{2,0},{4,2},{6,4},{3,1},{5,3},{7,5},{10,8},{12,10},{14,12},{11,9},... | collective-permute-start | bytes 466952 | tf_op jit(solution)/shard_map/ppermute | solution.py:594
  19.1 14.4 %collective-permute-start.6 = (f32[608,128]{1,0:T(8,128)S(1)}, f32[608,128]{1,0:T(8,128)S(1)}, u32[]{:S(2)}, u32[]{:S(2)}) collective-permute-start(f32[608,128]{1,0:T(8,128)S(1)} %get-tuple-element.53), channel_id=1, source_target_pairs={{8,0},{16,8},{24,16},{9,1},{17,9},{25,17},{10,2},{18,10},{26,18},{... | collective-permute-start | bytes 933896 | tf_op jit(solution)/shard_map/ppermute | solution.py:594
  20.4 13.1 %collective-permute-start.5 = (f32[672,128]{1,0:T(8,128)S(1)}, f32[672,128]{1,0:T(8,128)S(1)}, u32[]{:S(2)}, u32[]{:S(2)}) collective-permute-start(f32[672,128]{1,0:T(8,128)S(1)} %get-tuple-element.52), channel_id=1, source_target_pairs={{0,8},{8,16},{16,24},{1,9},{9,17},{17,25},{2,10},{10,18},{18,26},{... | collective-permute-start | bytes 1032200 | tf_op jit(solution)/shard_map/ppermute | solution.py:594
  27.1 6.7 %collective-permute-start.3 = (f32[104,128]{1,0:T(8,128)S(1)}, f32[104,128]{1,0:T(8,128)S(1)}, u32[]{:S(2)}, u32[]{:S(2)}) collective-permute-start(f32[104,128]{1,0:T(8,128)S(1)} %get-tuple-element.50), channel_id=1, source_target_pairs={{0,8},{8,16},{16,24},{1,9},{9,17},{17,25},{2,10},{10,18},{18,26},{... | collective-permute-start | bytes 159752 | tf_op jit(solution)/shard_map/ppermute | solution.py:594
  30.6 6.0 %collective-permute-start.4 = (f32[104,128]{1,0:T(8,128)S(1)}, f32[104,128]{1,0:T(8,128)S(1)}, u32[]{:S(2)}, u32[]{:S(2)}) collective-permute-start(f32[104,128]{1,0:T(8,128)S(1)} %get-tuple-element.51), channel_id=1, source_target_pairs={{8,0},{16,8},{24,16},{9,1},{17,9},{25,17},{10,2},{18,10},{26,18},{... | collective-permute-start | bytes 159752 | tf_op jit(solution)/shard_map/ppermute | solution.py:594
  39.3 8.1 %all-to-all-start.1 = ((f32[8,8,128]{2,1,0:T(8,128)}), f32[8,8,128]{2,1,0:T(8,128)S(1)}, u32[]{:S(2)}, u32[]{:S(2)}) async-start(f32[8,8,128]{2,1,0:T(8,128)} %get-tuple-element.71), calls=%async_computation.1 | async-start | bytes 65536 | tf_op jit(solution)/shard_map/all_to_all | solution.py:698
